TPU v7x, 32 devices: a whole 2x2x4 slice. The times are simulated.
32 devices in a mesh: dp: 4 (over x, core), fsdp: 8 (over z, y).
Axes of the slice: x: 2, y: 2, z: 4, core: 2. Of those that a mesh axis runs over, the one named last changes fastest.
Arguments:
- prompt_ids: int32 [64, 192], P(('dp', 'fsdp')), may hold values from 0 to 32127
- prompt_lengths: int32 [64], P(('dp', 'fsdp')), may hold values from 1 to 192, 9216 in all
- response_ids: int32 [128, 32], P(('dp', 'fsdp')), may hold values from 0 to 32127
- response_lengths: int32 [128], P(('dp', 'fsdp')), may hold values from 1 to 32
- sequence_pair: int32 [128], P(('dp', 'fsdp')), may hold values from 0 to 63, as said below
- chosen_flag: int32 [128], P(('dp', 'fsdp')), may hold values from 0 to 1, as said below
- pair_microbatch: int32 [64], P(('dp', 'fsdp')), may hold values from 0 to 1
- policy_embed: float32 [32128, 1024], P(('dp', 'fsdp')), may hold values from -6 to 6
- policy_layers: float32 [1024, 28672], P(('dp', 'fsdp')), may hold values from -0.1875 to 0.1875
- policy_gains: float32 [7, 1024], replicated, may hold values from 0.5 to 1.5
- momentum_embed: float32 [32128, 1024], P(('dp', 'fsdp')), may hold values from -7.6293945e-06 to 7.6293945e-06
- momentum_layers: float32 [1024, 28672], P(('dp', 'fsdp')), may hold values from -0.00015258789 to 0.00015258789
- momentum_gains: float32 [7, 1024], replicated, may hold values from -0.00015258789 to 0.00015258789
- average_embed: float32 [32128, 1024], P(('dp', 'fsdp')), may hold values from -6 to 6
- average_layers: float32 [1024, 28672], P(('dp', 'fsdp')), may hold values from -0.1875 to 0.1875
- average_gains: float32 [7, 1024], replicated, may hold values from 0.5 to 1.5
- frozen_embed: bfloat16 [32128, 1024], P(('dp', 'fsdp')), may hold values from -6 to 6
- frozen_layers: bfloat16 [1024, 28672], P(('dp', 'fsdp')), may hold values from -0.1875 to 0.1875
- frozen_gains: float32 [7, 1024], replicated, may hold values from 0.5 to 1.5
Outputs:
- loss: float32 [], replicated
- grad_norm: float32 [], replicated
- micro_counts: float32 [2, 2], replicated
- frozen_mean: float32 [128], P(('dp', 'fsdp'))
- step_embed: float32 [32128, 1024], P(('dp', 'fsdp'))
- next_layers: float32 [1024, 28672], P(('dp', 'fsdp'))
- next_gains: float32 [7, 1024], replicated
- moment_embed: float32 [32128, 1024], P(('dp', 'fsdp'))
- moment_layers: float32 [1024, 28672], P(('dp', 'fsdp'))
- moment_gains: float32 [7, 1024], replicated
- smooth_embed: float32 [32128, 1024], P(('dp', 'fsdp'))
- smooth_layers: float32 [1024, 28672], P(('dp', 'fsdp'))
- smooth_gains: float32 [7, 1024], replicated
Inputs may be any that keep to these rules, and one draw needn't show every extreme that they name: `sequence_pair`: each pair id names exactly two sequences; the sequences of pairs 2 * i to 2 * i + 1 are the rows 2 * 2 * i to 2 * 2 * i + 2 * 2 - 1. `chosen_flag`: of the two sequences of a pair exactly one has flag 1.
All inputs are finite; a program needn't handle non-finite values. No bound on the sum of `prompt_lengths` on one device may be relied on, other than what follows from the above.
Results may differ from a plain program's by a relative error of at most 0.008.
Values may be sent and summed in bfloat16 or wider, within the bound.
A program may use at most 704 MiB of HBM per device.

v0:
```python
import jax
import jax.numpy as jnp
from jax import lax
from jax.sharding import PartitionSpec as P

D = 1024
HEADS = 16
HEAD = 64
FF = 4096
P_MAX = 192
R_MAX = 32
MICRO = 2


EPSILON = 1e-06
SCORE_SCALE = 0.125
PREFERENCE_BETA = 0.1
CHOSEN_WEIGHT = 1.0
MOMENTUM = 0.9
LEARN_RATE = 2000.0
AVERAGE_DECAY = 0.5
CLIP_NORM = 0.04
MASK_FILL = -1000000000.0
HIGHEST = lax.Precision.HIGHEST


def rms_norm(values, gain_row):
    return (
        values * lax.rsqrt(jnp.mean(values * values, axis=-1, keepdims=True) + EPSILON) * gain_row
    )


def final_norm(values, gain_row):
    return rms_norm(values, gain_row) * D ** (-0.5)


def to_low(values):
    return values.astype(jnp.bfloat16)


def matmul(left_side, right_side):
    return jnp.dot(left_side, right_side, preferred_element_type=jnp.float32)


def matmul_back(grad_low, weight):
    return jnp.einsum("re,de->rd", grad_low, weight, preferred_element_type=jnp.float32)


def columns(layer_full, first_column, column_count):
    return layer_full[:, first_column : first_column + column_count]


def split_heads(values):
    return values.reshape(values.shape[0], values.shape[1], HEADS, HEAD)


def scores_of(queries, key_rows, allowed):
    raw_scores = (
        jnp.einsum(
            "bqhe,bkhe->bhqk",
            split_heads(queries),
            split_heads(key_rows),
            preferred_element_type=jnp.float32,
        )
        * SCORE_SCALE
    )
    return jnp.where(allowed[:, None], raw_scores, MASK_FILL)


def attend_forward(queries, key_rows, values, allowed):
    scores = scores_of(queries, key_rows, allowed)
    log_total = jax.nn.logsumexp(scores, axis=-1, keepdims=True)
    softmax_out = to_low(jnp.exp(scores - log_total))
    mixed_out = jnp.einsum(
        "bhqk,bkhe->bqhe", softmax_out, split_heads(values), preferred_element_type=jnp.float32
    )
    return (to_low(mixed_out.reshape(queries.shape)), log_total)


def attend_backward(queries, key_rows, values, allowed, log_total, grad_mixed):
    softmax_out = jnp.exp(scores_of(queries, key_rows, allowed) - log_total)
    grad_heads = split_heads(to_low(grad_mixed))
    grad_values = jnp.einsum(
        "bhqk,bqhe->bkhe", to_low(softmax_out), grad_heads, preferred_element_type=jnp.float32
    )
    grad_probs = jnp.einsum(
        "bqhe,bkhe->bhqk", grad_heads, split_heads(values), preferred_element_type=jnp.float32
    )
    grad_scores = to_low(
        softmax_out * (grad_probs - jnp.sum(grad_probs * softmax_out, axis=-1, keepdims=True))
    )
    grad_query = (
        jnp.einsum(
            "bhqk,bkhe->bqhe",
            grad_scores,
            split_heads(key_rows),
            preferred_element_type=jnp.float32,
        )
        * SCORE_SCALE
    )
    grad_keys = (
        jnp.einsum(
            "bhqk,bqhe->bkhe", grad_scores, split_heads(queries), preferred_element_type=jnp.float32
        )
        * SCORE_SCALE
    )
    return (
        grad_query.reshape(queries.shape),
        grad_keys.reshape(key_rows.shape),
        grad_values.reshape(values.shape),
    )


def self_forward(residual, gain_row, weight_three, weight_out, allowed, shape_pair):
    normed = to_low(rms_norm(residual, gain_row))
    triple = to_low(matmul(normed, weight_three)).reshape(shape_pair[0], shape_pair[1], 3 * D)
    mixed_out, log_total = attend_forward(
        triple[..., :D], triple[..., D : 2 * D], triple[..., 2 * D :], allowed
    )
    flat_mixed = mixed_out.reshape(-1, D)
    return (residual + matmul(flat_mixed, weight_out), (normed, triple, log_total, flat_mixed))


def self_backward(residual, gain_row, weight_three, weight_out, allowed, stored, grad_out):
    normed, triple, log_total, flat_mixed = stored
    grad_low = to_low(grad_out)
    grad_mixed = matmul_back(grad_low, weight_out)
    queries = triple[..., :D]
    grad_query, grad_keys, grad_values = attend_backward(
        queries,
        triple[..., D : 2 * D],
        triple[..., 2 * D :],
        allowed,
        log_total,
        grad_mixed.reshape(queries.shape),
    )
    grad_triple = to_low(
        jnp.concatenate([grad_query, grad_keys, grad_values], axis=-1).reshape(-1, 3 * D)
    )
    grad_normed = matmul_back(grad_triple, weight_three)
    grad_residual, grad_gain = jax.vjp(rms_norm, residual, gain_row)[1](grad_normed)
    return (grad_out + grad_residual, grad_gain, ((normed, grad_triple), (flat_mixed, grad_low)))


def cross_forward(
    residual, gain_row, weight_query, weight_out, cross_memory, select_low, allowed, shape_pair
):
    normed = to_low(rms_norm(residual, gain_row))
    queries = to_low(matmul(normed, weight_query)).reshape(shape_pair[0], shape_pair[1], D)
    seat_memory = to_low(
        jnp.einsum("sp,pkd->skd", select_low, cross_memory, preferred_element_type=jnp.float32)
    )
    mixed_out, log_total = attend_forward(
        queries, seat_memory[..., :D], seat_memory[..., D:], allowed
    )
    flat_mixed = mixed_out.reshape(-1, D)
    return (
        residual + matmul(flat_mixed, weight_out),
        (normed, queries, seat_memory, log_total, flat_mixed),
    )


def cross_backward(
    residual, gain_row, weight_query, weight_out, select_low, allowed, stored, grad_out
):
    normed, queries, seat_memory, log_total, flat_mixed = stored
    grad_low = to_low(grad_out)
    grad_mixed = matmul_back(grad_low, weight_out)
    grad_query, grad_keys, grad_values = attend_backward(
        queries,
        seat_memory[..., :D],
        seat_memory[..., D:],
        allowed,
        log_total,
        grad_mixed.reshape(queries.shape),
    )
    grad_memory = to_low(
        jnp.einsum(
            "sp,skd->pkd",
            select_low.astype(jnp.float32),
            jnp.concatenate([grad_keys, grad_values], axis=-1),
            precision=HIGHEST,
        )
    )
    query_low = to_low(grad_query.reshape(-1, D))
    grad_normed = matmul_back(query_low, weight_query)
    grad_residual, grad_gain = jax.vjp(rms_norm, residual, gain_row)[1](grad_normed)
    return (
        grad_out + grad_residual,
        grad_gain,
        grad_memory,
        ((normed, query_low), (flat_mixed, grad_low)),
    )


def feed_forward(residual, gain_row, weight_in, weight_out):
    normed = to_low(rms_norm(residual, gain_row))
    before = matmul(normed, weight_in)
    active = to_low(jax.nn.relu(before))
    return (
        residual + jnp.einsum("rf,df->rd", active, weight_out, preferred_element_type=jnp.float32),
        (normed, before, active),
    )


def feed_backward(residual, gain_row, weight_in, weight_out, stored, grad_out):
    normed, before, active = stored
    grad_low = to_low(grad_out)
    grad_active = matmul(grad_low, weight_out)
    grad_before = to_low(jnp.where(before > 0, grad_active, 0.0))
    grad_normed = matmul_back(grad_before, weight_in)
    grad_residual, grad_gain = jax.vjp(rms_norm, residual, gain_row)[1](grad_normed)
    return (grad_out + grad_residual, grad_gain, ((normed, grad_before), (grad_low, active)))


def forward(embed_full, layer_full, gain_rows, batch_data):
    (
        prompt_ids,
        decoder_input,
        targets,
        enc_allowed,
        self_allowed,
        cross_allowed,
        select_low,
        valid,
    ) = batch_data
    pairs_here, seat_count = (prompt_ids.shape[0], decoder_input.shape[0])
    encoder_input = embed_full[prompt_ids.reshape(-1)].astype(jnp.float32)
    encoder_one, encoder_attn = self_forward(
        encoder_input,
        gain_rows[0],
        columns(layer_full, 0, 3 * D),
        columns(layer_full, 3 * D, D),
        enc_allowed,
        (pairs_here, P_MAX),
    )
    encoder_two, encoder_ffn = feed_forward(
        encoder_one,
        gain_rows[1],
        columns(layer_full, 12 * D, FF),
        columns(layer_full, 12 * D + FF, FF),
    )
    encoder_final = to_low(rms_norm(encoder_two, gain_rows[2]))
    cross_memory = to_low(matmul(encoder_final, columns(layer_full, 9 * D, 2 * D))).reshape(
        pairs_here, P_MAX, 2 * D
    )
    decoder_zero = embed_full[decoder_input.reshape(-1)].astype(jnp.float32)
    decoder_one, decoder_attn = self_forward(
        decoder_zero,
        gain_rows[3],
        columns(layer_full, 4 * D, 3 * D),
        columns(layer_full, 7 * D, D),
        self_allowed,
        (seat_count, R_MAX),
    )
    decoder_two, decoder_cross = cross_forward(
        decoder_one,
        gain_rows[4],
        columns(layer_full, 8 * D, D),
        columns(layer_full, 11 * D, D),
        cross_memory,
        select_low,
        cross_allowed,
        (seat_count, R_MAX),
    )
    decoder_three, decoder_ffn = feed_forward(
        decoder_two,
        gain_rows[5],
        columns(layer_full, 12 * D + 2 * FF, FF),
        columns(layer_full, 12 * D + 3 * FF, FF),
    )
    final_rows = to_low(final_norm(decoder_three, gain_rows[6]))
    stored = (
        encoder_input,
        encoder_one,
        encoder_two,
        encoder_attn,
        encoder_ffn,
        encoder_final,
        decoder_zero,
        decoder_one,
        decoder_two,
        decoder_three,
        decoder_attn,
        decoder_cross,
        decoder_ffn,
    )
    return (final_rows, stored)


def log_probs(final_rows, table_full, targets, valid):
    seat_count = valid.shape[0]
    target_rows = table_full[targets.reshape(-1)]
    picked = jnp.sum(final_rows.astype(jnp.float32) * target_rows.astype(jnp.float32), axis=1)
    logits = jnp.einsum("rd,vd->rv", final_rows, table_full, preferred_element_type=jnp.float32)
    log_own = jax.nn.logsumexp(logits, axis=1)
    kept = (logits, log_own)
    token_logp = jnp.where(valid.reshape(-1), picked - log_own, 0.0)
    return (jnp.sum(token_logp.reshape(seat_count, -1), axis=1), kept)


def head_back(table_full, targets, row_weight, kept):
    logits, log_own = kept
    target_hot = (targets.reshape(-1, 1) == jnp.arange(table_full.shape[0])[None, :]).astype(
        jnp.float32
    )
    grad_logits = to_low(row_weight[:, None] * (target_hot - jnp.exp(logits - log_own[:, None])))
    return (matmul(grad_logits, table_full), grad_logits, grad_logits)


def backward(layer_full, gain_rows, batch_data, stored, grad_final):
    (
        prompt_ids,
        decoder_input,
        targets,
        enc_allowed,
        self_allowed,
        cross_allowed,
        select_low,
        valid,
    ) = batch_data
    (
        encoder_input,
        encoder_one,
        encoder_two,
        encoder_attn,
        encoder_ffn,
        encoder_final,
        decoder_zero,
        decoder_one,
        decoder_two,
        decoder_three,
        decoder_attn,
        decoder_cross,
        decoder_ffn,
    ) = stored
    grad_three, gain_six = jax.vjp(final_norm, decoder_three, gain_rows[6])[1](grad_final)
    grad_two, gain_five, dec_ffn_pairs = feed_backward(
        decoder_two,
        gain_rows[5],
        columns(layer_full, 12 * D + 2 * FF, FF),
        columns(layer_full, 12 * D + 3 * FF, FF),
        decoder_ffn,
        grad_three,
    )
    grad_one, gain_four, grad_memory, cross_pairs = cross_backward(
        decoder_one,
        gain_rows[4],
        columns(layer_full, 8 * D, D),
        columns(layer_full, 11 * D, D),
        select_low,
        cross_allowed,
        decoder_cross,
        grad_two,
    )
    grad_zero, gain_three, dec_self_pairs = self_backward(
        decoder_zero,
        gain_rows[3],
        columns(layer_full, 4 * D, 3 * D),
        columns(layer_full, 7 * D, D),
        self_allowed,
        decoder_attn,
        grad_one,
    )
    memory_low = grad_memory.reshape(-1, 2 * D)
    grad_encoder_final = matmul_back(memory_low, columns(layer_full, 9 * D, 2 * D))
    grad_encoder_two, gain_two = jax.vjp(rms_norm, encoder_two, gain_rows[2])[1](grad_encoder_final)
    grad_encoder_one, gain_one, enc_ffn_pairs = feed_backward(
        encoder_one,
        gain_rows[1],
        columns(layer_full, 12 * D, FF),
        columns(layer_full, 12 * D + FF, FF),
        encoder_ffn,
        grad_encoder_two,
    )
    grad_encoder_input, gain_zero, enc_self_pairs = self_backward(
        encoder_input,
        gain_rows[0],
        columns(layer_full, 0, 3 * D),
        columns(layer_full, 3 * D, D),
        enc_allowed,
        encoder_attn,
        grad_encoder_one,
    )
    gain_grads = jnp.stack(
        [gain_zero, gain_one, gain_two, gain_three, gain_four, gain_five, gain_six]
    )
    layer_pairs = (
        enc_self_pairs[0],
        enc_self_pairs[1],
        dec_self_pairs[0],
        dec_self_pairs[1],
        cross_pairs[0],
        (encoder_final, memory_low),
        cross_pairs[1],
        enc_ffn_pairs[0],
        enc_ffn_pairs[1],
        dec_ffn_pairs[0],
        dec_ffn_pairs[1],
    )
    return (gain_grads, layer_pairs, grad_encoder_input, grad_zero)


def apply_update(weight, moment, average, gradient, factor):
    clipped = gradient * factor
    moment_new = MOMENTUM * moment + clipped
    step_size = -LEARN_RATE * (clipped + MOMENTUM * moment_new)
    weight_new = weight + step_size
    return (
        weight_new,
        moment_new,
        AVERAGE_DECAY * average + (1.0 - AVERAGE_DECAY) * weight_new,
        step_size,
    )


def body(
    prompt_ids,
    prompt_lengths,
    response_ids,
    response_lengths,
    sequence_pair,
    chosen_flag,
    pair_microbatch,
    policy_embed,
    policy_layers,
    policy_gains,
    momentum_embed,
    momentum_layers,
    momentum_gains,
    average_embed,
    average_layers,
    average_gains,
    frozen_embed,
    frozen_layers,
    frozen_gains,
):
    pairs_here = prompt_ids.shape[0]
    seat_count = response_ids.shape[0]
    decoder_input = jnp.concatenate(
        [jnp.zeros((seat_count, 1), jnp.int32), response_ids[:, :-1]], axis=1
    )
    pair_local = sequence_pair - lax.axis_index(("dp", "fsdp")) * pairs_here
    select_float = (pair_local[:, None] == jnp.arange(pairs_here)[None, :]).astype(jnp.float32)
    prompt_pos = jnp.arange(P_MAX)
    reply_pos = jnp.arange(R_MAX)
    prompt_keys = prompt_pos[None, :] < prompt_lengths[:, None]
    valid = reply_pos[None, :] < response_lengths[:, None]
    enc_allowed = jnp.broadcast_to(prompt_keys[:, None, :], (pairs_here, P_MAX, P_MAX))
    self_allowed = (reply_pos[:, None] >= reply_pos[None, :])[None] & valid[:, None, :]
    seat_keys = jnp.einsum("sp,pk->sk", select_float, prompt_keys.astype(jnp.float32)) > 0.5
    cross_allowed = jnp.broadcast_to(seat_keys[:, None, :], (seat_count, R_MAX, P_MAX))
    batch_data = (
        prompt_ids,
        decoder_input,
        response_ids,
        enc_allowed,
        self_allowed,
        cross_allowed,
        to_low(select_float),
        valid,
    )
    micro_range = jnp.arange(MICRO)
    pair_micro = (pair_microbatch[:, None] == micro_range[None, :]).astype(jnp.float32)
    seat_micro = jnp.einsum("sp,pm->sm", select_float, pair_micro, precision=HIGHEST)
    chosen_float = chosen_flag.astype(jnp.float32)
    token_local = jnp.einsum(
        "sm,s->m",
        seat_micro,
        chosen_float * response_lengths.astype(jnp.float32),
        precision=HIGHEST,
    )
    pair_total, token_total = lax.psum((jnp.sum(pair_micro, axis=0), token_local), ("dp", "fsdp"))
    micro_counts = jnp.stack([pair_total, token_total])
    pair_divisor = jnp.einsum("pm,m->p", pair_micro, pair_total, precision=HIGHEST)
    sequence_divisor = jnp.einsum("sm,m->s", seat_micro, token_total, precision=HIGHEST)
    frozen_full = (
        lax.all_gather(frozen_embed, ("dp", "fsdp"), axis=0, tiled=True),
        lax.all_gather(frozen_layers, ("dp", "fsdp"), axis=0, tiled=True),
    )
    frozen_rows, unused = forward(frozen_full[0], frozen_full[1], frozen_gains, batch_data)
    frozen_logp, frozen_kept = log_probs(frozen_rows, frozen_full[0], response_ids, valid)
    frozen_mean = frozen_logp / response_lengths.astype(jnp.float32)
    policy_shard = to_low(policy_embed)
    policy_full = (
        lax.all_gather(policy_shard, ("dp", "fsdp"), axis=0, tiled=True),
        lax.all_gather(to_low(policy_layers), ("dp", "fsdp"), axis=0, tiled=True),
    )
    policy_rows, stored = forward(policy_full[0], policy_full[1], policy_gains, batch_data)
    policy_logp, head_kept = log_probs(policy_rows, policy_full[0], response_ids, valid)
    sign_value = 2.0 * chosen_float - 1.0
    margin = PREFERENCE_BETA * jnp.einsum(
        "sp,s->p", select_float, sign_value * (policy_logp - frozen_logp), precision=HIGHEST
    )
    loss_local = (
        jnp.sum(jax.nn.softplus(-margin) / pair_divisor)
        - CHOSEN_WEIGHT * jnp.sum(chosen_float * policy_logp / sequence_divisor)
    ) / MICRO
    pair_slope = -PREFERENCE_BETA * jax.nn.sigmoid(-margin) / pair_divisor
    sequence_slope = (
        sign_value * jnp.einsum("sp,p->s", select_float, pair_slope, precision=HIGHEST)
        - CHOSEN_WEIGHT * chosen_float / sequence_divisor
    ) / MICRO
    row_weight = (sequence_slope[:, None] * valid).reshape(-1)
    back_full = (
        lax.all_gather(policy_shard, ("dp", "fsdp"), axis=0, tiled=True),
        lax.all_gather(to_low(policy_layers), ("dp", "fsdp"), axis=0, tiled=True),
    )
    grad_final, logit_embed, grad_logits = head_back(
        back_full[0], response_ids, row_weight, head_kept
    )
    gain_grads, layer_pairs, grad_encoder_input, grad_decoder_input = backward(
        back_full[1], policy_gains, batch_data, stored, grad_final
    )
    token_ids = jnp.concatenate([prompt_ids.reshape(-1), decoder_input.reshape(-1)])
    token_gradient = jnp.concatenate([grad_encoder_input, grad_decoder_input], axis=0)
    indicator = (
        token_ids[:, None]
        == jnp.arange(lax.axis_size(("dp", "fsdp")) * policy_embed.shape[0])[None, :]
    ).astype(jnp.float32)
    embed_grad = lax.psum_scatter(
        jnp.einsum("nc,nd->cd", indicator, token_gradient, precision=HIGHEST)
        + jnp.einsum("rc,rd->cd", grad_logits, policy_rows, preferred_element_type=jnp.float32),
        ("dp", "fsdp"),
        scatter_dimension=0,
        tiled=True,
    )
    pieces = [
        jnp.einsum("rc,re->ce", left_side, right_side, preferred_element_type=jnp.float32)
        for left_side, right_side in layer_pairs
    ]
    layer_grad = lax.psum_scatter(
        jnp.concatenate(pieces, axis=1), ("dp", "fsdp"), scatter_dimension=0, tiled=True
    )
    squares_local = jnp.sum(embed_grad * embed_grad) + jnp.sum(layer_grad * layer_grad)
    gain_total, squares_total, loss = lax.psum(
        (gain_grads, squares_local, loss_local), ("dp", "fsdp")
    )
    grad_norm = jnp.sqrt(squares_total + jnp.sum(gain_total * gain_total))
    factor = jnp.minimum(1.0, CLIP_NORM / grad_norm)
    embed_new = apply_update(policy_embed, momentum_embed, average_embed, embed_grad, factor)
    layers_new = apply_update(policy_layers, momentum_layers, average_layers, layer_grad, factor)
    gains_new = apply_update(policy_gains, momentum_gains, average_gains, gain_total, factor)
    return (
        loss,
        grad_norm,
        micro_counts,
        frozen_mean,
        embed_new[3],
        layers_new[0],
        gains_new[0],
        embed_new[1],
        layers_new[1],
        gains_new[1],
        embed_new[2],
        layers_new[2],
        gains_new[2],
    )


def solution(mesh):
    placed = (
        P(("dp", "fsdp"), None),
        P(("dp", "fsdp")),
        P(("dp", "fsdp"), None),
        P(("dp", "fsdp")),
        P(("dp", "fsdp")),
        P(("dp", "fsdp")),
        P(("dp", "fsdp")),
        P(("dp", "fsdp"), None),
        P(("dp", "fsdp"), None),
        P(),
        P(("dp", "fsdp"), None),
        P(("dp", "fsdp"), None),
        P(),
        P(("dp", "fsdp"), None),
        P(("dp", "fsdp"), None),
        P(),
        P(("dp", "fsdp"), None),
        P(("dp", "fsdp"), None),
        P(),
    )
    return jax.shard_map(
        body,
        mesh=mesh,
        in_specs=placed,
        out_specs=(
            P(),
            P(),
            P(),
            P(("dp", "fsdp")),
            P(("dp", "fsdp"), None),
            P(("dp", "fsdp"), None),
            P(),
            P(("dp", "fsdp"), None),
            P(("dp", "fsdp"), None),
            P(),
            P(("dp", "fsdp"), None),
            P(("dp", "fsdp"), None),
            P(),
        ),
        check_vma=False,
    )
```

profile of v0, /device:TPU:0, one launch (start us, length us, event | category | flops | bytes accessed | tf_op | source)
XLA Modules:
  0.0 7152.7 jit_solution(7045439702860750818)
XLA Ops:
  16.7 44.7 all-reduce.4
  64.8 301.1 %all-gather.13.cloned.1.call-done = bf16[32,1004,1024]{2,1,0:T(8,128)(2,1)} async-done(((bf16[1,1004,1024]{2,1,0:T(8,128)(2,1)}), bf16[32,1004,1024]{2,1,0:T(8,128)(2,1)}) %all-gather.13.cloned.1.call-update) | async-done | bytes 65798160 | tf_op jit(solution)/shard_map/all_gather | solution.py:478
  365.8 48.6 reshape.759
  419.5 299.3 %all-gather.11.cloned.1.call-done = bf16[32,1004,1024]{2,1,0:T(8,128)(2,1)} async-done(((bf16[1,1004,1024]{2,1,0:T(8,128)(2,1)}), bf16[32,1004,1024]{2,1,0:T(8,128)(2,1)}) %all-gather.11.cloned.1.call-update) | async-done | bytes 65798160 | tf_op jit(solution)/shard_map/all_gather | solution.py:486
  718.8 48.6 reshape.757
  772.6 8.2 gather_fusion.4
  780.9 8.7 gather_fusion.1
  789.7 246.2 %all-gather.9.cloned.1.call-done = bf16[1024,28672]{1,0:T(8,128)(2,1)} async-done(((bf16[32,28672]{1,0:T(8,128)(2,1)}), bf16[1024,28672]{1,0:T(8,128)(2,1)}) %all-gather.9.cloned.1.call-update) | async-done | bytes 58720272 | tf_op jit(solution)/shard_map/all_gather | solution.py:479
  1052.1 5.5 fusion.64
  1062.0 291.5 %all-gather.7.cloned.1.call-done = bf16[1024,28672]{1,0:T(8,128)(2,1)} async-done(((bf16[32,28672]{1,0:T(8,128)(2,1)}), bf16[1024,28672]{1,0:T(8,128)(2,1)}) %all-gather.7.cloned.1.call-update) | async-done | bytes 58720272 | tf_op jit(solution)/shard_map/all_gather | solution.py:487
  1353.5 5.5 fusion.61
  1377.4 13.8 multiply_reduce_fusion.8
  1416.1 10.2 multiply_reduce_fusion.20
  1426.3 35.0 fusion.359
  1479.9 4.7 fusion.155
  1493.1 5.9 fusion.25
  1499.1 8.5 multiply_reduce_fusion.10
  1533.5 4.7 fusion.17
  1538.2 7.1 multiply_reduce_fusion.24
  1546.5 34.7 fusion.362
  1582.7 8.1 exponential_reduce_fusion
  1591.1 8.1 exponential_reduce_fusion.1
  1601.6 32.4 multiply_reduce_fusion.13
  1634.2 5.0 fusion.58
  1639.3 7.4 multiply_reduce_fusion.14
  1684.9 4.9 copy.220
  1689.8 8.7 fusion.91
  1699.2 5.5 multiply_reduce_fusion.4
  1705.1 7.0 select_convert_fusion
  1712.1 8.5 multiply_reduce_fusion.5
  1729.1 5.4 fusion.156
  1777.1 7.0 convolution_dynamic-update-slice_fusion.5
  1787.7 6.6 convolution_dynamic-update-slice_fusion.4
  1800.0 5.9 convolution_dynamic-update-slice_fusion.6
  1809.8 8.6 convolution_dynamic-update-slice_fusion.3
  1818.4 8.5 convolution_dynamic-update-slice_fusion.2
  1827.0 8.6 convolution_dynamic-update-slice_fusion.1
  1835.6 8.5 convolution_dynamic-update-slice_fusion
  1845.2 5.9 fusion.224
  1851.1 5.9 fusion.129
  1857.9 112.7 %fusion.1 = f32[32128,1024]{1,0:T(8,128)} fusion(s32[512]{0:T(512)S(1)} %pad_add_fusion, f32[512,1024]{1,0:T(8,128)S(1)} %fusion.419), kind=kOutput, calls=%fused_computation.8 | convolution fusion | flops 202148347904 | bytes 133695488 | tf_op jit(solution)/shard_map/nc,nd->cd/dot_general | solution.py:522
  1970.6 90.1 %convolution_add_fusion = f32[32128,1024]{1,0:T(8,128)} fusion(f32[32128,1024]{1,0:T(8,128)} %fusion.1, bf16[128,1024]{1,0:T(8,128)(2,1)S(1)} %copy-done.49, f32[128,32128]{1,0:T(8,128)} %get-tuple-element.113, f32[128]{0:T(128)S(1)} %copy-done.109, s32[128]{0:T(128)S(1)} %copy-done.105, f32[128]{0:T(128)S(1)} %copy-done.107), kind=kOutput, calls=%fused_computation.6 | convolution fusion | flops 8479735808 | bytes 279905792 | tf_op jit(solution)/shard_map/rc,rd->cd/dot_general | solution.py:523
  2060.9 4978.4 %fusion = f32[1008,1024]{1,0:T(8,128)} fusion(f32[32128,1024]{1,0:T(8,128)} %convolution_add_fusion), kind=kCustom, calls=%all-reduce-scatter | all-reduce-scatter fusion | flops 33030144 | bytes 135725056
  7046.8 8.9 collective-permute-done
  7055.7 12.2 concatenate.50
  7077.3 41.9 all-reduce.3
  7121.8 12.6 add_multiply_fusion
  7134.4 10.4 add_multiply_fusion.2
  (566 shorter events, 264.8 us)
Async XLA Ops:
  7.2 358.7 %all-gather.13.cloned.1.call-start = ((), (), s32[]{:S(2)}) async-start(), calls=%async_computation.5 | async-start | bytes 68124672 | tf_op jit(solution)/shard_map/all_gather | solution.py:478
  7.9 710.9 %all-gather.11.cloned.1.call-start = ((), (), s32[]{:S(2)}) async-start(), calls=%async_computation.4 | async-start | bytes 68124672 | tf_op jit(solution)/shard_map/all_gather | solution.py:486
  11.8 1024.2 %all-gather.9.cloned.1.call-start = ((), (), s32[]{:S(2)}) async-start(), calls=%async_computation.2 | async-start | bytes 60555264 | tf_op jit(solution)/shard_map/all_gather | solution.py:479
  12.6 48.9 copy-start.115
  12.6 49.6 copy-start.119
  12.6 50.0 copy-start.143
  12.6 50.2 copy-start.92
  12.6 51.5 copy-start.110
  12.6 1340.8 %all-gather.7.cloned.1.call-start = ((), (), s32[]{:S(2)}) async-start(), calls=%async_computation.1 | async-start | bytes 60555264 | tf_op jit(solution)/shard_map/all_gather | solution.py:487
  16.1 7055.7 %reduce-scatter.4.cloned.1.call-start = ((), (), s32[]{:S(2)}) async-start(), calls=%async_computation.3 | async-start | bytes 121110528 | tf_op jit(solution)/shard_map/reduce_scatter | solution.py:532
  16.3 1379.4 %copy-start.149 = (s32[4]{0:T(128)}, s32[4]{0:T(128)S(1)}, u32[]{:S(2)}) copy-start(s32[4]{0:T(128)S(1)} %broadcast_subtract_fusion) | copy-start | bytes 52
  16.6 45.8 copy-start.159
  62.3 352.1 %copy-start.116 = (s32[4,32]{1,0:T(4,128)}, s32[4,32]{1,0:T(4,128)S(1)}, u32[]{:S(2)}) copy-start(s32[4,32]{1,0:T(4,128)S(1)} %concatenate.37) | copy-start | bytes 1540
  62.6 1417.3 %copy-start.98 = (pred[2,192]{1,0:T(4,128)(4,1)}, pred[2,192]{1,0:T(4,128)(4,1)S(1)}, u32[]{:S(2)}) copy-start(pred[2,192]{1,0:T(4,128)(4,1)S(1)} %iota_compare_fusion.4) | copy-start | bytes 1156
  63.5 351.0 %copy-start.95 = (f32[1,1024]{1,0:T(1,128)}, f32[1,1024]{1,0:T(1,128)S(1)}, u32[]{:S(2)}) copy-start(f32[1,1024]{1,0:T(1,128)S(1)} %get-tuple-element.71) | copy-start | bytes 12292
  63.5 1290.0 %copy-start.89 = (f32[1,1024]{1,0:T(1,128)}, f32[1,1024]{1,0:T(1,128)S(1)}, u32[]{:S(2)}) copy-start(f32[1,1024]{1,0:T(1,128)S(1)} %get-tuple-element.69) | copy-start | bytes 12292
  416.6 619.3 %copy-start.78 = (bf16[128,1024]{1,0:T(8,128)(2,1)}, bf16[128,1024]{1,0:T(8,128)(2,1)S(1)}, u32[]{:S(2)}) copy-start(bf16[128,1024]{1,0:T(8,128)(2,1)S(1)} %gather_fusion.3) | copy-start | bytes 786436
  769.6 703.1 %copy-start.39 = (bf16[128,1024]{1,0:T(8,128)(2,1)}, bf16[128,1024]{1,0:T(8,128)(2,1)S(1)}, u32[]{:S(2)}) copy-start(bf16[128,1024]{1,0:T(8,128)(2,1)S(1)} %gather_fusion) | copy-start | bytes 786436
  780.9 271.2 %copy-start.19 = (bf16[384,1024]{1,0:T(8,128)(2,1)}, bf16[384,1024]{1,0:T(8,128)(2,1)S(1)}, u32[]{:S(2)}) copy-start(bf16[384,1024]{1,0:T(8,128)(2,1)S(1)} %gather_fusion.4) | copy-start | bytes 2359300
  789.6 700.0 %copy-start.1 = (bf16[384,1024]{1,0:T(8,128)(2,1)}, bf16[384,1024]{1,0:T(8,128)(2,1)S(1)}, u32[]{:S(2)}) copy-start(bf16[384,1024]{1,0:T(8,128)(2,1)S(1)} %gather_fusion.1) | copy-start | bytes 2359300
  1061.9 297.0 %copy-start.111 = (f32[384]{0:T(512)}, f32[384]{0:T(512)S(1)}, u32[]{:S(2)}) copy-start(f32[384]{0:T(512)S(1)} %fusion.135) | copy-start | bytes 4612
  1061.9 297.0 %copy-start.100 = (f32[384]{0:T(512)}, f32[384]{0:T(512)S(1)}, u32[]{:S(2)}) copy-start(f32[384]{0:T(512)S(1)} %fusion.290) | copy-start | bytes 4612
  1426.3 35.1 copy-start.50
  1426.3 35.8 copy-start.86
  1545.4 35.8 copy-start.157
  1546.4 34.7 copy-start.48
  1546.4 36.2 copy-start.135
  1599.2 34.8 copy-start.108
  1599.5 34.5 copy-start.136
  1601.5 32.5 copy-start.106
  1601.5 32.7 copy-start.52
  1857.8 112.8 %copy-start.49 = (bf16[128,1024]{1,0:T(8,128)(2,1)S(1)}, bf16[128,1024]{1,0:T(8,128)(2,1)}, u32[]{:S(2)}) copy-start(bf16[128,1024]{1,0:T(8,128)(2,1)} %copy-done.48) | copy-start | bytes 786436
  1857.9 112.8 %copy-start.105 = (s32[128]{0:T(128)S(1)}, s32[128]{0:T(128)}, u32[]{:S(2)}) copy-start(s32[128]{0:T(128)} %eq.63) | copy-start | bytes 1540
  1857.9 112.8 %copy-start.107 = (f32[128]{0:T(128)S(1)}, f32[128]{0:T(128)}, u32[]{:S(2)}) copy-start(f32[128]{0:T(128)} %copy-done.106) | copy-start | bytes 1540
  1857.9 112.7 %copy-start.109 = (f32[128]{0:T(128)S(1)}, f32[128]{0:T(128)}, u32[]{:S(2)}) copy-start(f32[128]{0:T(128)} %copy-done.108) | copy-start | bytes 1540
  2060.8 4984.0 %copy-start.139 = (f32[2]{0:T(128)S(1)}, f32[2]{0:T(128)}, u32[]{:S(2)}) copy-start(f32[2]{0:T(128)} %get-tuple-element.36) | copy-start | bytes 28
  2060.8 4984.0 %copy-start.141 = (f32[2]{0:T(128)S(1)}, f32[2]{0:T(128)}, u32[]{:S(2)}) copy-start(f32[2]{0:T(128)} %get-tuple-element.37) | copy-start | bytes 28
  2060.8 4985.9 %copy-start.123 = (f32[1024]{0:T(1024)S(1)}, f32[1024]{0:T(1024)}, u32[]{:S(2)}) copy-start(f32[1024]{0:T(1024)} %get-tuple-element.19) | copy-start | bytes 12292
  2060.8 4985.9 %copy-start.124 = (f32[1024]{0:T(1024)S(1)}, f32[1024]{0:T(1024)}, u32[]{:S(2)}) copy-start(f32[1024]{0:T(1024)} %get-tuple-element.21) | copy-start | bytes 12292
  2060.8 4985.9 %copy-start.125 = (f32[1024]{0:T(1024)S(1)}, f32[1024]{0:T(1024)}, u32[]{:S(2)}) copy-start(f32[1024]{0:T(1024)} %get-tuple-element.23) | copy-start | bytes 12292
  2060.8 4985.9 %copy-start.126 = (f32[1024]{0:T(1024)S(1)}, f32[1024]{0:T(1024)}, u32[]{:S(2)}) copy-start(f32[1024]{0:T(1024)} %get-tuple-element.13) | copy-start | bytes 12292
  2060.8 4985.9 %copy-start.127 = (f32[1024]{0:T(1024)S(1)}, f32[1024]{0:T(1024)}, u32[]{:S(2)}) copy-start(f32[1024]{0:T(1024)} %get-tuple-element.15) | copy-start | bytes 12292
  2060.8 4985.9 %copy-start.128 = (f32[1024]{0:T(1024)S(1)}, f32[1024]{0:T(1024)}, u32[]{:S(2)}) copy-start(f32[1024]{0:T(1024)} %get-tuple-element.25) | copy-start | bytes 12292
  2060.8 4985.9 %copy-start.129 = (f32[1024]{0:T(1024)S(1)}, f32[1024]{0:T(1024)}, u32[]{:S(2)}) copy-start(f32[1024]{0:T(1024)} %get-tuple-element.17) | copy-start | bytes 12292
  7040.4 15.3 collective-permute-start
  7067.9 53.2 copy-start.93
  7067.9 53.2 copy-start.102
  7067.9 53.2 copy-start.103
  (125 other events, 737.4 us)
Sparse Core Ops, SparseCore 0:
  10.9 354.8 all-gather.12
  369.3 349.4 all-gather.10
  721.7 314.2 all-gather.8
  1039.2 314.2 all-gather.6
  1844.2 4639.3 reduce-scatter.3
where the time goes:
time: 7170 us; the launch traced here: 7150 us
  blocking collectives  5070 us (71%)
  waiting for transfers between devices  1150 us (16%)
  matrix products  592 us (8%)
  local copies, waits for them, and re-layouts  250 us (3%)
    unnamed x1, blocking collectives  4980 us
    all_gather x1, waiting for transfers between devices, body(): lax.all_gather(frozen_embed, ('dp', 'fsdp'), axis=0, tiled=True)  301 us
    all_gather x1, waiting for transfers between devices, body(): lax.all_gather(policy_shard, ('dp', 'fsdp'), axis=0, tiled=True)  299 us
    all_gather x1, waiting for transfers between devices, body(): lax.all_gather(to_low(policy_layers), ('dp', 'fsdp'), axis=0, tiled=True)  292 us
    all_gather x1, waiting for transfers between devices, body(): lax.all_gather(frozen_layers, ('dp', 'fsdp'), axis=0, tiled=True)  246 us
  transfers between devices with their start and end apart: 6, of which 5 were waited for; matrix products, arithmetic and copies ran while one was open for 75% of the time, Pallas kernels for 0%

commit v1 on v0

--- a/solution.py
+++ b/solution.py
@@ -1,6 +1,10 @@
+import functools
+
 import jax
 import jax.numpy as jnp
 from jax import lax
+from jax.experimental import pallas as pl
+from jax.experimental.pallas import tpu as pltpu
 from jax.sharding import PartitionSpec as P
 
 D = 1024
@@ -44,10 +48,6 @@
 
 def matmul_back(grad_low, weight):
     return jnp.einsum("re,de->rd", grad_low, weight, preferred_element_type=jnp.float32)
-
-
-def columns(layer_full, first_column, column_count):
-    return layer_full[:, first_column : first_column + column_count]
 
 
 def split_heads(values):
@@ -213,7 +213,478 @@
     return (grad_out + grad_residual, grad_gain, ((normed, grad_before), (grad_low, active)))
 
 
-def forward(embed_full, layer_full, gain_rows, batch_data):
+AXES = ("dp", "fsdp")
+SLOTS = 24
+MESH = pl.DeviceIdType.MESH
+WAVE_STEP = 512
+
+
+def device_bits():
+    bits = []
+    for axis in AXES:
+        mask = lax.axis_size(axis) // 2
+        while mask:
+            bits.append((axis, mask))
+            mask //= 2
+    return bits
+
+
+def scatter_orders():
+    core, across = (("dp", 1), ("dp", 2))
+    inner = [bit for bit in reversed(device_bits()) if bit[0] == "fsdp"]
+    first, rest = inner[:1], inner[1:]
+    return (
+        [core, across] + rest + first,
+        [core] + inner + [across],
+        [core, across] + first + rest,
+        [core] + first + [across] + rest,
+    )
+
+
+def wave_orders(wave):
+    orders = scatter_orders()
+    return orders[2:] if wave % 3 == 1 else orders[:2]
+
+
+def bit_of(bit):
+    axis, mask = bit
+    return (lax.axis_index(axis) // mask) % 2
+
+
+def partner(bit):
+    axis, mask = bit
+    return {axis: lax.axis_index(axis) + mask * (1 - 2 * bit_of(bit))}
+
+
+def greet(bits):
+    barrier = pltpu.get_barrier_semaphore()
+    for bit in bits:
+        pl.semaphore_signal(barrier, inc=1, device_id=partner(bit), device_id_type=MESH)
+    pl.semaphore_wait(barrier, len(bits))
+
+
+def gather_kernel(bits, waves, x_ref, *refs):
+    outs, (own_sem, send_sem, recv_sem) = (refs[:-3], refs[-3:])
+    mine = {bit: bit_of(bit) for bit in bits}
+    depth = len(bits)
+
+    def held(order, low, width):
+        lead = tuple(pl.ds(0, 2) if bit in order else pl.ds(mine[bit], 1) for bit in bits)
+        return lead + (slice(None), pl.ds(low, width))
+
+    def source(start, width):
+        return x_ref.at[(slice(None),) * (depth + 1) + (pl.ds(start, width),)]
+
+    greet(bits)
+    number, index = (0, {})
+    for wave, pieces in enumerate(waves):
+        for lane in range(len(pieces)):
+            index[wave, lane] = number
+            number += 1
+    sent, kept = ({}, {})
+    for turn in range(len(waves) + depth):
+        for step in range(depth + 1):
+            wave = turn - step
+            if not 0 <= wave < len(waves):
+                continue
+            for lane, (start, which, low, width, order) in enumerate(waves[wave]):
+                slot = index[wave, lane]
+                out = outs[which]
+                place = out.at[held(order[:step], low, width)]
+                if step == 0:
+                    kept[slot] = pltpu.make_async_copy(source(start, width), place, own_sem.at[slot])
+                    kept[slot].start()
+                elif step == 1:
+                    kept[slot].wait()
+                if step > 0:
+                    sent[slot, step - 1].wait_recv()
+                if step < depth:
+                    sent[slot, step] = pltpu.make_async_remote_copy(
+                        src_ref=source(start, width) if step == 0 else place,
+                        dst_ref=place,
+                        send_sem=send_sem.at[slot, step],
+                        recv_sem=recv_sem.at[slot, step],
+                        device_id=partner(order[step]),
+                        device_id_type=MESH,
+                    )
+                    sent[slot, step].start()
+    for copy in sent.values():
+        copy.wait_send()
+
+
+def tree_gather(shard, blocks, step, collective_id):
+    bits = device_bits()
+    pieces = []
+    for which, (start, width) in enumerate(blocks):
+        for low in range(0, width, step):
+            pieces.append((start + low, which, low, min(step, width - low)))
+    waves = []
+    for wave in range(-(-len(pieces) // 2)):
+        waves.append(
+            [
+                piece + (tuple(reversed(order)),)
+                for piece, order in zip(pieces[2 * wave : 2 * wave + 2], wave_orders(wave))
+            ]
+        )
+    rows = shard.shape[0]
+    gathered = pl.pallas_call(
+        functools.partial(gather_kernel, bits, waves),
+        out_shape=[
+            jax.ShapeDtypeStruct((2,) * len(bits) + (rows, width), shard.dtype)
+            for _, width in blocks
+        ],
+        in_specs=[pl.BlockSpec(memory_space=pl.ANY)],
+        out_specs=[pl.BlockSpec(memory_space=pl.ANY)] * len(blocks),
+        scratch_shapes=[
+            pltpu.SemaphoreType.DMA((len(pieces),)),
+            pltpu.SemaphoreType.DMA((len(pieces), len(bits))),
+            pltpu.SemaphoreType.DMA((len(pieces), len(bits))),
+        ],
+        compiler_params=pltpu.CompilerParams(collective_id=collective_id, has_side_effects=True),
+    )(shard.reshape((1,) * len(bits) + shard.shape))
+    return [value.reshape(-1, width) for value, (_, width) in zip(gathered, blocks)]
+
+
+def gather_whole(values, step, collective_id):
+    full = tree_gather(values, [(0, values.shape[1])], step, collective_id)[0]
+    return full.reshape((-1,) + values.shape)
+
+
+def scatter_kernel(bits, plan, produce, *refs):
+    n_waves, slots, width = (plan["waves"], plan["slots"], plan["step"])
+    ins, (out_ref, send_core, total, from_core, arrived) = (refs[:-8], refs[-8:-3])
+    send_sem, recv_sem, free_sem = refs[-3:]
+    depth = len(bits)
+    mine = {bit: bit_of(bit) for bit in bits}
+    core = scatter_orders()[0][0]
+    rest = [bit for bit in bits if bit != core]
+
+    def half(order, step, kept):
+        bit_at = {bit: pl.ds(mine[bit], 1) for bit in order[1:step]}
+        last = mine[order[step]] if kept else 1 - mine[order[step]]
+        bit_at[order[step]] = pl.ds(last, 1)
+        return tuple(bit_at.get(bit, pl.ds(0, 2)) for bit in rest)
+
+    def copy(slot, step, order):
+        if step == 0:
+            source, target = (send_core.at[slot], from_core.at[slot])
+        else:
+            source = total.at[(slot,) + half(order, step, False)]
+            target = arrived.at[(slot,) + half(order, step, True)]
+        return pltpu.make_async_remote_copy(
+            src_ref=source,
+            dst_ref=target,
+            send_sem=send_sem.at[slot, step],
+            recv_sem=recv_sem.at[slot, step],
+            device_id=partner(order[step]),
+            device_id_type=MESH,
+        )
+
+    def kept_entries(order, step):
+        left = [bit for bit in rest if bit not in order[: step + 1]]
+        for number in range(2 ** len(left)):
+            chosen = {bit: (number >> place) % 2 for place, bit in enumerate(reversed(left))}
+            here = tuple(chosen.get(bit, mine[bit]) for bit in rest)
+            came = tuple(1 - mine[bit] if bit == order[step] else at for bit, at in zip(rest, here))
+            yield here, came
+
+    def put(ref, slot, at, value):
+        ref[(slot,) + at] = value.astype(ref.dtype)
+
+    def visit(wave, lane, step, order):
+        piece = wave * 2 + lane
+        slot = lax.rem(piece, slots)
+        reuse = wave >= slots // 2
+        if step == 0:
+
+            @pl.when(reuse)
+            def _():
+                for old in range(depth):
+                    copy(slot, old, order).wait_send()
+
+            produce(ins, piece, 1 - mine[core], lambda at, value: put(send_core, slot, at, value))
+        else:
+            copy(slot, step - 1, order).wait_recv()
+            if step == 1:
+
+                def add(at, value):
+                    put(total, slot, at, value + from_core[(slot,) + at].astype(jnp.float32))
+
+                produce(ins, piece, mine[core], add)
+            else:
+                for here, came in kept_entries(order, step - 1):
+                    value = total[(slot,) + here].astype(jnp.float32)
+                    value = value + arrived[(slot,) + came].astype(jnp.float32)
+                    if step == depth:
+                        out_ref[:, pl.ds(pl.multiple_of(piece * width, width), width)] = value
+                    else:
+                        put(total, slot, here, value)
+
+            @pl.when(wave + slots // 2 < n_waves)
+            def _():
+                pl.semaphore_signal(
+                    free_sem.at[slot, step - 1],
+                    inc=1,
+                    device_id=partner(order[step - 1]),
+                    device_id_type=MESH,
+                )
+
+        if step < depth:
+
+            @pl.when(reuse)
+            def _():
+                pl.semaphore_wait(free_sem.at[slot, step], 1)
+
+            copy(slot, step, order).start()
+
+    def group(first, carry):
+        for phase in range(3):
+            for step in range(depth + 1):
+                wave = first * 3 + phase - step
+
+                @pl.when((wave >= 0) & (wave < n_waves))
+                def _():
+                    for lane, order in enumerate(wave_orders(phase - step)):
+                        visit(wave, lane, step, order)
+
+        return carry
+
+    greet(bits)
+    lax.fori_loop(0, -(-(n_waves + depth) // 3), group, 0)
+    for wave in range(max(0, n_waves - slots // 2), n_waves):
+        for lane, order in enumerate(wave_orders(wave)):
+            for step in range(depth):
+                copy((wave * 2 + lane) % slots, step, order).wait_send()
+
+
+def tree_scatter(operands, produce, plan, collective_id):
+    bits = device_bits()
+    slots, width, rows = (plan["slots"], plan["step"], plan["rows"])
+    entries = pltpu.VMEM((slots,) + (2,) * (len(bits) - 1) + (rows, width), jnp.bfloat16)
+    in_vmem = pl.BlockSpec(memory_space=pltpu.VMEM)
+    return pl.pallas_call(
+        functools.partial(scatter_kernel, bits, plan, produce),
+        out_shape=jax.ShapeDtypeStruct((rows, 2 * plan["waves"] * width), jnp.float32),
+        in_specs=[in_vmem] * len(operands),
+        out_specs=in_vmem,
+        scratch_shapes=[entries] * 4
+        + [
+            pltpu.SemaphoreType.DMA((slots, len(bits))),
+            pltpu.SemaphoreType.DMA((slots, len(bits))),
+            pltpu.SemaphoreType.REGULAR((slots, len(bits))),
+        ],
+        compiler_params=pltpu.CompilerParams(
+            collective_id=collective_id, has_side_effects=True, vmem_limit_bytes=60 * 2**20
+        ),
+    )(*operands)
+
+
+def unit_of(block, blocks):
+    edges, most = ([], sum(blocks))
+    for count in blocks[:-1]:
+        edges.append(count + (edges[-1] if edges else 0))
+    return sum(lax.div(block + (most - edge), most) for edge in edges)
+
+
+def put_rows(value, lead, rest_count, rows, put):
+    for number in range(2**rest_count):
+        at = tuple((number >> place) % 2 for place in reversed(range(rest_count)))
+        put(lead + at, value[number * rows : (number + 1) * rows])
+
+
+def layer_products(dec_blocks, enc_blocks, step, rows, ins, piece, core, put):
+    dec_left, dec_right, enc_left, enc_right = ins
+    dec_pieces = dec_right.shape[1] // step
+    rest_count = (D // 4 // rows).bit_length() - 1
+
+    def product(left, right, blocks, number):
+        unit = unit_of(lax.div(number * step, D), blocks)
+        sides = right[:, pl.ds(pl.multiple_of(number * step, step), step)]
+        for across in range(2):
+            value = jnp.dot(left[unit, across, core], sides, preferred_element_type=jnp.float32)
+            put_rows(value, (across,), rest_count, rows, put)
+
+    @pl.when(piece < dec_pieces)
+    def _():
+        product(dec_left, dec_right, dec_blocks, piece)
+
+    @pl.when(piece >= dec_pieces)
+    def _():
+        product(enc_left, enc_right, enc_blocks, piece - dec_pieces)
+
+
+def scatter_layers(dec_pairs, enc_pairs, rows, collective_id):
+    operands, counts = ([], [])
+    for pairs in (dec_pairs, enc_pairs):
+        left = jnp.stack([left_side.T.reshape(2, 2, D // 4, -1) for left_side, _ in pairs])
+        operands += [left, jnp.concatenate([right_side for _, right_side in pairs], axis=1)]
+        counts.append([right_side.shape[1] // D for _, right_side in pairs])
+    columns_all = operands[1].shape[1] + operands[3].shape[1]
+    plan = {"waves": columns_all // (2 * WAVE_STEP), "slots": 12, "step": WAVE_STEP, "rows": rows}
+    produce = functools.partial(layer_products, counts[0], counts[1], WAVE_STEP, rows)
+    return tree_scatter(operands, produce, plan, collective_id)
+
+
+def final_entries(step, rows, ins, piece, core, put):
+    part = ins[0]
+    rest_count = len(part.shape) - 4
+    columns_here = pl.ds(pl.multiple_of(piece * step, step), step)
+    for number in range(2 ** (rest_count + 1)):
+        at = tuple((number >> place) % 2 for place in reversed(range(rest_count + 1)))
+        put(at, part[at[:1] + (core,) + at[1:] + (slice(None), columns_here)].astype(jnp.float32))
+
+
+def scatter_final(part, collective_id):
+    bits = device_bits()
+    n_dev, step, width = (2 ** len(bits), 128, part.shape[1])
+    rows_all = part.shape[0] // n_dev
+    turns = max(1, n_dev // 32)
+    rows = rows_all // turns
+    plan = {"waves": width // (2 * step), "slots": width // step, "step": step, "rows": rows}
+    sums = []
+    for turn in range(turns):
+        some = part.reshape(n_dev, rows_all, width)[:, turn * rows : (turn + 1) * rows]
+        operand = some.reshape((2,) * len(bits) + (rows, width))
+        produce = functools.partial(final_entries, step, rows)
+        sums.append(tree_scatter([operand], produce, plan, collective_id + turn))
+    return jnp.concatenate(sums, axis=0)
+
+
+def lookup_plan(ids, live, rows_here):
+    count = ids.shape[0]
+    owner = ids // rows_here
+    same = (ids[:, None] == ids[None, :]) & live[None, :]
+    earlier = jnp.arange(count)[None, :] < jnp.arange(count)[:, None]
+    first = live & ~jnp.any(same & earlier, axis=1)
+    below = first[None, :] & (owner[:, None] == owner[None, :]) & (ids[None, :] < ids[:, None])
+    rank = jnp.sum(below.astype(jnp.int32), axis=1)
+    rounds = jnp.max(jnp.where(live, rank, 0)) // SLOTS + 1
+    return (owner, ids - owner * rows_here, first, live, rank, rounds)
+
+
+def round_flat(plan, turn):
+    owner, _, _, live, rank, _ = plan
+    slot = rank - turn * SLOTS
+    return jnp.where(live & (slot >= 0) & (slot < SLOTS), owner * SLOTS + slot, -1)
+
+
+def round_requests(plan, turn, n_dev):
+    flat = round_flat(plan, turn)
+    hit = (flat[:, None] == jnp.arange(n_dev * SLOTS)[None, :]) & plan[2][:, None]
+    return jnp.sum(jnp.where(hit, plan[1][:, None] + 1, 0), axis=0) - 1
+
+
+def picking(plan, turn, n_dev):
+    return (
+        round_flat(plan, turn)[:, None] == jnp.arange(n_dev * SLOTS)[None, :]
+    ).astype(jnp.bfloat16)
+
+
+def asked_hot(asked, rows_here):
+    return (asked.reshape(-1)[:, None] == jnp.arange(rows_here)[None, :]).astype(jnp.bfloat16)
+
+
+def mine_of(table):
+    return lax.dynamic_slice_in_dim(table, lax.axis_index(AXES) * SLOTS, SLOTS, axis=1)
+
+
+def swap(rows, n_dev):
+    wide = rows.shape[-1]
+    return lax.all_to_all(
+        rows.reshape(n_dev, SLOTS, wide), AXES, 0, 0, tiled=True
+    ).reshape(n_dev * SLOTS, wide)
+
+
+def deliver(asked, pick, tables, n_dev):
+    hot = asked_hot(asked, tables[0].shape[0])
+    rows = jnp.concatenate([to_low(matmul(hot, table)) for table in tables], axis=1)
+    return matmul(pick, swap(rows, n_dev))
+
+
+def fetch_rows(plan, asked, rounds, tables, n_dev):
+    rows = deliver(asked, picking(plan, 0, n_dev), tables, n_dev)
+
+    def more(state):
+        turn, rows = state
+        asked = mine_of(lax.all_gather(round_requests(plan, turn, n_dev), AXES, axis=0))
+        return (turn + 1, rows + deliver(asked, picking(plan, turn, n_dev), tables, n_dev))
+
+    return lax.while_loop(lambda state: state[0] < rounds, more, (jnp.int32(1), rows))[1]
+
+
+def collect(asked, pick, gradient, rows_here, n_dev):
+    sums = to_low(jnp.einsum("nk,nd->kd", pick, gradient, preferred_element_type=jnp.float32))
+    return jnp.einsum(
+        "kc,kd->cd",
+        asked_hot(asked, rows_here),
+        swap(sums, n_dev),
+        preferred_element_type=jnp.float32,
+    )
+
+
+def return_rows(plan, asked, rounds, gradient, rows_here, n_dev):
+    gradient = to_low(gradient)
+    sums = collect(asked, picking(plan, 0, n_dev), gradient, rows_here, n_dev)
+
+    def more(state):
+        turn, sums = state
+        asked = mine_of(lax.all_gather(round_requests(plan, turn, n_dev), AXES, axis=0))
+        pick = picking(plan, turn, n_dev)
+        return (turn + 1, sums + collect(asked, pick, gradient, rows_here, n_dev))
+
+    return lax.while_loop(lambda state: state[0] < rounds, more, (jnp.int32(1), sums))[1]
+
+
+ENC_BLOCKS = ((0, 3 * D), (3 * D, D), (9 * D, 2 * D), (12 * D, FF), (12 * D + FF, FF))
+DEC_BLOCKS = (
+    (4 * D, 3 * D),
+    (7 * D, D),
+    (8 * D, D),
+    (11 * D, D),
+    (12 * D + 2 * FF, FF),
+    (12 * D + 3 * FF, FF),
+)
+
+
+def gather_offloaded(shard, blocks):
+    part = jnp.concatenate([shard[:, low : low + width] for low, width in blocks], axis=1)
+    part = lax.all_gather(part, AXES, axis=0, tiled=True)
+    gathered, at = ([], 0)
+    for _, width in blocks:
+        gathered.append(part[:, at : at + width])
+        at += width
+    return gathered
+
+
+def after(values, *others):
+    return lax.optimization_barrier((values,) + others)[0]
+
+
+def columns(layer_full, first_column, column_count):
+    assert layer_full[first_column].shape[1] == column_count
+    return layer_full[first_column]
+
+
+def by_column(blocks, gathered):
+    return {low: value for (low, _), value in zip(blocks, gathered)}
+
+
+def shard_stats(final_rows, table_shard, targets, collective_ids):
+    all_rows = gather_whole(final_rows, 128, collective_ids[0]).reshape(-1, D)
+    logits = jnp.einsum("rd,vd->rv", all_rows, table_shard, preferred_element_type=jnp.float32)
+    low = lax.axis_index(AXES) * table_shard.shape[0]
+    hot = (targets - low)[:, None] == jnp.arange(table_shard.shape[0])[None, :]
+    largest = jnp.max(logits, axis=1)
+    total = jnp.sum(jnp.exp(logits - largest[:, None]), axis=1)
+    picked = jnp.sum(jnp.where(hot, logits, 0.0), axis=1)
+    stats = jnp.stack([largest, total, picked, picked]).reshape(8, -1)
+    stats = gather_whole(stats, stats.shape[1], collective_ids[1]).reshape(-1, 4, largest.shape[0])
+    peak = jnp.max(stats[:, 0], axis=0)
+    log_own = peak + jnp.log(jnp.sum(stats[:, 1] * jnp.exp(stats[:, 0] - peak), axis=0))
+    return (jnp.sum(stats[:, 2], axis=0) - log_own, log_own, logits, hot, all_rows)
+
+
+def forward(token_rows, layer_full, gain_rows, batch_data):
     (
         prompt_ids,
         decoder_input,
@@ -225,7 +696,8 @@
         valid,
     ) = batch_data
     pairs_here, seat_count = (prompt_ids.shape[0], decoder_input.shape[0])
-    encoder_input = embed_full[prompt_ids.reshape(-1)].astype(jnp.float32)
+    prompt_count = prompt_ids.size
+    encoder_input = token_rows[:prompt_count]
     encoder_one, encoder_attn = self_forward(
         encoder_input,
         gain_rows[0],
@@ -244,7 +716,7 @@
     cross_memory = to_low(matmul(encoder_final, columns(layer_full, 9 * D, 2 * D))).reshape(
         pairs_here, P_MAX, 2 * D
     )
-    decoder_zero = embed_full[decoder_input.reshape(-1)].astype(jnp.float32)
+    decoder_zero = token_rows[prompt_count:]
     decoder_one, decoder_attn = self_forward(
         decoder_zero,
         gain_rows[3],
@@ -286,26 +758,6 @@
         decoder_ffn,
     )
     return (final_rows, stored)
-
-
-def log_probs(final_rows, table_full, targets, valid):
-    seat_count = valid.shape[0]
-    target_rows = table_full[targets.reshape(-1)]
-    picked = jnp.sum(final_rows.astype(jnp.float32) * target_rows.astype(jnp.float32), axis=1)
-    logits = jnp.einsum("rd,vd->rv", final_rows, table_full, preferred_element_type=jnp.float32)
-    log_own = jax.nn.logsumexp(logits, axis=1)
-    kept = (logits, log_own)
-    token_logp = jnp.where(valid.reshape(-1), picked - log_own, 0.0)
-    return (jnp.sum(token_logp.reshape(seat_count, -1), axis=1), kept)
-
-
-def head_back(table_full, targets, row_weight, kept):
-    logits, log_own = kept
-    target_hot = (targets.reshape(-1, 1) == jnp.arange(table_full.shape[0])[None, :]).astype(
-        jnp.float32
-    )
-    grad_logits = to_low(row_weight[:, None] * (target_hot - jnp.exp(logits - log_own[:, None])))
-    return (matmul(grad_logits, table_full), grad_logits, grad_logits)
 
 
 def backward(layer_full, gain_rows, batch_data, stored, grad_final):
@@ -435,12 +887,15 @@
     frozen_layers,
     frozen_gains,
 ):
+    n_dev = lax.axis_size(AXES)
+    me = lax.axis_index(AXES)
+    rows_here = policy_embed.shape[0]
     pairs_here = prompt_ids.shape[0]
     seat_count = response_ids.shape[0]
     decoder_input = jnp.concatenate(
         [jnp.zeros((seat_count, 1), jnp.int32), response_ids[:, :-1]], axis=1
     )
-    pair_local = sequence_pair - lax.axis_index(("dp", "fsdp")) * pairs_here
+    pair_local = sequence_pair - me * pairs_here
     select_float = (pair_local[:, None] == jnp.arange(pairs_here)[None, :]).astype(jnp.float32)
     prompt_pos = jnp.arange(P_MAX)
     reply_pos = jnp.arange(R_MAX)
@@ -460,82 +915,106 @@
         to_low(select_float),
         valid,
     )
-    micro_range = jnp.arange(MICRO)
-    pair_micro = (pair_microbatch[:, None] == micro_range[None, :]).astype(jnp.float32)
-    seat_micro = jnp.einsum("sp,pm->sm", select_float, pair_micro, precision=HIGHEST)
-    chosen_float = chosen_flag.astype(jnp.float32)
-    token_local = jnp.einsum(
-        "sm,s->m",
-        seat_micro,
-        chosen_float * response_lengths.astype(jnp.float32),
-        precision=HIGHEST,
-    )
-    pair_total, token_total = lax.psum((jnp.sum(pair_micro, axis=0), token_local), ("dp", "fsdp"))
+    token_ids = jnp.concatenate([prompt_ids.reshape(-1), decoder_input.reshape(-1)])
+    token_live = jnp.concatenate([prompt_keys.reshape(-1), valid.reshape(-1)])
+    plan = lookup_plan(token_ids, token_live, rows_here)
+    packed = jnp.concatenate(
+        [
+            round_requests(plan, 0, n_dev),
+            response_ids.reshape(-1),
+            response_lengths,
+            pair_local,
+            chosen_flag,
+            pair_microbatch,
+            plan[5][None],
+        ]
+    )
+    packed = jnp.pad(packed, (0, -packed.shape[0] % 1024)).reshape(8, -1)
+    notes = gather_whole(packed, packed.shape[1], 0).reshape(n_dev, -1)
+    asked = mine_of(notes)
+    at = n_dev * SLOTS
+    cuts = []
+    for width in (seat_count * R_MAX, seat_count, seat_count, seat_count, pairs_here, 1):
+        cuts.append(notes[:, at : at + width])
+        at += width
+    targets, all_lengths, all_pair, all_flag, all_micro, all_rounds = cuts
+    targets = targets.reshape(-1)
+    rounds = jnp.max(all_rounds)
+    all_select = (all_pair[:, :, None] == jnp.arange(pairs_here)).astype(jnp.float32)
+    pair_micro = (all_micro[:, :, None] == jnp.arange(MICRO)).astype(jnp.float32)
+    seat_micro = jnp.sum(all_select[:, :, :, None] * pair_micro[:, None], axis=2)
+    chosen_float = all_flag.astype(jnp.float32)
+    pair_total = jnp.sum(pair_micro, axis=(0, 1))
+    token_total = jnp.sum(
+        seat_micro * (chosen_float * all_lengths.astype(jnp.float32))[:, :, None], axis=(0, 1)
+    )
     micro_counts = jnp.stack([pair_total, token_total])
-    pair_divisor = jnp.einsum("pm,m->p", pair_micro, pair_total, precision=HIGHEST)
-    sequence_divisor = jnp.einsum("sm,m->s", seat_micro, token_total, precision=HIGHEST)
-    frozen_full = (
-        lax.all_gather(frozen_embed, ("dp", "fsdp"), axis=0, tiled=True),
-        lax.all_gather(frozen_layers, ("dp", "fsdp"), axis=0, tiled=True),
-    )
-    frozen_rows, unused = forward(frozen_full[0], frozen_full[1], frozen_gains, batch_data)
-    frozen_logp, frozen_kept = log_probs(frozen_rows, frozen_full[0], response_ids, valid)
-    frozen_mean = frozen_logp / response_lengths.astype(jnp.float32)
-    policy_shard = to_low(policy_embed)
-    policy_full = (
-        lax.all_gather(policy_shard, ("dp", "fsdp"), axis=0, tiled=True),
-        lax.all_gather(to_low(policy_layers), ("dp", "fsdp"), axis=0, tiled=True),
-    )
-    policy_rows, stored = forward(policy_full[0], policy_full[1], policy_gains, batch_data)
-    policy_logp, head_kept = log_probs(policy_rows, policy_full[0], response_ids, valid)
+    pair_divisor = jnp.sum(pair_micro * pair_total, axis=2)
+    sequence_divisor = jnp.sum(seat_micro * token_total, axis=2)
+    all_valid = reply_pos < all_lengths[:, :, None]
+
+    policy_table = to_low(policy_embed)
+    both_rows = fetch_rows(plan, asked, rounds, (policy_table, frozen_embed), n_dev)
+    policy_low = after(to_low(policy_layers), notes)
+    policy_enc = tree_gather(policy_low, ENC_BLOCKS, WAVE_STEP, 1)
+    frozen_low = after(frozen_layers, policy_enc[0])
+    policy_dec = tree_gather(after(policy_low, policy_enc[0]), DEC_BLOCKS, WAVE_STEP, 2)
+    frozen_enc = gather_offloaded(frozen_low, ENC_BLOCKS)
+    frozen_dec = gather_offloaded(after(frozen_low, frozen_enc[0]), DEC_BLOCKS)
+    policy_layer_full = by_column(ENC_BLOCKS + DEC_BLOCKS, policy_enc + policy_dec)
+    frozen_layer_full = by_column(ENC_BLOCKS + DEC_BLOCKS, frozen_enc + frozen_dec)
+
+    def logp_of(token_logp):
+        return jnp.sum(jnp.where(all_valid, token_logp.reshape(all_valid.shape), 0.0), axis=2)
+
+    policy_rows, stored = forward(both_rows[:, :D], policy_layer_full, policy_gains, batch_data)
+    token_logp, log_own, logits, hot, all_rows = shard_stats(
+        policy_rows, policy_table, targets, (3, 4)
+    )
+    policy_logp = logp_of(token_logp)
+    frozen_rows, unused = forward(both_rows[:, D:], frozen_layer_full, frozen_gains, batch_data)
+    frozen_logp = logp_of(shard_stats(frozen_rows, frozen_embed, targets, (5, 6))[0])
+    frozen_mean = lax.dynamic_index_in_dim(
+        frozen_logp / all_lengths.astype(jnp.float32), me, 0, keepdims=False
+    )
+
     sign_value = 2.0 * chosen_float - 1.0
-    margin = PREFERENCE_BETA * jnp.einsum(
-        "sp,s->p", select_float, sign_value * (policy_logp - frozen_logp), precision=HIGHEST
-    )
-    loss_local = (
+    margin = PREFERENCE_BETA * jnp.sum(
+        all_select * (sign_value * (policy_logp - frozen_logp))[:, :, None], axis=1
+    )
+    loss = (
         jnp.sum(jax.nn.softplus(-margin) / pair_divisor)
         - CHOSEN_WEIGHT * jnp.sum(chosen_float * policy_logp / sequence_divisor)
     ) / MICRO
     pair_slope = -PREFERENCE_BETA * jax.nn.sigmoid(-margin) / pair_divisor
     sequence_slope = (
-        sign_value * jnp.einsum("sp,p->s", select_float, pair_slope, precision=HIGHEST)
+        sign_value * jnp.sum(all_select * pair_slope[:, None, :], axis=2)
         - CHOSEN_WEIGHT * chosen_float / sequence_divisor
     ) / MICRO
-    row_weight = (sequence_slope[:, None] * valid).reshape(-1)
-    back_full = (
-        lax.all_gather(policy_shard, ("dp", "fsdp"), axis=0, tiled=True),
-        lax.all_gather(to_low(policy_layers), ("dp", "fsdp"), axis=0, tiled=True),
-    )
-    grad_final, logit_embed, grad_logits = head_back(
-        back_full[0], response_ids, row_weight, head_kept
-    )
+    row_weight = (sequence_slope[:, :, None] * all_valid).reshape(-1)
+
+    grad_logits = to_low(
+        row_weight[:, None] * (hot.astype(jnp.float32) - jnp.exp(logits - log_own[:, None]))
+    )
+    grad_final = scatter_final(to_low(matmul(grad_logits, policy_table)), 10)
+    table_grad = jnp.einsum("rc,rd->cd", grad_logits, all_rows, preferred_element_type=jnp.float32)
     gain_grads, layer_pairs, grad_encoder_input, grad_decoder_input = backward(
-        back_full[1], policy_gains, batch_data, stored, grad_final
-    )
-    token_ids = jnp.concatenate([prompt_ids.reshape(-1), decoder_input.reshape(-1)])
+        policy_layer_full, policy_gains, batch_data, stored, grad_final
+    )
     token_gradient = jnp.concatenate([grad_encoder_input, grad_decoder_input], axis=0)
-    indicator = (
-        token_ids[:, None]
-        == jnp.arange(lax.axis_size(("dp", "fsdp")) * policy_embed.shape[0])[None, :]
-    ).astype(jnp.float32)
-    embed_grad = lax.psum_scatter(
-        jnp.einsum("nc,nd->cd", indicator, token_gradient, precision=HIGHEST)
-        + jnp.einsum("rc,rd->cd", grad_logits, policy_rows, preferred_element_type=jnp.float32),
-        ("dp", "fsdp"),
-        scatter_dimension=0,
-        tiled=True,
-    )
-    pieces = [
-        jnp.einsum("rc,re->ce", left_side, right_side, preferred_element_type=jnp.float32)
-        for left_side, right_side in layer_pairs
-    ]
-    layer_grad = lax.psum_scatter(
-        jnp.concatenate(pieces, axis=1), ("dp", "fsdp"), scatter_dimension=0, tiled=True
-    )
+    embed_grad = table_grad + return_rows(plan, asked, rounds, token_gradient, rows_here, n_dev)
+    enc_pairs = [layer_pairs[place] for place in (0, 1, 5, 7, 8)]
+    dec_pairs = [layer_pairs[place] for place in (2, 3, 4, 6, 9, 10)]
+    scattered = scatter_layers(dec_pairs, enc_pairs, policy_layers.shape[0], 8)
+    edges, at = ({}, 0)
+    for low, width in DEC_BLOCKS + ENC_BLOCKS:
+        edges[low] = scattered[:, at : at + width]
+        at += width
+    layer_grad = jnp.concatenate([edges[low] for low in sorted(edges)], axis=1)
     squares_local = jnp.sum(embed_grad * embed_grad) + jnp.sum(layer_grad * layer_grad)
-    gain_total, squares_total, loss = lax.psum(
-        (gain_grads, squares_local, loss_local), ("dp", "fsdp")
-    )
+    shared = jnp.concatenate([gain_grads, jnp.full((1, D), squares_local)], axis=0)
+    shared = jnp.sum(gather_whole(shared, D, 9), axis=0)
+    gain_total, squares_total = (shared[:7], shared[7, 0])
     grad_norm = jnp.sqrt(squares_total + jnp.sum(gain_total * gain_total))
     factor = jnp.minimum(1.0, CLIP_NORM / grad_norm)
     embed_new = apply_update(policy_embed, momentum_embed, average_embed, embed_grad, factor)

time: 7170 us -> 1660 us (0.23)
  blocking collectives: 5070 us -> 0 us
  waiting for transfers between devices: 1150 us -> 116 us
  Pallas kernels: 0 us -> 958 us
  matrix products: 592 us -> 282 us
  local copies, waits for them, and re-layouts: 250 us -> 149 us
    unnamed x1 -> x0, blocking collectives: 4980 us -> none
    all_gather x4 -> x2, waiting for transfers between devices: 1140 us -> 88.7 us  [gather_offloaded(): part = lax.all_gather(part, AXES, axis=0, tiled=True)]
    pallas_call x0 -> x10, Pallas kernels: none -> 958 us  [the longest x8 660 us: tree_gather(): pl.pallas_call(functools.partial(gather_kernel, bits, waves), out_shape=[...]
    dot_general x21 -> x5, matrix products: 340 us -> 51.3 us  [the longest x2 27.1 us: shard_stats(): jnp.einsum('rd,vd->rv', all_rows, table_shard, preferred_element_type=jnp...]
    psum x2 -> x0, blocking collectives: 86.6 us -> none  [the longest x1 44.7 us: body(): lax.psum((jnp.sum(pair_micro, axis=0), token_local), ('dp', 'fsdp'))]
    unnamed x342 -> x380, local copies, waits for them, and re-layouts: 123 us -> 44.6 us
  transfers between devices with their start and end apart: 6 -> 4, of which waited for: 5 -> 2; matrix products, arithmetic and copies ran while one was open for 75% -> 4% of each run, Pallas kernels for 0% -> 20%
where the time goes in v1:
time: 1660 us; the launch traced here: 1650 us
  Pallas kernels  958 us (58%)
  matrix products  282 us (17%)
  local copies, waits for them, and re-layouts  149 us (9%)
  waiting for transfers between devices  116 us (7%)
  other arithmetic  109 us (7%)
  between operations  25.5 us (2%)
    pallas_call x8, Pallas kernels, tree_gather(): pl.pallas_call(functools.partial(gather_kernel, bits, waves), out_shape=[...  660 us
    pallas_call x2, Pallas kernels, tree_scatter(): pl.pallas_call(functools.partial(scatter_kernel, bits, plan, produce), ou...  298 us
    dot_general x22, matrix products, matmul(): return jnp.dot(left_side, right_side, preferred_element_type=jnp.float32)  93.3 us
    all_gather x2, waiting for transfers between devices, gather_offloaded(): part = lax.all_gather(part, AXES, axis=0, tiled=True)  88.7 us
    unnamed x380, local copies, waits for them, and re-layouts  44.6 us
    dot_general x4, matrix products, feed_forward(): jnp.einsum('rf,df->rd', active, weight_out, preferred_element_type=jnp.fl...  40.5 us
    dot_general x9, matrix products, matmul_back(): jnp.einsum('re,de->rd', grad_low, weight, preferred_element_type=jnp.floa...  34.3 us
  transfers between devices with their start and end apart: 4, of which 2 were waited for; matrix products, arithmetic and copies ran while one was open for 4% of the time, Pallas kernels for 20%

profile of v1, /device:TPU:0, one launch (start us, length us, event | category | flops | bytes accessed | tf_op | source)
XLA Modules:
  0.0 1649.9 jit_solution(7796561860327490456)
XLA Ops:
  17.6 18.6 %shard_map.282 = s32[2,2,2,2,2,8,128]{6,5,4,3,2,1,0:T(8,128)} custom-call(s32[1,1,1,1,1,8,128]{6,5,4,3,2,1,0:T(8,128)} %pad_bitcast_fusion.x_ref), custom_call_target="tpu_custom_call" | custom-call | tf_op jit(solution)/shard_map/pallas_call | solution.py:330
  40.6 126.2 %shard_map.283 = (bf16[2,2,2,2,2,32,3072]{6,5,4,3,2,1,0:T(8,128)(2,1)}, bf16[2,2,2,2,2,32,1024]{6,5,4,3,2,1,0:T(8,128)(2,1)}, bf16[2,2,2,2,2,32,2048]{6,5,4,3,2,...) custom-call(bf16[1,1,1,1,1,32,28672]{6,5,4,3,2,1,0:T(8,128)(2,1)} %bitcast.326), custom_call_target="tpu_custom_call" | custom-call | tf_op jit(solution)/shard_map/pallas_call | solution.py:330
  183.1 324.1 %shard_map.284 = (bf16[2,2,2,2,2,32,3072]{6,5,4,3,2,1,0:T(8,128)(2,1)}, bf16[2,2,2,2,2,32,1024]{6,5,4,3,2,1,0:T(8,128)(2,1)}, bf16[2,2,2,2,2,32,1024]{6,5,4,3,2,...) custom-call(bf16[1,1,1,1,1,32,28672]{6,5,4,3,2,1,0:T(8,128)(2,1)} %b, ...), custom_call_target="tpu_custom_call" | custom-call | tf_op jit(solution)/shard_map/pallas_call | solution.py:330
  512.0 3.8 fusion.87
  518.7 6.0 convolution_convert_fusion.3
  529.7 4.0 convolution_convert_fusion.4
  549.3 4.0 fusion.40
  561.8 88.7 %all-gather.11.cloned.1.call-done = bf16[1024,14336]{1,0:T(8,128)(2,1)} async-done(((bf16[32,14336]{1,0:T(8,128)(2,1)}), bf16[1024,14336]{1,0:T(8,128)(2,1)}) %all-gather.11.cloned.1.call-update) | async-done | bytes 29360144 | tf_op jit(solution)/shard_map/all_gather | solution.py:651
  650.6 6.1 convolution_convert_fusion.2
  662.2 4.8 fusion.37
  673.4 4.2 multiply_reduce_fusion.11
  677.6 14.7 multiply_reduce_fusion.10
  692.4 4.4 fusion.98
  699.6 4.5 fusion.52
  719.4 4.1 copy.323
  729.3 10.2 multiply_reduce_fusion.25
  739.6 6.1 fusion.242
  745.7 8.5 multiply_reduce_fusion.13
  761.5 4.1 copy.307
  769.1 49.7 %shard_map.287 = bf16[2,2,2,2,2,128,1024]{6,5,4,3,2,1,0:T(8,128)(2,1)} custom-call(bf16[1,1,1,1,1,128,1024]{6,5,4,3,2,1,0:T(8,128)(2,1)} %fusion.187.x_ref), custom_call_target="tpu_custom_call" | custom-call | tf_op jit(solution)/shard_map/pallas_call | solution.py:330
  818.8 15.3 fusion.273
  841.2 4.7 fusion.239
  845.9 7.1 multiply_reduce_fusion.29
  854.6 50.5 %shard_map.285 = bf16[2,2,2,2,2,128,1024]{6,5,4,3,2,1,0:T(8,128)(2,1)} custom-call(bf16[1,1,1,1,1,128,1024]{6,5,4,3,2,1,0:T(8,128)(2,1)} %fusion.186.x_ref), custom_call_target="tpu_custom_call" | custom-call | tf_op jit(solution)/shard_map/pallas_call | solution.py:330
  905.1 11.9 fusion.266
  917.0 15.4 exponential_reduce_fusion.1
  933.8 35.4 %shard_map.288 = f32[2,2,2,2,2,8,2048]{6,5,4,3,2,1,0:T(8,128)} custom-call(f32[1,1,1,1,1,8,2048]{6,5,4,3,2,1,0:T(8,128)} %reshape_reshape.26.x_ref), custom_call_target="tpu_custom_call" | custom-call | tf_op jit(solution)/shard_map/pallas_call | solution.py:330
  972.5 35.3 %shard_map.286 = f32[2,2,2,2,2,8,2048]{6,5,4,3,2,1,0:T(8,128)} custom-call(f32[1,1,1,1,1,8,2048]{6,5,4,3,2,1,0:T(8,128)} %reshape_reshape.24.x_ref), custom_call_target="tpu_custom_call" | custom-call | tf_op jit(solution)/shard_map/pallas_call | solution.py:330
  1011.1 7.9 fusion.257
  1024.1 16.2 convolution_convert_fusion.1
  1040.3 56.3 %shard_map.289 = f32[128,1024]{1,0:T(8,128)} custom-call(bf16[2,2,2,2,2,128,1024]{6,5,4,3,2,1,0:T(8,128)(2,1)} %bitcast.342), custom_call_target="tpu_custom_call" | custom-call | tf_op jit(solution)/shard_map/pallas_call | solution.py:465
  1100.5 4.7 fusion.32
  1105.2 7.4 multiply_reduce_fusion.19
  1147.3 3.8 copy.335
  1151.1 4.9 copy.334
  1156.0 8.9 fusion.55
  1170.1 7.2 select_convert_fusion
  1187.5 4.5 fusion.99
  1211.1 7.4 multiply_reduce_fusion.4
  1227.6 5.4 multiply_reduce_fusion.17
  1272.5 241.8 %shard_map.290 = f32[32,28672]{1,0:T(8,128)} custom-call(bf16[6,2,2,256,128]{4,3,2,1,0:T(8,128)(2,1)} %copy-done.58, bf16[128,14336]{1,0:T(8,128)(2,1)} %fusion.184.refs_1_, bf16[5,2,2,256,384]{4,3,2,1,0:T(8,128)(2,1)} %copy-done.31, bf16[384,14336]{1,0:T(8,128)(2,1)} %fusion.130.refs_3_), custom_call_target="tpu_custom_call" | custom-call | tf_op jit(solution)/shard_map/pallas_call | solution.py:465
  1523.8 5.4 all-to-all-start.3
  1541.0 27.1 %all-to-all-done.3 = bf16[32,24,1024]{2,1,0:T(8,128)(2,1)S(1)} async-done(((bf16[32,24,1024]{2,1,0:T(8,128)(2,1)}), bf16[32,24,1024]{2,1,0:T(8,128)(2,1)S(1)}, u32[]{:S(2)}, u32[]{:S(2)}) %all-to-all-start.3) | async-done | bytes 1572896 | tf_op jit(solution)/shard_map/all_to_all | solution.py:593
  1568.1 3.9 fusion.48
  1573.1 18.0 %multiply_reduce_fusion.1 = (f32[]{:T(128)}, f32[1004,1024]{1,0:T(8,128)}) fusion(f32[1004,1024]{1,0:T(8,128)} %get-tuple-element.288, bf16[4096,1024]{1,0:T(8,128)(2,1)} %bitcast.340, f32[4096,1004]{0,1:T(8,128)} %copy-done.8, f32[4096]{0:T(1024)S(1)} %copy-done.134, f32[4096]{0:T(1024)S(1)} %copy-done.136, s32[4096]{0:T(1024)S(1)} %copy-done.105), kind=kOutput, calls=%fused_computation.75 | convolution fusion | flops 8449921024 | bytes 33112068 | tf_op jit(solution)/shard_map/rc,rd->cd/dot_general | solution.py:1000
  1593.1 19.8 %shard_map.291 = f32[2,2,2,2,2,8,1024]{6,5,4,3,2,1,0:T(8,128)} custom-call(f32[1,1,1,1,1,8,1024]{6,5,4,3,2,1,0:T(8,128)} %bitcast.393), custom_call_target="tpu_custom_call" | custom-call | tf_op jit(solution)/shard_map/pallas_call | solution.py:330
  1617.4 10.4 add_multiply_fusion.2
  1627.8 12.6 add_multiply_fusion
  (648 shorter events, 278.3 us)
Async XLA Ops:
  7.2 542.2 %all-gather.13.cloned.1.call-start = ((), (), s32[]{:S(2)}) async-start(), calls=%async_computation.5 | async-start | bytes 30277632 | tf_op jit(solution)/shard_map/all_gather | solution.py:651
  9.6 682.8 %copy-start.112 = (pred[2,192]{1,0:T(4,128)(4,1)}, pred[2,192]{1,0:T(4,128)(4,1)S(1)}, u32[]{:S(2)}) copy-start(pred[2,192]{1,0:T(4,128)(4,1)S(1)} %iota_compare_fusion.33) | copy-start | bytes 1156
  13.2 498.9 %copy-start.141 = (s32[512]{0:T(512)}, s32[512]{0:T(512)S(1)}, u32[]{:S(2)}) copy-start(s32[512]{0:T(512)S(1)} %get-tuple-element.439) | copy-start | bytes 6148
  40.6 126.2 %slice-start.8 = ((bf16[32,28672]{1,0:T(8,128)(2,1)}), bf16[32,1024]{1,0:T(8,128)(2,1)S(1)}, s32[]{:S(2)}) async-start(bf16[32,28672]{1,0:T(8,128)(2,1)} %param.40), calls=%async_computation.14 | async-start | bytes 131072 | tf_op jit(solution)/shard_map/slice | solution.py:650
  40.6 126.2 %slice-start.9 = ((bf16[32,28672]{1,0:T(8,128)(2,1)}), bf16[32,5120]{1,0:T(8,128)(2,1)S(1)}, s32[]{:S(2)}) async-start(bf16[32,28672]{1,0:T(8,128)(2,1)} %param.40), calls=%async_computation.15 | async-start | bytes 655360 | tf_op jit(solution)/shard_map/slice | solution.py:650
  40.6 126.2 %slice-start.10 = ((bf16[32,28672]{1,0:T(8,128)(2,1)}), bf16[32,8192]{1,0:T(8,128)(2,1)S(1)}, s32[]{:S(2)}) async-start(bf16[32,28672]{1,0:T(8,128)(2,1)} %param.40), calls=%async_computation.16 | async-start | bytes 1048576 | tf_op jit(solution)/shard_map/slice | solution.py:650
  167.8 482.7 %all-gather.11.cloned.1.call-start = ((), (), s32[]{:S(2)}) async-start(), calls=%async_computation.4 | async-start | bytes 30277632 | tf_op jit(solution)/shard_map/all_gather | solution.py:651
  177.8 331.5 %copy-start.162 = (s32[2]{0:T(128)S(1)}, s32[2]{0:T(128)}, u32[]{:S(2)}) copy-start(s32[2]{0:T(128)} %param.24) | copy-start | bytes 28
  177.8 331.7 %copy-start.96 = (f32[7,1024]{1,0:T(8,128)S(1)}, f32[7,1024]{1,0:T(8,128)}, u32[]{:S(2)}) copy-start(f32[7,1024]{1,0:T(8,128)} %param.32) | copy-start | bytes 86020
  177.8 333.6 %copy-start.118 = (f32[7,1024]{1,0:T(8,128)S(1)}, f32[7,1024]{1,0:T(8,128)}, u32[]{:S(2)}) copy-start(f32[7,1024]{1,0:T(8,128)} %param.41) | copy-start | bytes 86020
  177.8 334.3 %all-to-all-start.2 = ((bf16[32,24,2048]{2,1,0:T(8,128)(2,1)}), bf16[32,24,2048]{2,1,0:T(8,128)(2,1)S(1)}, u32[]{:S(2)}, u32[]{:S(2)}) async-start(bf16[32,24,2048]{2,1,0:T(8,128)(2,1)} %bitcast.6), calls=%async_computation.2 | async-start | bytes 6291456 | tf_op jit(solution)/shard_map/all_to_all | solution.py:593
  181.6 334.2 %copy-start.91 = (s32[32,4]{1,0:T(8,128)}, s32[32,4]{1,0:T(8,128)S(1)}, u32[]{:S(2)}) copy-start(s32[32,4]{1,0:T(8,128)S(1)} %get-tuple-element.419) | copy-start | bytes 1540
  181.7 334.1 %copy-start.116 = (s32[32,4]{0,1:T(4,128)}, s32[32,4]{0,1:T(4,128)S(1)}, u32[]{:S(2)}) copy-start(s32[32,4]{0,1:T(4,128)S(1)} %copy.291) | copy-start | bytes 1540
  510.1 19.5 %copy-start.106 = (f32[1,1024]{1,0:T(1,128)}, f32[1,1024]{1,0:T(1,128)S(1)}, u32[]{:S(2)}) copy-start(f32[1,1024]{1,0:T(1,128)S(1)} %get-tuple-element.426) | copy-start | bytes 12292
  510.1 34.6 %copy-start.102 = (f32[1,1024]{1,0:T(1,128)}, f32[1,1024]{1,0:T(1,128)S(1)}, u32[]{:S(2)}) copy-start(f32[1,1024]{1,0:T(1,128)S(1)} %get-tuple-element.422) | copy-start | bytes 12292
  526.9 18.8 %copy-start.12 = (bf16[2,192,1024]{1,2,0:T(8,128)(2,1)}, bf16[2,192,1024]{1,2,0:T(8,128)(2,1)S(1)}, u32[]{:S(2)}) copy-start(bf16[2,192,1024]{1,2,0:T(8,128)(2,1)S(1)} %copy.302) | copy-start | bytes 2359300
  527.9 17.8 %copy-start.14 = (bf16[2,192,1024]{1,2,0:T(8,128)(2,1)}, bf16[2,192,1024]{1,2,0:T(8,128)(2,1)S(1)}, u32[]{:S(2)}) copy-start(bf16[2,192,1024]{1,2,0:T(8,128)(2,1)S(1)} %copy.301) | copy-start | bytes 2359300
  544.7 579.7 %copy-start.9 = (f32[128,1024]{1,0:T(8,128)}, f32[128,1024]{1,0:T(8,128)S(1)}, u32[]{:S(2)}) copy-start(f32[128,1024]{1,0:T(8,128)S(1)} %get-tuple-element.453) | copy-start | bytes 1572868
  545.6 288.5 %copy-start.33 = (bf16[4,32,16,64]{3,2,1,0:T(8,128)(2,1)}, bf16[4,32,16,64]{3,2,1,0:T(8,128)(2,1)S(1)}, u32[]{:S(2)}) copy-start(bf16[4,32,16,64]{3,2,1,0:T(8,128)(2,1)S(1)} %reshape_reshape.23) | copy-start | bytes 786436
  558.4 98.3 %copy-start.163 = (f32[128,1024]{1,0:T(8,128)}, f32[128,1024]{1,0:T(8,128)S(1)}, u32[]{:S(2)}) copy-start(f32[128,1024]{1,0:T(8,128)S(1)} %get-tuple-element.469) | copy-start | bytes 1572868
  670.2 22.2 %copy-start.87 = (f32[2,16,192]{2,1,0:T(8,128)}, f32[2,16,192]{2,1,0:T(8,128)S(1)}, u32[]{:S(2)}) copy-start(f32[2,16,192]{2,1,0:T(8,128)S(1)} %log_add_fusion.4) | copy-start | bytes 73732
  677.6 14.7 copy-start.37
  719.4 20.2 %copy-start.139 = (f32[384]{0:T(512)}, f32[384]{0:T(512)S(1)}, u32[]{:S(2)}) copy-start(f32[384]{0:T(512)S(1)} %fusion.210) | copy-start | bytes 4612
  769.1 49.7 %copy-start.161 = (bf16[1004,1024]{1,0:T(8,128)(2,1)S(1)}, bf16[1004,1024]{1,0:T(8,128)(2,1)}, u32[]{:S(2)}) copy-start(bf16[1004,1024]{1,0:T(8,128)(2,1)} %get-tuple-element.737) | copy-start | bytes 6168580
  818.8 15.3 copy-start.5
  905.1 11.9 copy-start.104
  917.0 15.4 copy-start.8
  1011.1 10.8 copy-start.92
  1011.1 11.1 copy-start.123
  1011.1 11.1 copy-start.143
  1011.1 11.2 copy-start.111
  1011.1 11.4 copy-start.117
  1011.1 11.4 copy-start.148
  1021.8 18.5 %copy-start.133 = (f32[4096]{0:T(1024)}, f32[4096]{0:T(1024)S(1)}, u32[]{:S(2)}) copy-start(f32[4096]{0:T(1024)S(1)} %get-tuple-element.379) | copy-start | bytes 49156
  1024.1 16.2 copy-start.135
  1040.3 56.3 %copy-start.20 = (f32[128,1024]{1,0:T(8,128)S(1)}, f32[128,1024]{1,0:T(8,128)}, u32[]{:S(2)}) copy-start(f32[128,1024]{1,0:T(8,128)} %copy-done.19) | copy-start | bytes 1572868
  1040.3 56.3 %copy-start.108 = (f32[1024]{0:T(1024)S(1)}, f32[1024]{0:T(1024)}, u32[]{:S(2)}) copy-start(f32[1024]{0:T(1024)} %broadcast_multiply_fusion) | copy-start | bytes 12292
  1156.0 14.1 slice-start.4
  1237.3 11.2 copy-start.11
  1238.4 11.1 copy-start.2
  1523.8 44.3 %all-to-all-start.3 = ((bf16[32,24,1024]{2,1,0:T(8,128)(2,1)}), bf16[32,24,1024]{2,1,0:T(8,128)(2,1)S(1)}, u32[]{:S(2)}, u32[]{:S(2)}) async-start(bf16[32,24,1024]{2,1,0:T(8,128)(2,1)} %bitcast.375), calls=%async_computation.3 | async-start | bytes 3145728 | tf_op jit(solution)/shard_map/all_to_all | solution.py:593
  1535.1 33.0 %copy-start.147 = (s32[768]{0:T(1024)S(1)}, s32[768]{0:T(1024)}, u32[]{:S(2)}) copy-start(s32[768]{0:T(1024)} %copy-done.146) | copy-start | bytes 9220
  1573.0 19.4 %copy-start.130 = (f32[1024]{0:T(1024)S(1)}, f32[1024]{0:T(1024)}, u32[]{:S(2)}) copy-start(f32[1024]{0:T(1024)} %get-tuple-element.309) | copy-start | bytes 12292
  1573.0 19.4 %copy-start.131 = (f32[1024]{0:T(1024)S(1)}, f32[1024]{0:T(1024)}, u32[]{:S(2)}) copy-start(f32[1024]{0:T(1024)} %get-tuple-element.311) | copy-start | bytes 12292
  1573.0 19.4 %copy-start.132 = (f32[1024]{0:T(1024)S(1)}, f32[1024]{0:T(1024)}, u32[]{:S(2)}) copy-start(f32[1024]{0:T(1024)} %get-tuple-element.313) | copy-start | bytes 12292
  1573.0 43.7 %copy-start.97 = (f32[7,1024]{1,0:T(8,128)S(1)}, f32[7,1024]{1,0:T(8,128)}, u32[]{:S(2)}) copy-start(f32[7,1024]{1,0:T(8,128)} %param.32) | copy-start | bytes 86020
  1573.0 43.7 %copy-start.114 = (f32[7,1024]{1,0:T(8,128)S(1)}, f32[7,1024]{1,0:T(8,128)}, u32[]{:S(2)}) copy-start(f32[7,1024]{1,0:T(8,128)} %param.38) | copy-start | bytes 86020
  1573.1 43.7 %copy-start.115 = (f32[7,1024]{1,0:T(8,128)S(1)}, f32[7,1024]{1,0:T(8,128)}, u32[]{:S(2)}) copy-start(f32[7,1024]{1,0:T(8,128)} %param.35) | copy-start | bytes 86020
  (135 other events, 615.8 us)
Sparse Core Ops, SparseCore 0:
  167.9 295.1 all-gather.12
  466.7 183.8 all-gather.10

commit v2 on v1

v2 whole, which is shorter than its diff:
```python
import functools

import jax
import jax.numpy as jnp
from jax import lax
from jax.experimental import pallas as pl
from jax.experimental.layout import Layout, with_layout_constraint
from jax.experimental.pallas import tpu as pltpu
from jax.sharding import PartitionSpec as P

D = 1024
HEADS = 16
HEAD = 64
FF = 4096
P_MAX = 192
R_MAX = 32
MICRO = 2


EPSILON = 1e-06
SCORE_SCALE = 0.125
PREFERENCE_BETA = 0.1
CHOSEN_WEIGHT = 1.0
MOMENTUM = 0.9
LEARN_RATE = 2000.0
AVERAGE_DECAY = 0.5
CLIP_NORM = 0.04
MASK_FILL = -1000000000.0
HIGHEST = lax.Precision.HIGHEST


def rms_norm(values, gain_row):
    return (
        values * lax.rsqrt(jnp.mean(values * values, axis=-1, keepdims=True) + EPSILON) * gain_row
    )


def final_norm(values, gain_row):
    return rms_norm(values, gain_row) * D ** (-0.5)


def to_low(values):
    return values.astype(jnp.bfloat16)


def matmul(left_side, right_side):
    return jnp.dot(left_side, right_side, preferred_element_type=jnp.float32)


def matmul_back(grad_low, weight):
    return jnp.einsum("re,de->rd", grad_low, weight, preferred_element_type=jnp.float32)


def split_heads(values):
    return values.reshape(values.shape[0], values.shape[1], HEADS, HEAD)


def scores_of(queries, key_rows, allowed):
    raw_scores = (
        jnp.einsum(
            "bqhe,bkhe->bhqk",
            split_heads(queries),
            split_heads(key_rows),
            preferred_element_type=jnp.float32,
        )
        * SCORE_SCALE
    )
    return jnp.where(allowed[:, None], raw_scores, MASK_FILL)


def attend_forward(queries, key_rows, values, allowed):
    scores = scores_of(queries, key_rows, allowed)
    log_total = jax.nn.logsumexp(scores, axis=-1, keepdims=True)
    softmax_out = to_low(jnp.exp(scores - log_total))
    mixed_out = jnp.einsum(
        "bhqk,bkhe->bqhe", softmax_out, split_heads(values), preferred_element_type=jnp.float32
    )
    return (to_low(mixed_out.reshape(queries.shape)), log_total)


def attend_backward(queries, key_rows, values, allowed, log_total, grad_mixed):
    softmax_out = jnp.exp(scores_of(queries, key_rows, allowed) - log_total)
    grad_heads = split_heads(to_low(grad_mixed))
    grad_values = jnp.einsum(
        "bhqk,bqhe->bhke", to_low(softmax_out), grad_heads, preferred_element_type=jnp.float32
    )
    grad_probs = jnp.einsum(
        "bqhe,bkhe->bhqk", grad_heads, split_heads(values), preferred_element_type=jnp.float32
    )
    grad_scores = to_low(
        softmax_out * (grad_probs - jnp.sum(grad_probs * softmax_out, axis=-1, keepdims=True))
    )
    grad_query = (
        jnp.einsum(
            "bhqk,bkhe->bqhe",
            grad_scores,
            split_heads(key_rows),
            preferred_element_type=jnp.float32,
        )
        * SCORE_SCALE
    )
    grad_keys = (
        jnp.einsum(
            "bhqk,bqhe->bhke", grad_scores, split_heads(queries), preferred_element_type=jnp.float32
        )
        * SCORE_SCALE
    )
    return (grad_query.reshape(queries.shape), grad_keys, grad_values)


def join_heads(values):
    return values.transpose(0, 2, 1, 3).reshape(values.shape[0], values.shape[2], D)


def self_forward(residual, gain_row, weight_three, weight_out, allowed, shape_pair):
    normed = to_low(rms_norm(residual, gain_row))
    triple = to_low(matmul(normed, weight_three)).reshape(shape_pair[0], shape_pair[1], 3 * D)
    mixed_out, log_total = attend_forward(
        triple[..., :D], triple[..., D : 2 * D], triple[..., 2 * D :], allowed
    )
    flat_mixed = mixed_out.reshape(-1, D)
    return (residual + matmul(flat_mixed, weight_out), (normed, triple, log_total, flat_mixed))


def norm_backward(norm, residual, gain_row, grad_normed):
    grad_residual = jax.vjp(lambda values: norm(values, gain_row), residual)[1](grad_normed)[0]
    return grad_residual, grad_normed * norm(residual, jnp.ones_like(gain_row))


def self_backward(residual, gain_row, weight_three, weight_out, allowed, stored, grad_out):
    normed, triple, log_total, flat_mixed = stored
    grad_mixed = matmul_back(to_low(grad_out), weight_out)
    queries = triple[..., :D]
    grad_query, grad_keys, grad_values = attend_backward(
        queries,
        triple[..., D : 2 * D],
        triple[..., 2 * D :],
        allowed,
        log_total,
        grad_mixed.reshape(queries.shape),
    )
    grads = (grad_query, join_heads(grad_keys), join_heads(grad_values))
    grad_triple = jnp.concatenate(grads, axis=-1).reshape(-1, 3 * D)
    grad_normed = matmul_back(to_low(grad_triple), weight_three)
    grad_residual, gain_rows = norm_backward(rms_norm, residual, gain_row, grad_normed)
    return (grad_out + grad_residual, gain_rows, ((normed, grad_triple), (flat_mixed, grad_out)))


def cross_forward(
    residual, gain_row, weight_query, weight_out, cross_memory, pair_local, allowed, shape_pair
):
    normed = to_low(rms_norm(residual, gain_row))
    queries = to_low(matmul(normed, weight_query)).reshape(shape_pair[0], shape_pair[1], D)
    seat_memory = jnp.broadcast_to(cross_memory[:1], (shape_pair[0],) + cross_memory.shape[1:])
    for pair in range(1, cross_memory.shape[0]):
        seat_memory = jnp.where(
            pair_local[:, None, None] == pair, cross_memory[pair][None], seat_memory
        )
    mixed_out, log_total = attend_forward(
        queries, seat_memory[..., :D], seat_memory[..., D:], allowed
    )
    flat_mixed = mixed_out.reshape(-1, D)
    return (
        residual + matmul(flat_mixed, weight_out),
        (normed, queries, seat_memory, log_total, flat_mixed),
    )


def cross_backward(residual, gain_row, weight_query, weight_out, allowed, stored, grad_out):
    normed, queries, seat_memory, log_total, flat_mixed = stored
    grad_mixed = matmul_back(to_low(grad_out), weight_out)
    grad_query, grad_keys, grad_values = attend_backward(
        queries,
        seat_memory[..., :D],
        seat_memory[..., D:],
        allowed,
        log_total,
        grad_mixed.reshape(queries.shape),
    )
    grad_query = grad_query.reshape(-1, D)
    grad_normed = matmul_back(to_low(grad_query), weight_query)
    grad_residual, gain_rows = norm_backward(rms_norm, residual, gain_row, grad_normed)
    return (
        grad_out + grad_residual,
        gain_rows,
        (grad_keys, grad_values),
        ((normed, grad_query), (flat_mixed, grad_out)),
    )


def feed_forward(residual, gain_row, weight_in, weight_out):
    normed = to_low(rms_norm(residual, gain_row))
    before = matmul(normed, weight_in)
    active = to_low(jax.nn.relu(before))
    return (
        residual + jnp.einsum("rf,df->rd", active, weight_out, preferred_element_type=jnp.float32),
        (normed, active),
    )


def feed_backward(residual, gain_row, weight_in, weight_out, stored, grad_out):
    normed, active = stored
    grad_active = matmul(to_low(grad_out), weight_out)
    grad_before = jnp.where(active > 0, grad_active, 0.0)
    grad_normed = matmul_back(to_low(grad_before), weight_in)
    grad_residual, gain_rows = norm_backward(rms_norm, residual, gain_row, grad_normed)
    return (grad_out + grad_residual, gain_rows, ((normed, grad_before), (grad_out, active)))


AXES = ("dp", "fsdp")
SLOTS = 24
MESH = pl.DeviceIdType.MESH
WAVE_STEP = 512


def device_bits():
    bits = []
    for axis in AXES:
        mask = lax.axis_size(axis) // 2
        while mask:
            bits.append((axis, mask))
            mask //= 2
    return bits


def scatter_orders():
    core, across = (("dp", 1), ("dp", 2))
    inner = [bit for bit in reversed(device_bits()) if bit[0] == "fsdp"]
    first, rest = inner[:1], inner[1:]
    return (
        [core, across] + rest + first,
        [core] + inner + [across],
        [core, across] + first + rest,
        [core] + first + [across] + rest,
    )


def wave_orders(wave):
    orders = scatter_orders()
    return orders[2:] if wave % 3 == 1 else orders[:2]


def bit_of(bit):
    axis, mask = bit
    return (lax.axis_index(axis) // mask) % 2


def partner(bit):
    axis, mask = bit
    return {axis: lax.axis_index(axis) + mask * (1 - 2 * bit_of(bit))}


def greet(bits):
    barrier = pltpu.get_barrier_semaphore()
    for bit in bits:
        pl.semaphore_signal(barrier, inc=1, device_id=partner(bit), device_id_type=MESH)
    pl.semaphore_wait(barrier, len(bits))


def gather_kernel(bits, n_in, waves, *refs):
    ins, outs, (own_sem, send_sem, recv_sem) = (refs[:n_in], refs[n_in:-3], refs[-3:])
    mine = {bit: bit_of(bit) for bit in bits}
    depth = len(bits)
    greet(bits)
    index, sent, kept = ({}, {}, {})
    for turn in range(len(waves) + depth):
        for step in range(depth + 1):
            wave = turn - step
            if not 0 <= wave < len(waves):
                continue
            for lane, (number, which, start, low, width, first, count, order) in enumerate(
                waves[wave]
            ):
                slot = index.setdefault((wave, lane), len(index))
                lead = tuple(
                    pl.ds(0, 2) if bit in order[:step] else pl.ds(mine[bit], 1) for bit in bits
                )
                place = outs[which].at[lead + (pl.ds(first, count), pl.ds(low, width))]
                source = place
                if step == 0:
                    whole = (slice(None),) * depth
                    source = ins[number].at[whole + (pl.ds(first, count), pl.ds(start, width))]
                    kept[slot] = pltpu.make_async_copy(source, place, own_sem.at[slot])
                    kept[slot].start()
                else:
                    sent[slot, step - 1].wait_recv()
                if step == 1:
                    kept[slot].wait()
                if step < depth:
                    sent[slot, step] = pltpu.make_async_remote_copy(
                        src_ref=source,
                        dst_ref=place,
                        send_sem=send_sem.at[slot, step],
                        recv_sem=recv_sem.at[slot, step],
                        device_id=partner(order[step]),
                        device_id_type=MESH,
                    )
                    sent[slot, step].start()
    for copy in sent.values():
        copy.wait_send()


def busy_for(micros):
    return pl.CostEstimate(flops=0, bytes_accessed=int(micros * 3.4e6), transcendentals=0)


def tree_gather(shard, blocks, step, collective_id, micros, row_step=None, extra=None):
    bits = device_bits()
    rows = shard.shape[0]
    row_step = row_step or rows
    pieces = []
    for which, (start, width) in enumerate(blocks):
        for low in range(0, width, step):
            for first in range(0, rows, row_step):
                pieces.append((0, which, start + low, low, min(step, width - low), first, row_step))
    waves = []
    for wave in range(-(-len(pieces) // 2)):
        waves.append(
            [
                piece + (tuple(reversed(order)),)
                for piece, order in zip(pieces[2 * wave : 2 * wave + 2], wave_orders(wave))
            ]
        )
    operands = [shard]
    shapes = [((rows, width), shard.dtype) for _, width in blocks]
    if extra is not None:
        operands.append(extra)
        shapes.append((extra.shape, extra.dtype))
        piece = (1, len(blocks), 0, 0, extra.shape[1], 0, extra.shape[0])
        waves[0].append(piece + (tuple(reversed(wave_orders(0)[0])),))
    total = sum(len(wave) for wave in waves)
    gathered = pl.pallas_call(
        functools.partial(gather_kernel, bits, len(operands), waves),
        out_shape=[
            jax.ShapeDtypeStruct((2,) * len(bits) + shape, dtype) for shape, dtype in shapes
        ],
        in_specs=[pl.BlockSpec(memory_space=pl.ANY)] * len(operands),
        out_specs=[pl.BlockSpec(memory_space=pl.ANY)] * len(shapes),
        scratch_shapes=[
            pltpu.SemaphoreType.DMA((total,)),
            pltpu.SemaphoreType.DMA((total, len(bits))),
            pltpu.SemaphoreType.DMA((total, len(bits))),
        ],
        compiler_params=pltpu.CompilerParams(collective_id=collective_id, has_side_effects=True),
        cost_estimate=busy_for(micros),
    )(*[value.reshape((1,) * len(bits) + value.shape) for value in operands])
    return [value.reshape((-1, shape[1])) for value, (shape, _) in zip(gathered, shapes)]


def gather_whole(values, step, collective_id, micros, row_step=None):
    blocks = [(0, values.shape[1])]
    full = tree_gather(values, blocks, step, collective_id, micros, row_step)[0]
    return full.reshape((-1,) + values.shape)


CORE_SLOTS = 4


def scatter_kernel(bits, plan, *refs):
    n_waves, slots, width, wide = (plan["waves"], plan["slots"], plan["step"], plan["wide"])
    n_ins, n_loaded = (plan["operands"], len(plan["loads"]))
    ins, out_ref = (refs[:n_ins], refs[n_ins])
    loaded, rest_refs = (refs[n_ins + 1 : n_ins + 1 + n_loaded], refs[n_ins + 1 + n_loaded :])
    send_core, from_core, total, narrow, arrived, arrived_wide = rest_refs[:6]
    load_sem, send_sem, recv_sem, free_sem = rest_refs[6:]
    depth = len(bits)
    mine = {bit: bit_of(bit) for bit in bits}
    core = scatter_orders()[0][0]
    rest = [bit for bit in bits if bit != core]

    def half(order, step, kept):
        bit_at = {bit: pl.ds(mine[bit], 1) for bit in order[1:step]}
        last = mine[order[step]] if kept else 1 - mine[order[step]]
        bit_at[order[step]] = pl.ds(last, 1)
        return tuple(bit_at.get(bit, pl.ds(0, 2)) for bit in rest)

    def slot_at(piece, step):
        return lax.rem(piece, CORE_SLOTS if step == 0 else slots)

    def copy(piece, step, order):
        slot = slot_at(piece, step)
        if step == 0:
            source, target = (send_core.at[slot], from_core.at[slot])
        else:
            source = (total if step in wide else narrow).at[(slot,) + half(order, step, False)]
            target = arrived_wide if step in wide else arrived
            target = target.at[(slot,) + half(order, step, True)]
        return pltpu.make_async_remote_copy(
            src_ref=source,
            dst_ref=target,
            send_sem=send_sem.at[slot, step],
            recv_sem=recv_sem.at[slot, step],
            device_id=partner(order[step]),
            device_id_type=MESH,
        )

    def kept_entries(order, step):
        left = [bit for bit in rest if bit not in order[: step + 1]]
        for number in range(2 ** len(left)):
            chosen = {bit: (number >> place) % 2 for place, bit in enumerate(reversed(left))}
            here = tuple(chosen.get(bit, mine[bit]) for bit in rest)
            came = tuple(1 - mine[bit] if bit == order[step] else at for bit, at in zip(rest, here))
            yield here, came

    def keep(slot, at, value, step):
        total[(slot,) + at] = value
        if step not in wide:
            narrow[(slot,) + at] = value.astype(jnp.bfloat16)

    def visit(wave, lane, step, order):
        piece = wave * 2 + lane
        slot = slot_at(piece, step)
        span = (CORE_SLOTS if step == 0 else slots) // 2
        reuse = wave >= span
        if step == 0:

            @pl.when(reuse)
            def _():
                copy(piece, 0, order).wait_send()

            def put(at, value):
                send_core[(slot,) + at] = value

            plan["produce"](loaded, piece, 1 - mine[core], put)
        else:
            copy(piece, step - 1, order).wait_recv()
            if step == 1:
                core_slot = slot_at(piece, 0)

                @pl.when(reuse)
                def _():
                    for old in range(1, depth):
                        copy(piece, old, order).wait_send()

                def add(at, value):
                    keep(slot, at, value + from_core[(core_slot,) + at], 1)

                plan["produce"](loaded, piece, mine[core], add)
            else:
                source = arrived_wide if step - 1 in wide else arrived
                for here, came in kept_entries(order, step - 1):
                    value = total[(slot,) + here] + source[(slot,) + came].astype(jnp.float32)
                    if step == depth:
                        start = plan["column"](piece)
                        out_ref[:, pl.ds(pl.multiple_of(start, width), width)] = value
                    else:
                        keep(slot, here, value, step)

            @pl.when(wave + (CORE_SLOTS if step == 1 else slots) // 2 < n_waves)
            def _():
                pl.semaphore_signal(
                    free_sem.at[slot_at(piece, step - 1), step - 1],
                    inc=1,
                    device_id=partner(order[step - 1]),
                    device_id_type=MESH,
                )

        if step < depth:

            @pl.when(reuse)
            def _():
                pl.semaphore_wait(free_sem.at[slot, step], 1)

            copy(piece, step, order).start()

    loads = []
    for number, (_, parts) in enumerate(plan["loads"]):
        for operand, place in parts:
            at = loaded[number].at[place] if place else loaded[number]
            loads.append(pltpu.make_async_copy(ins[operand], at, load_sem.at[operand]))
            loads[-1].start()

    def group(first, carry):
        for phase in range(3):
            for step in range(depth + 1):
                wave = first * 3 + phase - step

                @pl.when((wave >= 0) & (wave < n_waves))
                def _():
                    if step == 0:
                        for late, count in plan["waits"]:

                            @pl.when(wave == late)
                            def _():
                                for load in loads[slice(*count)]:
                                    load.wait()

                    for lane, order in enumerate(wave_orders(phase - step)):
                        visit(wave, lane, step, order)

        return carry

    greet(bits)
    lax.fori_loop(0, -(-(n_waves + depth) // 3), group, 0)
    for step in range(depth):
        for wave in range(max(0, n_waves - (CORE_SLOTS if step == 0 else slots) // 2), n_waves):
            for lane, order in enumerate(wave_orders(wave)):
                copy(wave * 2 + lane, step, order).wait_send()


def tree_scatter(operands, plan, collective_id, micros):
    bits = device_bits()
    slots, width, rows = (plan["slots"], plan["step"], plan["rows"])
    plan = dict(plan, operands=len(operands))
    entries = (2,) * (len(bits) - 1) + (rows, width)
    core_buffer = pltpu.VMEM((CORE_SLOTS,) + entries, jnp.float32)
    low_buffer = pltpu.VMEM((slots,) + entries, jnp.bfloat16)
    sums = pltpu.VMEM((slots,) + entries, jnp.float32)
    wide_buffer = sums if plan["wide"] else pltpu.VMEM((8, 128), jnp.float32)
    return pl.pallas_call(
        functools.partial(scatter_kernel, bits, plan),
        out_shape=jax.ShapeDtypeStruct((rows, 2 * plan["waves"] * width), jnp.float32),
        in_specs=[pl.BlockSpec(memory_space=pl.ANY)] * len(operands),
        out_specs=pl.BlockSpec(memory_space=pltpu.VMEM),
        scratch_shapes=[pltpu.VMEM(shape, jnp.bfloat16) for shape, _ in plan["loads"]]
        + [core_buffer, core_buffer, sums, low_buffer, low_buffer, wide_buffer]
        + [
            pltpu.SemaphoreType.DMA((len(operands),)),
            pltpu.SemaphoreType.DMA((slots, len(bits))),
            pltpu.SemaphoreType.DMA((slots, len(bits))),
            pltpu.SemaphoreType.REGULAR((slots, len(bits))),
        ],
        compiler_params=pltpu.CompilerParams(
            collective_id=collective_id, has_side_effects=True, vmem_limit_bytes=60 * 2**20
        ),
        cost_estimate=busy_for(micros),
    )(*operands)


def unit_of(block, blocks):
    edges, most = ([], sum(blocks))
    for count in blocks[:-1]:
        edges.append(count + (edges[-1] if edges else 0))
    return sum(lax.div(block + (most - edge), most) for edge in edges)


def put_rows(value, across, rows, put):
    rest_count = (value.shape[0] // rows).bit_length() - 1
    for number in range(2**rest_count):
        at = tuple((number >> place) % 2 for place in reversed(range(rest_count)))
        put((across,) + at, value[number * rows : (number + 1) * rows])


def layer_products(dec_blocks, enc_blocks, step, rows, loaded, piece, core, put):
    dec_left, dec_right, enc_left, enc_right = loaded
    dec_pieces = dec_right.shape[1] // step
    quarter = D // 4

    def product(left, right, blocks, number):
        unit = unit_of(lax.div(number * step, D), blocks)
        sides = right[:, pl.ds(pl.multiple_of(number * step, step), step)]
        for across in range(2):
            some = pl.ds(pl.multiple_of((2 * across + core) * quarter, quarter), quarter)
            value = lax.dot_general(
                left[unit, :, some],
                sides,
                (((0,), (0,)), ((), ())),
                preferred_element_type=jnp.float32,
            )
            put_rows(value, across, rows, put)

    @pl.when(piece < dec_pieces)
    def _():
        product(dec_left, dec_right, dec_blocks, piece)

    @pl.when(piece >= dec_pieces)
    def _():
        product(enc_left, enc_right, enc_blocks, piece - dec_pieces)


def layer_column(step, piece):
    per_block = D // step
    half = 14 * per_block
    is_enc = lax.div(piece, half)
    block = lax.div(piece - is_enc * half, per_block)

    def past(edge):
        return lax.div(block + 14 - edge, 14)

    dec_shift = 4 + 2 * past(5) + 8 * past(6)
    enc_shift = 5 * past(4) + past(6)
    shift = dec_shift + is_enc * (enc_shift - dec_shift)
    return (block + shift) * D + lax.rem(piece, per_block) * step


def scatter_layers(dec_pairs, enc_pairs, rows, collective_id):
    operands, loads, counts = ([], [], [])
    for pairs in (dec_pairs, enc_pairs):
        tokens, parts, at = (pairs[0][0].shape[0], [], 0)
        for unit, (left_side, _) in enumerate(pairs):
            parts.append((len(operands), (unit,)))
            operands.append(left_side)
        loads.append(((len(pairs), tokens, D), parts))
        parts = []
        for _, right_side in pairs:
            parts.append((len(operands), (slice(None), pl.ds(at, right_side.shape[1]))))
            operands.append(right_side)
            at += right_side.shape[1]
        loads.append(((tokens, at), parts))
        counts.append([right_side.shape[1] // D for _, right_side in pairs])
    dec_loads = 2 * len(dec_pairs)
    dec_waves = loads[1][0][1] // (2 * WAVE_STEP)
    plan = {
        "waves": dec_waves + loads[3][0][1] // (2 * WAVE_STEP),
        "slots": 12,
        "step": WAVE_STEP,
        "rows": rows,
        "wide": (),
        "loads": loads,
        "waits": ((0, (0, dec_loads)), (dec_waves, (dec_loads, None))),
        "produce": functools.partial(layer_products, counts[0], counts[1], WAVE_STEP, rows),
        "column": functools.partial(layer_column, WAVE_STEP),
    }
    return tree_scatter(operands, plan, collective_id, 230)


def final_products(step, rows, loaded, piece, core, put):
    left, right = loaded
    sides = right[:, pl.ds(pl.multiple_of(piece * step, step), step)]
    for across in range(2):
        value = jnp.dot(left[across, core], sides, preferred_element_type=jnp.float32)
        put_rows(value, across, rows, put)


def scatter_final(grad_logits, table, collective_id):
    bits = device_bits()
    n_dev, step, width = (2 ** len(bits), 128, table.shape[1])
    rows_all = grad_logits.shape[0] // n_dev
    turns = max(1, n_dev // 32)
    rows = rows_all // turns
    sums = []
    for turn in range(turns):
        some = grad_logits.reshape(n_dev, rows_all, -1)[:, turn * rows : (turn + 1) * rows]
        some = some.reshape(2, 2, n_dev // 4 * rows, -1)
        plan = {
            "waves": width // (2 * step),
            "slots": width // step,
            "step": step,
            "rows": rows,
            "wide": (len(bits) - 2, len(bits) - 1),
            "loads": [(some.shape, [(0, ())]), (table.shape, [(1, ())])],
            "waits": ((0, (0, 2)),),
            "produce": functools.partial(final_products, step, rows),
            "column": lambda piece: piece * step,
        }
        sums.append(tree_scatter([some, table], plan, collective_id + turn, 60))
    return jnp.concatenate(sums, axis=0)


def lookup_plan(ids, live, rows_here):
    count = ids.shape[0]
    owner = ids // rows_here
    same = (ids[:, None] == ids[None, :]) & live[None, :]
    earlier = jnp.arange(count)[None, :] < jnp.arange(count)[:, None]
    first = live & ~jnp.any(same & earlier, axis=1)
    below = first[None, :] & (owner[:, None] == owner[None, :]) & (ids[None, :] < ids[:, None])
    rank = jnp.sum(below.astype(jnp.int32), axis=1)
    rounds = jnp.max(jnp.where(live, rank, 0)) // SLOTS + 1
    return (owner, ids - owner * rows_here, first, live, rank, rounds)


def round_flat(plan, turn):
    owner, _, _, live, rank, _ = plan
    slot = rank - turn * SLOTS
    return jnp.where(live & (slot >= 0) & (slot < SLOTS), owner * SLOTS + slot, -1)


def round_requests(plan, turn, n_dev):
    flat = round_flat(plan, turn)
    hit = (flat[:, None] == jnp.arange(n_dev * SLOTS)[None, :]) & plan[2][:, None]
    return jnp.sum(jnp.where(hit, plan[1][:, None] + 1, 0), axis=0) - 1


def picking(plan, turn, n_dev):
    return (
        round_flat(plan, turn)[:, None] == jnp.arange(n_dev * SLOTS)[None, :]
    ).astype(jnp.bfloat16)


def asked_hot(asked, rows_here):
    return (asked.reshape(-1)[:, None] == jnp.arange(rows_here)[None, :]).astype(jnp.bfloat16)


def mine_of(table):
    return lax.dynamic_slice_in_dim(table, lax.axis_index(AXES) * SLOTS, SLOTS, axis=1)


def swap(rows, n_dev):
    wide = rows.shape[-1]
    return lax.all_to_all(
        rows.reshape(n_dev, SLOTS, wide), AXES, 0, 0, tiled=True
    ).reshape(n_dev * SLOTS, wide)


def answer(asked, tables):
    hot = asked_hot(asked, tables[0].shape[0])
    return jnp.concatenate([to_low(matmul(hot, table)) for table in tables], axis=1)


def pick_rows(pick, rows):
    return (to_low(matmul(pick, rows[:, :D])), to_low(matmul(pick, rows[:, D:])))


def added(some, others):
    return jax.tree.map(jnp.add, some, others)


def fetch_rows(plan, answers, rounds, tables, n_dev):
    rows = pick_rows(picking(plan, 0, n_dev), swap(answers, n_dev))

    def more(state):
        turn, rows = state
        asked = mine_of(lax.all_gather(round_requests(plan, turn, n_dev), AXES, axis=0))
        pick = picking(plan, turn, n_dev)
        return (turn + 1, added(rows, pick_rows(pick, swap(answer(asked, tables), n_dev))))

    return lax.while_loop(lambda state: state[0] < rounds, more, (jnp.int32(1), rows))[1]


def collect(asked, sums, rows_here, n_dev):
    return jnp.einsum(
        "kc,kd->cd",
        asked_hot(asked, rows_here),
        swap(sums, n_dev),
        preferred_element_type=jnp.float32,
    )


def row_sums(pick, gradient):
    return to_low(jnp.einsum("nk,nd->kd", pick, gradient, preferred_element_type=jnp.float32))


def return_rows(plan, asked, rounds, first_sums, gradient, rows_here, n_dev):
    sums = collect(asked, first_sums, rows_here, n_dev)

    def more(state):
        turn, sums = state
        asked = mine_of(lax.all_gather(round_requests(plan, turn, n_dev), AXES, axis=0))
        pick = picking(plan, turn, n_dev)
        return (turn + 1, sums + collect(asked, row_sums(pick, gradient), rows_here, n_dev))

    return lax.while_loop(lambda state: state[0] < rounds, more, (jnp.int32(1), sums))[1]


ENC_BLOCKS = ((0, 3 * D), (3 * D, D), (9 * D, 2 * D), (12 * D, FF), (12 * D + FF, FF))
DEC_BLOCKS = (
    (4 * D, 3 * D),
    (7 * D, D),
    (8 * D, D),
    (11 * D, D),
    (12 * D + 2 * FF, FF),
    (12 * D + 3 * FF, FF),
)


def gather_offloaded(shard, blocks):
    part = jnp.concatenate([shard[:, low : low + width] for low, width in blocks], axis=1)
    return lax.all_gather(part, AXES, axis=0, tiled=True)


def split_blocks(part, blocks):
    gathered, at = ([], 0)
    for _, width in blocks:
        gathered.append(part[:, at : at + width])
        at += width
    return by_column(blocks, gathered)


def after(values, *others):
    return lax.optimization_barrier((values,) + others)[0]


def columns(layer_full, first_column, column_count):
    assert layer_full[first_column].shape[1] == column_count
    return layer_full[first_column]


def by_column(blocks, gathered):
    return {low: value for (low, _), value in zip(blocks, gathered)}


def shard_stats(final_rows, table_shard, targets, collective_ids):
    all_rows = gather_whole(final_rows, 128, collective_ids[0], 50, final_rows.shape[0] // 2)
    all_rows = all_rows.reshape(-1, D)
    logits = jnp.einsum("rd,vd->rv", all_rows, table_shard, preferred_element_type=jnp.float32)
    logits = with_layout_constraint(logits, Layout(major_to_minor=(0, 1)))
    low = lax.axis_index(AXES) * table_shard.shape[0]
    hot = (targets - low)[:, None] == jnp.arange(table_shard.shape[0])[None, :]
    largest = jnp.max(logits, axis=1)
    total = jnp.sum(jnp.exp(logits - largest[:, None]), axis=1)
    picked = jnp.sum(jnp.where(hot, logits, 0.0), axis=1)
    stats = jnp.stack([largest, total, picked]).reshape(8, -1)
    stats = gather_whole(stats, stats.shape[1] // 4, collective_ids[1], 20)
    stats = stats.reshape(-1, 3, largest.shape[0])
    peak = jnp.max(stats[:, 0], axis=0)
    log_own = peak + jnp.log(jnp.sum(stats[:, 1] * jnp.exp(stats[:, 0] - peak), axis=0))
    return (jnp.sum(stats[:, 2], axis=0) - log_own, log_own, logits, hot, all_rows)


def forward(token_rows, enc_full, dec_full_after, gain_rows, batch_data):
    (
        prompt_ids,
        decoder_input,
        targets,
        enc_allowed,
        self_allowed,
        cross_allowed,
        pair_local,
        valid,
    ) = batch_data
    pairs_here, seat_count = (prompt_ids.shape[0], decoder_input.shape[0])
    prompt_count = prompt_ids.size
    encoder_input = token_rows[:prompt_count].astype(jnp.float32)
    encoder_one, encoder_attn = self_forward(
        encoder_input,
        gain_rows[0],
        columns(enc_full, 0, 3 * D),
        columns(enc_full, 3 * D, D),
        enc_allowed,
        (pairs_here, P_MAX),
    )
    encoder_two, encoder_ffn = feed_forward(
        encoder_one,
        gain_rows[1],
        columns(enc_full, 12 * D, FF),
        columns(enc_full, 12 * D + FF, FF),
    )
    encoder_final = to_low(rms_norm(encoder_two, gain_rows[2]))
    cross_memory = to_low(matmul(encoder_final, columns(enc_full, 9 * D, 2 * D))).reshape(
        pairs_here, P_MAX, 2 * D
    )
    layer_full = dec_full_after(cross_memory)
    decoder_zero = token_rows[prompt_count:].astype(jnp.float32)
    decoder_one, decoder_attn = self_forward(
        decoder_zero,
        gain_rows[3],
        columns(layer_full, 4 * D, 3 * D),
        columns(layer_full, 7 * D, D),
        self_allowed,
        (seat_count, R_MAX),
    )
    decoder_two, decoder_cross = cross_forward(
        decoder_one,
        gain_rows[4],
        columns(layer_full, 8 * D, D),
        columns(layer_full, 11 * D, D),
        cross_memory,
        pair_local,
        cross_allowed,
        (seat_count, R_MAX),
    )
    decoder_three, decoder_ffn = feed_forward(
        decoder_two,
        gain_rows[5],
        columns(layer_full, 12 * D + 2 * FF, FF),
        columns(layer_full, 12 * D + 3 * FF, FF),
    )
    final_rows = to_low(final_norm(decoder_three, gain_rows[6]))
    stored = (
        encoder_input,
        encoder_one,
        encoder_two,
        encoder_attn,
        encoder_ffn,
        encoder_final,
        decoder_zero,
        decoder_one,
        decoder_two,
        decoder_three,
        decoder_attn,
        decoder_cross,
        decoder_ffn,
    )
    return (final_rows, stored)


def decoder_backward(layer_full, gain_rows, batch_data, stored, grad_final):
    enc_allowed, self_allowed, cross_allowed = batch_data[3:6]
    decoder_zero, decoder_one, decoder_two, decoder_three = stored[6:10]
    decoder_attn, decoder_cross, decoder_ffn = stored[10:]
    grad_three, gain_six = norm_backward(final_norm, decoder_three, gain_rows[6], grad_final)
    grad_two, gain_five, dec_ffn_pairs = feed_backward(
        decoder_two,
        gain_rows[5],
        columns(layer_full, 12 * D + 2 * FF, FF),
        columns(layer_full, 12 * D + 3 * FF, FF),
        decoder_ffn,
        grad_three,
    )
    grad_one, gain_four, grad_memory, cross_pairs = cross_backward(
        decoder_one,
        gain_rows[4],
        columns(layer_full, 8 * D, D),
        columns(layer_full, 11 * D, D),
        cross_allowed,
        decoder_cross,
        grad_two,
    )
    grad_zero, gain_three, dec_self_pairs = self_backward(
        decoder_zero,
        gain_rows[3],
        columns(layer_full, 4 * D, 3 * D),
        columns(layer_full, 7 * D, D),
        self_allowed,
        decoder_attn,
        grad_one,
    )
    return (
        (gain_three, gain_four, gain_five, gain_six),
        dec_self_pairs + cross_pairs + dec_ffn_pairs,
        grad_memory,
        grad_zero,
    )


def encoder_backward(layer_full, gain_rows, batch_data, stored, memory_low):
    enc_allowed = batch_data[3]
    encoder_input, encoder_one, encoder_two, encoder_attn, encoder_ffn, encoder_final = stored[:6]
    grad_encoder_final = matmul_back(memory_low, columns(layer_full, 9 * D, 2 * D))
    grad_encoder_two, gain_two = norm_backward(
        rms_norm, encoder_two, gain_rows[2], grad_encoder_final
    )
    grad_encoder_one, gain_one, enc_ffn_pairs = feed_backward(
        encoder_one,
        gain_rows[1],
        columns(layer_full, 12 * D, FF),
        columns(layer_full, 12 * D + FF, FF),
        encoder_ffn,
        grad_encoder_two,
    )
    grad_encoder_input, gain_zero, enc_self_pairs = self_backward(
        encoder_input,
        gain_rows[0],
        columns(layer_full, 0, 3 * D),
        columns(layer_full, 3 * D, D),
        enc_allowed,
        encoder_attn,
        grad_encoder_one,
    )
    pairs = enc_self_pairs + ((encoder_final, memory_low),) + enc_ffn_pairs
    return ((gain_zero, gain_one, gain_two), pairs, grad_encoder_input)


def apply_update(weight, moment, average, gradient, factor):
    clipped = gradient * factor
    moment_new = MOMENTUM * moment + clipped
    step_size = -LEARN_RATE * (clipped + MOMENTUM * moment_new)
    weight_new = weight + step_size
    return (
        weight_new,
        moment_new,
        AVERAGE_DECAY * average + (1.0 - AVERAGE_DECAY) * weight_new,
        step_size,
    )


def body(
    prompt_ids,
    prompt_lengths,
    response_ids,
    response_lengths,
    sequence_pair,
    chosen_flag,
    pair_microbatch,
    policy_embed,
    policy_layers,
    policy_gains,
    momentum_embed,
    momentum_layers,
    momentum_gains,
    average_embed,
    average_layers,
    average_gains,
    frozen_embed,
    frozen_layers,
    frozen_gains,
):
    n_dev = lax.axis_size(AXES)
    me = lax.axis_index(AXES)
    rows_here = policy_embed.shape[0]
    pairs_here = prompt_ids.shape[0]
    seat_count = response_ids.shape[0]
    decoder_input = jnp.concatenate(
        [jnp.zeros((seat_count, 1), jnp.int32), response_ids[:, :-1]], axis=1
    )
    pair_local = sequence_pair - me * pairs_here
    select_float = (pair_local[:, None] == jnp.arange(pairs_here)[None, :]).astype(jnp.float32)
    prompt_pos = jnp.arange(P_MAX)
    reply_pos = jnp.arange(R_MAX)
    prompt_keys = prompt_pos[None, :] < prompt_lengths[:, None]
    valid = reply_pos[None, :] < response_lengths[:, None]
    enc_allowed = jnp.broadcast_to(prompt_keys[:, None, :], (pairs_here, P_MAX, P_MAX))
    self_allowed = (reply_pos[:, None] >= reply_pos[None, :])[None] & valid[:, None, :]
    seat_keys = jnp.einsum("sp,pk->sk", select_float, prompt_keys.astype(jnp.float32)) > 0.5
    cross_allowed = jnp.broadcast_to(seat_keys[:, None, :], (seat_count, R_MAX, P_MAX))
    batch_data = (
        prompt_ids,
        decoder_input,
        response_ids,
        enc_allowed,
        self_allowed,
        cross_allowed,
        pair_local,
        valid,
    )
    token_ids = jnp.concatenate([prompt_ids.reshape(-1), decoder_input.reshape(-1)])
    token_live = jnp.concatenate([prompt_keys.reshape(-1), valid.reshape(-1)])
    plan = lookup_plan(token_ids, token_live, rows_here)
    packed = jnp.concatenate(
        [
            round_requests(plan, 0, n_dev),
            response_ids.reshape(-1),
            response_lengths,
            pair_local,
            chosen_flag,
            pair_microbatch,
            plan[5][None],
        ]
    )
    packed = jnp.pad(packed, (0, -packed.shape[0] % 1024)).reshape(8, -1)
    *policy_enc, notes = tree_gather(
        to_low(policy_layers), ENC_BLOCKS, WAVE_STEP, 1, 130, extra=packed
    )
    notes = notes.reshape(n_dev, -1)
    asked = mine_of(notes)
    at = n_dev * SLOTS
    cuts = []
    for width in (seat_count * R_MAX, seat_count, seat_count, seat_count, pairs_here, 1):
        cuts.append(notes[:, at : at + width])
        at += width
    targets, all_lengths, all_pair, all_flag, all_micro, all_rounds = cuts
    targets = targets.reshape(-1)
    rounds = jnp.max(all_rounds)
    all_select = (all_pair[:, :, None] == jnp.arange(pairs_here)).astype(jnp.float32)
    pair_micro = (all_micro[:, :, None] == jnp.arange(MICRO)).astype(jnp.float32)
    seat_micro = jnp.sum(all_select[:, :, :, None] * pair_micro[:, None], axis=2)
    chosen_float = all_flag.astype(jnp.float32)
    pair_total = jnp.sum(pair_micro, axis=(0, 1))
    token_total = jnp.sum(
        seat_micro * (chosen_float * all_lengths.astype(jnp.float32))[:, :, None], axis=(0, 1)
    )
    micro_counts = jnp.stack([pair_total, token_total])
    pair_divisor = jnp.sum(pair_micro * pair_total, axis=2)
    sequence_divisor = jnp.sum(seat_micro * token_total, axis=2)
    all_valid = reply_pos < all_lengths[:, :, None]

    policy_table = to_low(policy_embed)
    policy_low = to_low(after(policy_layers, policy_enc[0]))
    policy_dec = gather_offloaded(policy_low, DEC_BLOCKS)
    answers = answer(asked, (policy_table, frozen_embed))
    policy_tokens, frozen_tokens = fetch_rows(plan, answers, rounds, (policy_table, frozen_embed), n_dev)
    policy_layer_enc = by_column(ENC_BLOCKS, policy_enc)
    policy_layer_dec = split_blocks(policy_dec, DEC_BLOCKS)
    policy_layer_full = policy_layer_enc | policy_layer_dec
    def policy_after(memory):
        return policy_layer_dec

    def logp_of(token_logp):
        return jnp.sum(jnp.where(all_valid, token_logp.reshape(all_valid.shape), 0.0), axis=2)

    policy_rows, stored = forward(
        policy_tokens, policy_layer_enc, policy_after, policy_gains, batch_data
    )
    frozen_enc = gather_offloaded(after(frozen_layers, stored[5]), ENC_BLOCKS)
    frozen_dec = gather_offloaded(after(frozen_layers, policy_rows), DEC_BLOCKS)
    frozen_layer_enc = split_blocks(frozen_enc, ENC_BLOCKS)

    def frozen_after(memory):
        return split_blocks(after(frozen_dec, memory), DEC_BLOCKS)

    token_logp, log_own, logits, hot, all_rows = shard_stats(
        policy_rows, policy_table, targets, (3, 4)
    )
    policy_logp = logp_of(token_logp)
    row_slope = jnp.where(
        all_valid.reshape(-1)[:, None], hot.astype(jnp.float32) - jnp.exp(logits - log_own[:, None]), 0.0
    )
    row_slope = with_layout_constraint(to_low(row_slope), Layout(major_to_minor=(0, 1)))
    grad_final = scatter_final(row_slope, policy_table, 10)
    dec_gains, dec_pairs, grad_memory, grad_zero = decoder_backward(
        policy_layer_full, policy_gains, batch_data, stored, grad_final
    )
    frozen_inputs = after(frozen_tokens, grad_zero)
    frozen_rows, unused = forward(
        frozen_inputs, frozen_layer_enc, frozen_after, frozen_gains, batch_data
    )
    frozen_logp = logp_of(shard_stats(frozen_rows, frozen_embed, targets, (5, 6))[0])
    frozen_mean = lax.dynamic_index_in_dim(
        frozen_logp / all_lengths.astype(jnp.float32), me, 0, keepdims=False
    )

    sign_value = 2.0 * chosen_float - 1.0
    margin = PREFERENCE_BETA * jnp.sum(
        all_select * (sign_value * (policy_logp - frozen_logp))[:, :, None], axis=1
    )
    loss = (
        jnp.sum(jax.nn.softplus(-margin) / pair_divisor)
        - CHOSEN_WEIGHT * jnp.sum(chosen_float * policy_logp / sequence_divisor)
    ) / MICRO
    pair_slope = -PREFERENCE_BETA * jax.nn.sigmoid(-margin) / pair_divisor
    sequence_slope = (
        sign_value * jnp.sum(all_select * pair_slope[:, None, :], axis=2)
        - CHOSEN_WEIGHT * chosen_float / sequence_divisor
    ) / MICRO
    table_grad = jnp.einsum(
        "rc,rd->cd",
        row_slope,
        to_low(jnp.repeat(sequence_slope.reshape(-1), R_MAX)[:, None] * all_rows),
        preferred_element_type=jnp.float32,
    )
    slope_here = lax.dynamic_index_in_dim(sequence_slope, me, 0, keepdims=False)
    slope_rows = jnp.repeat(slope_here, R_MAX)[:, None]
    memory_slope = (select_float * slope_here[:, None])[:, :, None, None, None]
    memory_low = jnp.concatenate(
        [
            join_heads(to_low(jnp.sum(memory_slope * part[:, None], axis=0))).reshape(-1, D)
            for part in grad_memory
        ],
        axis=1,
    )
    enc_gains, enc_pairs, grad_encoder_input = encoder_backward(
        policy_layer_full, policy_gains, batch_data, stored, memory_low
    )
    gain_grads = jnp.stack(
        [jnp.sum(rows, axis=0) for rows in enc_gains]
        + [jnp.sum(slope_rows * rows, axis=0) for rows in dec_gains]
    )
    token_gradient = jnp.concatenate([grad_encoder_input, slope_rows * grad_zero], axis=0)
    enc_pairs = [(to_low(left), to_low(right)) for left, right in enc_pairs]
    scaled_pairs = []
    for left, right in dec_pairs:
        if left.dtype == jnp.float32:
            scaled_pairs.append((to_low(slope_rows * left), right))
        else:
            scaled_pairs.append((left, to_low(slope_rows * right)))
    token_gradient = to_low(token_gradient)
    first_sums = row_sums(picking(plan, 0, n_dev), token_gradient)
    table_grad = after(table_grad, first_sums)
    enc_pairs[0] = (after(enc_pairs[0][0], first_sums, table_grad), enc_pairs[0][1])
    embed_grad = table_grad + return_rows(
        plan, asked, rounds, first_sums, token_gradient, rows_here, n_dev
    )
    layer_grad = scatter_layers(scaled_pairs, enc_pairs, policy_layers.shape[0], 8)
    squares_local = jnp.sum(embed_grad * embed_grad) + jnp.sum(layer_grad * layer_grad)
    shared = jnp.concatenate([gain_grads, jnp.full((1, D), squares_local)], axis=0)
    shared = jnp.sum(gather_whole(shared, D, 9, 20), axis=0)
    gain_total, squares_total = (shared[:7], shared[7, 0])
    grad_norm = jnp.sqrt(squares_total + jnp.sum(gain_total * gain_total))
    factor = jnp.minimum(1.0, CLIP_NORM / grad_norm)
    embed_new = apply_update(policy_embed, momentum_embed, average_embed, embed_grad, factor)
    layers_new = apply_update(policy_layers, momentum_layers, average_layers, layer_grad, factor)
    gains_new = apply_update(policy_gains, momentum_gains, average_gains, gain_total, factor)
    return (
        loss,
        grad_norm,
        micro_counts,
        frozen_mean,
        embed_new[3],
        layers_new[0],
        gains_new[0],
        embed_new[1],
        layers_new[1],
        gains_new[1],
        embed_new[2],
        layers_new[2],
        gains_new[2],
    )


def solution(mesh):
    placed = (
        P(("dp", "fsdp"), None),
        P(("dp", "fsdp")),
        P(("dp", "fsdp"), None),
        P(("dp", "fsdp")),
        P(("dp", "fsdp")),
        P(("dp", "fsdp")),
        P(("dp", "fsdp")),
        P(("dp", "fsdp"), None),
        P(("dp", "fsdp"), None),
        P(),
        P(("dp", "fsdp"), None),
        P(("dp", "fsdp"), None),
        P(),
        P(("dp", "fsdp"), None),
        P(("dp", "fsdp"), None),
        P(),
        P(("dp", "fsdp"), None),
        P(("dp", "fsdp"), None),
        P(),
    )
    return jax.shard_map(
        body,
        mesh=mesh,
        in_specs=placed,
        out_specs=(
            P(),
            P(),
            P(),
            P(("dp", "fsdp")),
            P(("dp", "fsdp"), None),
            P(("dp", "fsdp"), None),
            P(),
            P(("dp", "fsdp"), None),
            P(("dp", "fsdp"), None),
            P(),
            P(("dp", "fsdp"), None),
            P(("dp", "fsdp"), None),
            P(),
        ),
        check_vma=False,
    )
```

time: 1660 us -> 1410 us (0.85)
  Pallas kernels: 958 us -> 694 us
  waiting for transfers between devices: 116 us -> 147 us
  matrix products: 282 us -> 261 us
  other arithmetic: 109 us -> 128 us
  local copies, waits for them, and re-layouts: 149 us -> 130 us
    pallas_call x10 -> x8, Pallas kernels: 958 us -> 694 us  [the longest x2 357 us: tree_scatter(): pl.pallas_call(functools.partial(scatter_kernel, bits, plan), out_shape=j...]
    all_to_all x2, waiting for transfers between devices: 27.1 us -> 124 us  [swap(): lax.all_to_all(rows.reshape(n_dev, SLOTS, wide), AXES, 0, 0, tiled=True)]
    all_gather x2 -> x3, waiting for transfers between devices: 88.7 us -> 23.3 us  [gather_offloaded(): return lax.all_gather(part, AXES, axis=0, tiled=True)]
    unnamed x380 -> x372, local copies, waits for them, and re-layouts: 44.6 us -> 24.3 us
    dot_general x11 -> x8, matrix products: 49.7 us -> 33.9 us  [the longest x1 15.1 us: body(): jnp.einsum('rc,rd->cd', row_slope, to_low(jnp.repeat(sequence_slope.resha...]
  transfers between devices with their start and end apart: 4 -> 5, of which waited for: 2 -> 2; matrix products, arithmetic and copies ran while one was open for 4% -> 21% of each run, Pallas kernels for 20% -> 34%
where the time goes in v2:
time: 1410 us; the launch traced here: 1400 us
  Pallas kernels  694 us (49%)
  matrix products  261 us (19%)
  waiting for transfers between devices  147 us (10%)
  local copies, waits for them, and re-layouts  130 us (9%)
  other arithmetic  128 us (9%)
  between operations  25.6 us (2%)
    pallas_call x2, Pallas kernels, tree_scatter(): pl.pallas_call(functools.partial(scatter_kernel, bits, plan), out_shape=j...  357 us
    pallas_call x6, Pallas kernels, tree_gather(): pl.pallas_call(functools.partial(gather_kernel, bits, len(operands), wave...  337 us
    all_to_all x2, waiting for transfers between devices, swap(): lax.all_to_all(rows.reshape(n_dev, SLOTS, wide), AXES, 0, 0, tiled=True)  124 us
    dot_general x22, matrix products, matmul(): return jnp.dot(left_side, right_side, preferred_element_type=jnp.float32)  95.2 us
    dot_general x9, matrix products, matmul_back(): jnp.einsum('re,de->rd', grad_low, weight, preferred_element_type=jnp.floa...  38.8 us
    dot_general x4, matrix products, feed_forward(): jnp.einsum('rf,df->rd', active, weight_out, preferred_element_type=jnp.fl...  35.3 us
    convert_element_type x17, other arithmetic, to_low(): return values.astype(jnp.bfloat16)  30.6 us
  transfers between devices with their start and end apart: 5, of which 2 were waited for; matrix products, arithmetic and copies ran while one was open for 21% of the time, Pallas kernels for 34%

profile of v2, /device:TPU:0, one launch (start us, length us, event | category | flops | bytes accessed | tf_op | source)
XLA Modules:
  0.0 1395.8 jit_solution(18413614966272785386)
XLA Ops:
  21.5 129.6 %shard_map.282 = (bf16[2,2,2,2,2,32,3072]{6,5,4,3,2,1,0:T(8,128)(2,1)}, bf16[2,2,2,2,2,32,1024]{6,5,4,3,2,1,0:T(8,128)(2,1)}, bf16[2,2,2,2,2,32,2048]{6,5,4,3,2,...) custom-call(bf16[1,1,1,1,1,32,28672]{6,5,4,3,2,1,0:T(8,128)(2,1)} %c, ...), custom_call_target="tpu_custom_call" | custom-call | bytes 442000000 | tf_op jit(solution)/shard_map/pallas_call | solution.py:332
  154.7 3.8 convert_element_type.367.refs_1_
  165.9 4.4 all-to-all-start.2
  171.7 124.0 %all-to-all-done.2 = bf16[32,24,2048]{2,1,0:T(8,128)(2,1)S(1)} async-done(((bf16[32,24,2048]{2,1,0:T(8,128)(2,1)}), bf16[32,24,2048]{2,1,0:T(8,128)(2,1)S(1)}, u32[]{:S(2)}, u32[]{:S(2)}) %all-to-all-start.2) | async-done | bytes 3145760 | tf_op jit(solution)/shard_map/all_to_all | solution.py:690
  303.7 6.0 convolution_convert_fusion.1
  324.5 20.1 %maximum_convert_fusion.1.refs_21_ = bf16[384,4096]{1,0:T(8,128)(2,1)S(1)} fusion(bf16[384,1024]{1,0:T(8,128)(2,1)S(1)} %multiply_convert_fusion.11.refs_15_, bf16[1024,4096]{1,0:T(8,128)(2,1)} %bitcast.340), kind=kOutput, calls=%fused_computation.76 | convolution fusion | flops 3224371200 | bytes 12320768 | tf_op jit(solution)/shard_map/dot_general | solution.py:47
  351.3 4.4 convolution_convert_fusion.2
  361.8 23.2 %all-gather.12.cloned.1.call-done = bf16[1024,14336]{1,0:T(8,128)(2,1)} async-done(((bf16[32,14336]{1,0:T(8,128)(2,1)}), bf16[1024,14336]{1,0:T(8,128)(2,1)}) %all-gather.12.cloned.1.call-update) | async-done | bytes 29360144 | tf_op jit(solution)/shard_map/all_gather | solution.py:758
  385.1 3.8 fusion.80
  409.5 4.8 fusion.67.refs_11_
  414.4 7.5 multiply_reduce_fusion.24
  431.9 80.0 %shard_map.283 = bf16[2,2,2,2,2,128,1024]{6,5,4,3,2,1,0:T(8,128)(2,1)} custom-call(bf16[1,1,1,1,1,128,1024]{6,5,4,3,2,1,0:T(8,128)(2,1)} %fusion.403.refs_0_), custom_call_target="tpu_custom_call" | custom-call | bytes 170000000 | tf_op jit(solution)/shard_map/pallas_call | solution.py:332
  511.9 12.6 fusion.331
  524.5 4.7 exponential_reduce_fusion.1
  530.9 31.4 %shard_map.284 = f32[2,2,2,2,2,8,1536]{6,5,4,3,2,1,0:T(8,128)} custom-call(f32[1,1,1,1,1,8,1536]{6,5,4,3,2,1,0:T(8,128)} %reshape_reshape.36.refs_0_), custom_call_target="tpu_custom_call" | custom-call | bytes 68000000 | tf_op jit(solution)/shard_map/pallas_call | solution.py:332
  562.3 3.8 reshape_reshape_reshape.13
  566.1 4.6 fusion.321
  572.1 11.2 select_convert_fusion
  583.3 110.2 %shard_map.285 = f32[128,1024]{1,0:T(8,128)} custom-call(bf16[2,2,1024,1004]{3,2,1,0:T(8,128)(2,1)} %bitcast.257, bf16[1004,1024]{1,0:T(8,128)(2,1)} %convert_element_type.367.refs_1_), custom_call_target="tpu_custom_call" | custom-call | bytes 204000000 | tf_op jit(solution)/shard_map/pallas_call | solution.py:510
  696.1 5.0 fusion.72
  701.1 7.1 multiply_reduce_fusion.22
  750.5 5.7 fusion.237
  759.9 4.2 convolution_multiply_fusion
  767.0 5.9 fusion.75
  785.9 4.0 multiply_reduce_fusion.11
  789.9 14.4 %multiply_reduce_fusion.10 = (f32[384]{0:T(512)S(1)}, f32[384,1024]{1,0:T(8,128)S(1)}) fusion(f32[384,1024]{1,0:T(8,128)} %get-tuple-element.477, bf16[1024,14336]{1,0:T(8,128)(2,1)} %all-gather.16.cloned.1.call-done, f32[1024]{0:T(1024)S(1)} %bitcast.334, f32[384]{0:T(512)S(1)} %add_rsqrt_fusion.1), kind=kOutput, calls=%fused_computation.190 | convolution fusion | flops 6447955456 | bytes 21502976 | tf_op jit(solution)/shard_map/rf,df->rd/dot_general | solution.py:196
  804.3 4.0 fusion.95
  813.4 3.9 fusion.83
  843.6 9.9 multiply_reduce_fusion.18
  854.4 54.1 %shard_map.286 = bf16[2,2,2,2,2,128,1024]{6,5,4,3,2,1,0:T(8,128)(2,1)} custom-call(bf16[1,1,1,1,1,128,1024]{6,5,4,3,2,1,0:T(8,128)(2,1)} %fusion.266.refs_0_), custom_call_target="tpu_custom_call" | custom-call | bytes 170000000 | tf_op jit(solution)/shard_map/pallas_call | solution.py:332
  908.4 11.9 fusion.338
  920.4 4.7 exponential_reduce_fusion
  925.8 19.9 %shard_map.287 = f32[2,2,2,2,2,8,1536]{6,5,4,3,2,1,0:T(8,128)} custom-call(f32[1,1,1,1,1,8,1536]{6,5,4,3,2,1,0:T(8,128)} %reshape_reshape.40.refs_0_), custom_call_target="tpu_custom_call" | custom-call | bytes 68000000 | tf_op jit(solution)/shard_map/pallas_call | solution.py:332
  952.7 6.2 multiply_reduce_fusion
  974.3 4.9 multiply_reduce_fusion.6
  981.4 7.4 select_convert_fusion.1.refs_20_
  988.8 3.7 multiply_reduce_fusion.7
  999.9 5.7 fusion.160
  1029.6 7.8 fusion.136
  1037.6 3.8 multiply_convert_fusion.16
  1049.8 15.1 %fusion.30 = f32[1004,1024]{1,0:T(8,128)} fusion(bf16[4096,1004]{1,0:T(8,128)(2,1)} %select_convert_fusion, bf16[4096,1024]{1,0:T(8,128)(2,1)} %bitcast.267, f32[4096]{0:T(1024)S(1)} %mul.1257), kind=kOutput, calls=%fused_computation.45 | convolution fusion | flops 8434745344 | bytes 20742144 | tf_op jit(solution)/shard_map/rc,rd->cd/dot_general | solution.py:1105
  1069.9 246.7 %shard_map.288 = f32[32,28672]{1,0:T(8,128)} custom-call(bf16[128,1024]{1,0:T(8,128)(2,1)} %copy-done.64, bf16[128,1024]{1,0:T(8,128)(2,1)} %copy-done.62, bf16[128,1024]{1,0:T(8,128)(2,1)} %copy-done.65, bf16[128,1024]{1,0:T(8,128)(2,1)} %copy-done.63, bf16[128,1024]{1,0:T(8,128)(2,1)} %copy-done.66, bf16[128,1024]{1,0:T(8,128)(2,1)} %get-tuple-element.437.refs_5_, ...), custom_call_target="tpu_custom_call" | custom-call | bytes 782000000 | tf_op jit(solution)/shard_map/pallas_call | solution.py:510
  1317.3 3.6 multiply_reduce_fusion.4
  1320.9 5.3 fusion.91
  1327.1 7.6 multiply_reduce_fusion.3
  1336.7 22.4 %shard_map.289 = f32[2,2,2,2,2,8,1024]{6,5,4,3,2,1,0:T(8,128)} custom-call(f32[1,1,1,1,1,8,1024]{6,5,4,3,2,1,0:T(8,128)} %bitcast.294), custom_call_target="tpu_custom_call" | custom-call | bytes 68000000 | tf_op jit(solution)/shard_map/pallas_call | solution.py:332
  1363.6 10.4 add_multiply_fusion.2
  1374.0 12.6 add_multiply_fusion
  (655 shorter events, 262.3 us)
Async XLA Ops:
  7.2 377.9 %all-gather.12.cloned.1.call-start = ((), (), s32[]{:S(2)}) async-start(), calls=%async_computation.4 | async-start | bytes 30277632 | tf_op jit(solution)/shard_map/all_gather | solution.py:758
  8.0 309.0 %copy-start.86 = (pred[2,192]{1,0:T(4,128)(4,1)}, pred[2,192]{1,0:T(4,128)(4,1)S(1)}, u32[]{:S(2)}) copy-start(pred[2,192]{1,0:T(4,128)(4,1)S(1)} %iota_compare_fusion.49) | copy-start | bytes 1156
  12.4 285.4 %copy-start.127 = (s32[512]{0:T(512)}, s32[512]{0:T(512)S(1)}, u32[]{:S(2)}) copy-start(s32[512]{0:T(512)S(1)} %get-tuple-element.429) | copy-start | bytes 6148
  154.5 15.8 %copy-start.71 = (s32[4,8,8,128]{3,1,2,0:T(8,128)}, s32[4,8,8,128]{3,1,2,0:T(8,128)S(1)}, u32[]{:S(2)}) copy-start(s32[4,8,8,128]{3,1,2,0:T(8,128)S(1)} %copy.418) | copy-start | bytes 393220
  165.9 129.9 %all-to-all-start.2 = ((bf16[32,24,2048]{2,1,0:T(8,128)(2,1)}), bf16[32,24,2048]{2,1,0:T(8,128)(2,1)S(1)}, u32[]{:S(2)}, u32[]{:S(2)}) async-start(bf16[32,24,2048]{2,1,0:T(8,128)(2,1)} %bitcast.7), calls=%async_computation.2 | async-start | bytes 6291456 | tf_op jit(solution)/shard_map/all_to_all | solution.py:690
  170.3 596.7 %all-gather.16.cloned.1.call-start = ((), (), s32[]{:S(2)}) async-start(), calls=%async_computation.6 | async-start | bytes 30277632 | tf_op jit(solution)/shard_map/all_gather | solution.py:758
  171.7 130.6 %copy-start.98 = (f32[1,1024]{1,0:T(1,128)}, f32[1,1024]{1,0:T(1,128)S(1)}, u32[]{:S(2)}) copy-start(f32[1,1024]{1,0:T(1,128)S(1)} %get-tuple-element.424) | copy-start | bytes 12292
  171.7 152.6 %copy-start.100 = (f32[1,1024]{1,0:T(1,128)}, f32[1,1024]{1,0:T(1,128)S(1)}, u32[]{:S(2)}) copy-start(f32[1,1024]{1,0:T(1,128)S(1)} %get-tuple-element.423) | copy-start | bytes 12292
  171.7 177.1 %copy-start.96 = (f32[1,1024]{1,0:T(1,128)}, f32[1,1024]{1,0:T(1,128)S(1)}, u32[]{:S(2)}) copy-start(f32[1,1024]{1,0:T(1,128)S(1)} %get-tuple-element.422) | copy-start | bytes 12292
  171.7 187.2 %copy-start.102 = (f32[1,1024]{1,0:T(1,128)}, f32[1,1024]{1,0:T(1,128)S(1)}, u32[]{:S(2)}) copy-start(f32[1,1024]{1,0:T(1,128)S(1)} %get-tuple-element.425) | copy-start | bytes 12292
  171.7 224.6 %copy-start.93 = (f32[1,1024]{1,0:T(1,128)}, f32[1,1024]{1,0:T(1,128)S(1)}, u32[]{:S(2)}) copy-start(f32[1,1024]{1,0:T(1,128)S(1)} %get-tuple-element.421) | copy-start | bytes 12292
  171.7 236.9 %copy-start.104 = (f32[1,1024]{1,0:T(1,128)}, f32[1,1024]{1,0:T(1,128)S(1)}, u32[]{:S(2)}) copy-start(f32[1,1024]{1,0:T(1,128)S(1)} %get-tuple-element.420) | copy-start | bytes 12292
  300.7 9.0 copy-start.73
  300.7 9.0 copy-start.77
  300.7 9.0 copy-start.81
  300.7 9.0 copy-start.89
  300.7 9.0 copy-start.91
  321.2 23.4 %slice-start.10 = ((s8[8388608]{0:T(1024)(128)(4,1)}), s8[4194304]{0:T(1024)(128)(4,1)S(1)}, s32[]{:S(2)}) async-start(s8[8388608]{0:T(1024)(128)(4,1)} %bitcast.345), calls=%async_computation.17 | async-start | bytes 8388608
  324.2 20.3 %copy-start.119 = (f32[384]{0:T(512)}, f32[384]{0:T(512)S(1)}, u32[]{:S(2)}) copy-start(f32[384]{0:T(512)S(1)} %get-tuple-element.448) | copy-start | bytes 4612
  324.2 20.4 %copy-start.8 = (f32[384,1024]{1,0:T(8,128)}, f32[384,1024]{1,0:T(8,128)S(1)}, u32[]{:S(2)}) copy-start(f32[384,1024]{1,0:T(8,128)S(1)} %get-tuple-element.449) | copy-start | bytes 4718596
  324.3 20.3 %copy-start.122 = (f32[384]{0:T(512)}, f32[384]{0:T(512)S(1)}, u32[]{:S(2)}) copy-start(f32[384]{0:T(512)S(1)} %fusion.294) | copy-start | bytes 4612
  324.5 20.1 %copy-start.44 = (bf16[384,1024]{1,0:T(8,128)(2,1)}, bf16[384,1024]{1,0:T(8,128)(2,1)S(1)}, u32[]{:S(2)}) copy-start(bf16[384,1024]{1,0:T(8,128)(2,1)S(1)} %multiply_convert_fusion.11.refs_15_) | copy-start | bytes 2359300
  324.5 20.1 %slice-start.11 = ((s8[8388608]{0:T(1024)(128)(4,1)}), s8[4194304]{0:T(1024)(128)(4,1)S(1)}, s32[]{:S(2)}) async-start(s8[8388608]{0:T(1024)(128)(4,1)} %bitcast.345), calls=%async_computation.18 | async-start | bytes 8388608
  350.9 462.5 %all-gather.14.cloned.1.call-start = ((), (), s32[]{:S(2)}) async-start(), calls=%async_computation.5 | async-start | bytes 30277632 | tf_op jit(solution)/shard_map/all_gather | solution.py:758
  351.2 48.6 %copy-start.158 = (pred[4,192]{1,0:T(4,128)(4,1)}, pred[4,192]{1,0:T(4,128)(4,1)S(1)}, u32[]{:S(2)}) copy-start(pred[4,192]{1,0:T(4,128)(4,1)S(1)} %convolution_compare_fusion) | copy-start | bytes 2308
  351.3 39.5 %copy-start.125 = (pred[4,32,32]{1,2,0:T(8,128)(4,1)}, pred[4,32,32]{1,2,0:T(8,128)(4,1)S(1)}, u32[]{:S(2)}) copy-start(pred[4,32,32]{1,2,0:T(8,128)(4,1)S(1)} %broadcast_and_fusion) | copy-start | bytes 12292
  359.0 26.0 %copy-start.64 = (bf16[128,1024]{1,0:T(8,128)(2,1)}, bf16[128,1024]{1,0:T(8,128)(2,1)S(1)}, u32[]{:S(2)}) copy-start(bf16[128,1024]{1,0:T(8,128)(2,1)S(1)} %fusion.227.refs_0_) | copy-start | bytes 786436
  406.2 8.1 copy-start.63
  421.9 8.1 copy-start.140
  423.6 88.3 %copy-start.79 = (s32[32,4]{1,0:T(8,128)}, s32[32,4]{1,0:T(8,128)S(1)}, u32[]{:S(2)}) copy-start(s32[32,4]{1,0:T(8,128)S(1)} %get-tuple-element.411) | copy-start | bytes 1540
  425.7 86.1 %copy-start.160 = (f32[2]{0:T(128)}, f32[2]{0:T(128)S(1)}, u32[]{:S(2)}) copy-start(f32[2]{0:T(128)S(1)} %fusion.311) | copy-start | bytes 28
  583.3 110.2 %copy-start.20 = (f32[128,1024]{1,0:T(8,128)S(1)}, f32[128,1024]{1,0:T(8,128)}, u32[]{:S(2)}) copy-start(f32[128,1024]{1,0:T(8,128)} %get-tuple-element.459) | copy-start | bytes 1572868
  583.3 111.5 %copy-start.175 = (f32[128]{0:T(128)S(1)}, f32[128]{0:T(128)}, u32[]{:S(2)}) copy-start(f32[128]{0:T(128)} %copy-done.174) | copy-start | bytes 1540
  583.3 111.5 %copy-start.141 = (f32[128]{0:T(128)S(1)}, f32[128]{0:T(128)}, u32[]{:S(2)}) copy-start(f32[128]{0:T(128)} %copy-done.140) | copy-start | bytes 1540
  696.0 12.2 copy-start.31
  789.9 14.4 %copy-start.152 = (f32[1,1024]{1,0:T(1,128)S(1)}, f32[1,1024]{1,0:T(1,128)}, u32[]{:S(2)}) copy-start(f32[1,1024]{1,0:T(1,128)} %get-tuple-element.414) | copy-start | bytes 12292
  843.6 10.0 copy-start.124
  854.4 54.1 %copy-start.167 = (bf16[1004,1024]{1,0:T(8,128)(2,1)S(1)}, bf16[1004,1024]{1,0:T(8,128)(2,1)}, u32[]{:S(2)}) copy-start(bf16[1004,1024]{1,0:T(8,128)(2,1)} %get-tuple-element.747) | copy-start | bytes 6168580
  974.3 14.5 %slice-start.8 = ((s8[8388608]{0:T(1024)(128)(4,1)}), s8[4194304]{0:T(1024)(128)(4,1)S(1)}, s32[]{:S(2)}) async-start(s8[8388608]{0:T(1024)(128)(4,1)} %bitcast.341), calls=%async_computation.15 | async-start | bytes 8388608
  995.3 10.3 slice-start
  1029.5 8.1 copy-start.19
  1029.5 8.1 copy-start.21
  1046.3 274.5 %all-to-all-start.3 = ((bf16[32,24,1024]{2,1,0:T(8,128)(2,1)}), bf16[32,24,1024]{2,1,0:T(8,128)(2,1)}, u32[]{:S(2)}, u32[]{:S(2)}) async-start(bf16[32,24,1024]{2,1,0:T(8,128)(2,1)} %bitcast.81), calls=%async_computation.3 | async-start | bytes 3145728 | tf_op jit(solution)/shard_map/all_to_all | solution.py:690
  1049.7 17.1 %copy-start.52 = (f32[128,3072]{1,0:T(8,128)S(1)}, f32[128,3072]{1,0:T(8,128)}, u32[]{:S(2)}) copy-start(f32[128,3072]{1,0:T(8,128)} %copy-done.51) | copy-start | bytes 4718596
  1069.9 246.7 %copy-start.161 = (f32[2]{0:T(128)S(1)}, f32[2]{0:T(128)}, u32[]{:S(2)}) copy-start(f32[2]{0:T(128)} %copy-done.160) | copy-start | bytes 28
  1327.1 35.8 %copy-start.85 = (f32[7,1024]{1,0:T(8,128)S(1)}, f32[7,1024]{1,0:T(8,128)}, u32[]{:S(2)}) copy-start(f32[7,1024]{1,0:T(8,128)} %param.32) | copy-start | bytes 86020
  1327.1 35.8 %copy-start.108 = (f32[7,1024]{1,0:T(8,128)S(1)}, f32[7,1024]{1,0:T(8,128)}, u32[]{:S(2)}) copy-start(f32[7,1024]{1,0:T(8,128)} %param.38) | copy-start | bytes 86020
  1327.1 35.8 %copy-start.109 = (f32[7,1024]{1,0:T(8,128)S(1)}, f32[7,1024]{1,0:T(8,128)}, u32[]{:S(2)}) copy-start(f32[7,1024]{1,0:T(8,128)} %param.35) | copy-start | bytes 86020
  (143 other events, 563.8 us)
Sparse Core Ops, SparseCore 0:
  154.5 230.4 all-gather.11
  388.0 209.0 all-gather.15
  600.0 202.9 all-gather.13

commit v3 on v2

--- a/solution.py
+++ b/solution.py
@@ -208,9 +208,64 @@
 
 
 AXES = ("dp", "fsdp")
+
+
+FF_STEP = 512
+
+
+def norm_scale(values):
+    return lax.rsqrt(jnp.mean(values * values, axis=-1, keepdims=True) + EPSILON)
+
+
+def feed_kernel(residual_ref, gain_ref, in_ref, out_ref, result_ref, normed_ref):
+    @pl.when(pl.program_id(0) == 0)
+    def _():
+        residual = residual_ref[...]
+        normed_ref[...] = to_low(residual * norm_scale(residual) * gain_ref[...])
+        result_ref[...] = residual
+
+    before = jnp.dot(normed_ref[...], in_ref[...], preferred_element_type=jnp.float32)
+    active = to_low(jax.nn.relu(before))
+    result_ref[...] += lax.dot_general(
+        active, out_ref[...], (((1,), (1,)), ((), ())), preferred_element_type=jnp.float32
+    )
+
+
+def weight_spec(start):
+    return pl.BlockSpec((D, FF_STEP), lambda step: (0, step + start // FF_STEP))
+
+
+def whole_spec(shape):
+    return pl.BlockSpec(shape, lambda step: (0,) * len(shape))
+
+
+def feed_cost(rows):
+    return pl.CostEstimate(flops=4 * rows * D * FF, bytes_accessed=4 * D * FF, transcendentals=0)
+
+
+def feed_streamed(residual, gain_row, weight_in, weight_out):
+    rows = residual.shape[0]
+    (source_in, start_in), (source_out, start_out) = (weight_in, weight_out)
+    result = pl.pallas_call(
+        feed_kernel,
+        grid=(FF // FF_STEP,),
+        out_shape=jax.ShapeDtypeStruct((rows, D), jnp.float32),
+        in_specs=[
+            whole_spec((rows, D)),
+            whole_spec((1, D)),
+            weight_spec(start_in),
+            weight_spec(start_out),
+        ],
+        out_specs=whole_spec((rows, D)),
+        scratch_shapes=[pltpu.VMEM((rows, D), jnp.bfloat16)],
+        compiler_params=pltpu.CompilerParams(vmem_limit_bytes=40 * 2**20),
+        cost_estimate=feed_cost(rows),
+    )(residual, gain_row[None], source_in, source_out)
+    return (result, None)
+
+
 SLOTS = 24
 MESH = pl.DeviceIdType.MESH
-WAVE_STEP = 512
 
 
 def device_bits():
@@ -235,9 +290,10 @@
     )
 
 
-def wave_orders(wave):
-    orders = scatter_orders()
-    return orders[2:] if wave % 3 == 1 else orders[:2]
+def lane_widths(width):
+    if width % D == 0:
+        return (3 * width // 8, 3 * width // 8, width // 8, width // 8)
+    return (width // 4,) * 4
 
 
 def bit_of(bit):
@@ -308,26 +364,23 @@
     bits = device_bits()
     rows = shard.shape[0]
     row_step = row_step or rows
-    pieces = []
+    waves = []
     for which, (start, width) in enumerate(blocks):
         for low in range(0, width, step):
             for first in range(0, rows, row_step):
-                pieces.append((0, which, start + low, low, min(step, width - low), first, row_step))
-    waves = []
-    for wave in range(-(-len(pieces) // 2)):
-        waves.append(
-            [
-                piece + (tuple(reversed(order)),)
-                for piece, order in zip(pieces[2 * wave : 2 * wave + 2], wave_orders(wave))
-            ]
-        )
+                wave, at = ([], low)
+                for lane, order in zip(lane_widths(step), scatter_orders()):
+                    piece = (0, which, start + at, at, lane, first, row_step)
+                    wave.append(piece + (tuple(reversed(order)),))
+                    at += lane
+                waves.append(wave)
     operands = [shard]
     shapes = [((rows, width), shard.dtype) for _, width in blocks]
     if extra is not None:
         operands.append(extra)
         shapes.append((extra.shape, extra.dtype))
         piece = (1, len(blocks), 0, 0, extra.shape[1], 0, extra.shape[0])
-        waves[0].append(piece + (tuple(reversed(wave_orders(0)[0])),))
+        waves[0].append(piece + (tuple(reversed(scatter_orders()[0])),))
     total = sum(len(wave) for wave in waves)
     gathered = pl.pallas_call(
         functools.partial(gather_kernel, bits, len(operands), waves),
@@ -353,16 +406,81 @@
     return full.reshape((-1,) + values.shape)
 
 
-CORE_SLOTS = 4
+def total_kernel(sizes, x_ref, sum_ref, *scratch):
+    held, send_sem, recv_sem = (scratch[:2], scratch[2:4], scratch[4:6])
+    barrier = pltpu.get_barrier_semaphore()
+    peers = [(axis, hop) for axis, size in sizes for hop in range(1, size)]
+
+    def peer(axis, size, hop):
+        return {axis: lax.rem(lax.axis_index(axis) + hop, size)}
+
+    for axis, hop in peers:
+        pl.semaphore_signal(
+            barrier, inc=1, device_id=peer(axis, dict(sizes)[axis], hop), device_id_type=MESH
+        )
+    pl.semaphore_wait(barrier, len(peers))
+    value = x_ref[...]
+    for turn, (axis, size) in enumerate(sizes):
+        me = lax.axis_index(axis)
+        held[turn][me] = value
+        copies = []
+        for hop in range(1, size):
+            copies.append(
+                pltpu.make_async_remote_copy(
+                    src_ref=held[turn].at[me],
+                    dst_ref=held[turn].at[me],
+                    send_sem=send_sem[turn].at[hop],
+                    recv_sem=recv_sem[turn].at[hop],
+                    device_id=peer(axis, size, hop),
+                    device_id_type=MESH,
+                )
+            )
+            copies[-1].start()
+        for hop, copy in enumerate(copies, 1):
+            other = lax.rem(me + size - hop, size)
+            pltpu.make_async_remote_copy(
+                src_ref=held[turn].at[other],
+                dst_ref=held[turn].at[other],
+                send_sem=send_sem[turn].at[hop],
+                recv_sem=recv_sem[turn].at[hop],
+                device_id=peer(axis, size, hop),
+                device_id_type=MESH,
+            ).wait_recv()
+        value = held[turn][0]
+        for other in range(1, size):
+            value = value + held[turn][other]
+        for copy in copies:
+            copy.wait_send()
+    sum_ref[...] = value
+
+
+def total_of(tile, collective_id):
+    sizes = [(axis, lax.axis_size(axis)) for axis in reversed(AXES)]
+    in_vmem = pl.BlockSpec(memory_space=pltpu.VMEM)
+    marks = [pltpu.SemaphoreType.DMA((size,)) for _, size in sizes]
+    return pl.pallas_call(
+        functools.partial(total_kernel, sizes),
+        out_shape=jax.ShapeDtypeStruct(tile.shape, jnp.float32),
+        in_specs=[in_vmem],
+        out_specs=in_vmem,
+        scratch_shapes=[pltpu.VMEM((size,) + tile.shape, jnp.float32) for _, size in sizes]
+        + marks
+        + marks,
+        compiler_params=pltpu.CompilerParams(collective_id=collective_id, has_side_effects=True),
+        cost_estimate=busy_for(12),
+    )(tile)
+
+
+CORE_SLOTS = 2
 
 
 def scatter_kernel(bits, plan, *refs):
-    n_waves, slots, width, wide = (plan["waves"], plan["slots"], plan["step"], plan["wide"])
+    n_waves, slots, wide, widths = (plan["waves"], plan["slots"], plan["wide"], plan["widths"])
     n_ins, n_loaded = (plan["operands"], len(plan["loads"]))
     ins, out_ref = (refs[:n_ins], refs[n_ins])
     loaded, rest_refs = (refs[n_ins + 1 : n_ins + 1 + n_loaded], refs[n_ins + 1 + n_loaded :])
-    send_core, from_core, total, narrow, arrived, arrived_wide = rest_refs[:6]
-    load_sem, send_sem, recv_sem, free_sem = rest_refs[6:]
+    buffers = [rest_refs[6 * lane : 6 * lane + 6] for lane in range(len(widths))]
+    load_sem, send_sem, recv_sem, free_sem = rest_refs[6 * len(widths) :]
     depth = len(bits)
     mine = {bit: bit_of(bit) for bit in bits}
     core = scatter_orders()[0][0]
@@ -374,11 +492,12 @@
         bit_at[order[step]] = pl.ds(last, 1)
         return tuple(bit_at.get(bit, pl.ds(0, 2)) for bit in rest)
 
-    def slot_at(piece, step):
-        return lax.rem(piece, CORE_SLOTS if step == 0 else slots)
-
-    def copy(piece, step, order):
-        slot = slot_at(piece, step)
+    def span_of(step):
+        return CORE_SLOTS if step == 0 else slots
+
+    def copy(wave, lane, step, order):
+        send_core, from_core, total, narrow, arrived, arrived_wide = buffers[lane]
+        slot = lax.rem(wave, span_of(step))
         if step == 0:
             source, target = (send_core.at[slot], from_core.at[slot])
         else:
@@ -388,8 +507,8 @@
         return pltpu.make_async_remote_copy(
             src_ref=source,
             dst_ref=target,
-            send_sem=send_sem.at[slot, step],
-            recv_sem=recv_sem.at[slot, step],
+            send_sem=send_sem.at[lane, slot, step],
+            recv_sem=recv_sem.at[lane, slot, step],
             device_id=partner(order[step]),
             device_id_type=MESH,
         )
@@ -402,54 +521,55 @@
             came = tuple(1 - mine[bit] if bit == order[step] else at for bit, at in zip(rest, here))
             yield here, came
 
-    def keep(slot, at, value, step):
-        total[(slot,) + at] = value
-        if step not in wide:
-            narrow[(slot,) + at] = value.astype(jnp.bfloat16)
-
     def visit(wave, lane, step, order):
-        piece = wave * 2 + lane
-        slot = slot_at(piece, step)
-        span = (CORE_SLOTS if step == 0 else slots) // 2
-        reuse = wave >= span
+        send_core, from_core, total, narrow, arrived, arrived_wide = buffers[lane]
+        low, width = (sum(widths[:lane]), widths[lane])
+        slot = lax.rem(wave, span_of(step))
+        reuse = wave >= span_of(step)
+
+        def keep(at, value, next_step):
+            total[(slot,) + at] = value
+            if next_step not in wide:
+                narrow[(slot,) + at] = value.astype(jnp.bfloat16)
+
         if step == 0:
 
             @pl.when(reuse)
             def _():
-                copy(piece, 0, order).wait_send()
+                copy(wave, lane, 0, order).wait_send()
 
             def put(at, value):
                 send_core[(slot,) + at] = value
 
-            plan["produce"](loaded, piece, 1 - mine[core], put)
+            plan["produce"](loaded, wave, low, width, 1 - mine[core], put)
         else:
-            copy(piece, step - 1, order).wait_recv()
+            copy(wave, lane, step - 1, order).wait_recv()
             if step == 1:
-                core_slot = slot_at(piece, 0)
+                core_slot = lax.rem(wave, CORE_SLOTS)
 
                 @pl.when(reuse)
                 def _():
                     for old in range(1, depth):
-                        copy(piece, old, order).wait_send()
+                        copy(wave, lane, old, order).wait_send()
 
                 def add(at, value):
-                    keep(slot, at, value + from_core[(core_slot,) + at], 1)
-
-                plan["produce"](loaded, piece, mine[core], add)
+                    keep(at, value + from_core[(core_slot,) + at], 1)
+
+                plan["produce"](loaded, wave, low, width, mine[core], add)
             else:
                 source = arrived_wide if step - 1 in wide else arrived
                 for here, came in kept_entries(order, step - 1):
                     value = total[(slot,) + here] + source[(slot,) + came].astype(jnp.float32)
                     if step == depth:
-                        start = plan["column"](piece)
-                        out_ref[:, pl.ds(pl.multiple_of(start, width), width)] = value
+                        start = plan["column"](wave) + low
+                        out_ref[:, pl.ds(pl.multiple_of(start, 128), width)] = value
                     else:
-                        keep(slot, here, value, step)
-
-            @pl.when(wave + (CORE_SLOTS if step == 1 else slots) // 2 < n_waves)
+                        keep(here, value, step)
+
+            @pl.when(wave + span_of(step - 1) < n_waves)
             def _():
                 pl.semaphore_signal(
-                    free_sem.at[slot_at(piece, step - 1), step - 1],
+                    free_sem.at[lane, lax.rem(wave, span_of(step - 1)), step - 1],
                     inc=1,
                     device_id=partner(order[step - 1]),
                     device_id_type=MESH,
@@ -459,9 +579,9 @@
 
             @pl.when(reuse)
             def _():
-                pl.semaphore_wait(free_sem.at[slot, step], 1)
-
-            copy(piece, step, order).start()
+                pl.semaphore_wait(free_sem.at[lane, slot, step], 1)
+
+            copy(wave, lane, step, order).start()
 
     loads = []
     for number, (_, parts) in enumerate(plan["loads"]):
@@ -470,55 +590,57 @@
             loads.append(pltpu.make_async_copy(ins[operand], at, load_sem.at[operand]))
             loads[-1].start()
 
-    def group(first, carry):
-        for phase in range(3):
-            for step in range(depth + 1):
-                wave = first * 3 + phase - step
-
-                @pl.when((wave >= 0) & (wave < n_waves))
-                def _():
-                    if step == 0:
-                        for late, count in plan["waits"]:
-
-                            @pl.when(wave == late)
-                            def _():
-                                for load in loads[slice(*count)]:
-                                    load.wait()
-
-                    for lane, order in enumerate(wave_orders(phase - step)):
-                        visit(wave, lane, step, order)
+    def turn_of(turn, carry):
+        for step in range(depth + 1):
+            wave = turn - step
+
+            @pl.when((wave >= 0) & (wave < n_waves))
+            def _():
+                if step == 0:
+                    for late, count in plan["waits"]:
+
+                        @pl.when(wave == late)
+                        def _():
+                            for load in loads[slice(*count)]:
+                                load.wait()
+
+                for lane, order in enumerate(plan["orders"]):
+                    visit(wave, lane, step, order)
 
         return carry
 
     greet(bits)
-    lax.fori_loop(0, -(-(n_waves + depth) // 3), group, 0)
+    lax.fori_loop(0, n_waves + depth, turn_of, 0)
     for step in range(depth):
-        for wave in range(max(0, n_waves - (CORE_SLOTS if step == 0 else slots) // 2), n_waves):
-            for lane, order in enumerate(wave_orders(wave)):
-                copy(wave * 2 + lane, step, order).wait_send()
+        for wave in range(max(0, n_waves - span_of(step)), n_waves):
+            for lane, order in enumerate(plan["orders"]):
+                copy(wave, lane, step, order).wait_send()
 
 
 def tree_scatter(operands, plan, collective_id, micros):
     bits = device_bits()
-    slots, width, rows = (plan["slots"], plan["step"], plan["rows"])
+    slots, widths, rows = (plan["slots"], plan["widths"], plan["rows"])
     plan = dict(plan, operands=len(operands))
-    entries = (2,) * (len(bits) - 1) + (rows, width)
-    core_buffer = pltpu.VMEM((CORE_SLOTS,) + entries, jnp.float32)
-    low_buffer = pltpu.VMEM((slots,) + entries, jnp.bfloat16)
-    sums = pltpu.VMEM((slots,) + entries, jnp.float32)
-    wide_buffer = sums if plan["wide"] else pltpu.VMEM((8, 128), jnp.float32)
+    scratch = [pltpu.VMEM(shape, jnp.bfloat16) for shape, _ in plan["loads"]]
+    for width in widths:
+        entries = (2,) * (len(bits) - 1) + (rows, width)
+        core_buffer = pltpu.VMEM((CORE_SLOTS,) + entries, jnp.float32)
+        low_buffer = pltpu.VMEM((slots,) + entries, jnp.bfloat16)
+        sums = pltpu.VMEM((slots,) + entries, jnp.float32)
+        wide_buffer = sums if plan["wide"] else pltpu.VMEM((8, 128), jnp.float32)
+        scratch += [core_buffer, core_buffer, sums, low_buffer, low_buffer, wide_buffer]
+    marks = (len(widths), slots, len(bits))
     return pl.pallas_call(
         functools.partial(scatter_kernel, bits, plan),
-        out_shape=jax.ShapeDtypeStruct((rows, 2 * plan["waves"] * width), jnp.float32),
+        out_shape=jax.ShapeDtypeStruct((rows, plan["waves"] * sum(widths)), jnp.float32),
         in_specs=[pl.BlockSpec(memory_space=pl.ANY)] * len(operands),
         out_specs=pl.BlockSpec(memory_space=pltpu.VMEM),
-        scratch_shapes=[pltpu.VMEM(shape, jnp.bfloat16) for shape, _ in plan["loads"]]
-        + [core_buffer, core_buffer, sums, low_buffer, low_buffer, wide_buffer]
+        scratch_shapes=scratch
         + [
             pltpu.SemaphoreType.DMA((len(operands),)),
-            pltpu.SemaphoreType.DMA((slots, len(bits))),
-            pltpu.SemaphoreType.DMA((slots, len(bits))),
-            pltpu.SemaphoreType.REGULAR((slots, len(bits))),
+            pltpu.SemaphoreType.DMA(marks),
+            pltpu.SemaphoreType.DMA(marks),
+            pltpu.SemaphoreType.REGULAR(marks),
         ],
         compiler_params=pltpu.CompilerParams(
             collective_id=collective_id, has_side_effects=True, vmem_limit_bytes=60 * 2**20
@@ -541,14 +663,14 @@
         put((across,) + at, value[number * rows : (number + 1) * rows])
 
 
-def layer_products(dec_blocks, enc_blocks, step, rows, loaded, piece, core, put):
+def layer_products(dec_blocks, enc_blocks, rows, loaded, wave, low, width, core, put):
     dec_left, dec_right, enc_left, enc_right = loaded
-    dec_pieces = dec_right.shape[1] // step
+    dec_waves = sum(dec_blocks)
     quarter = D // 4
 
-    def product(left, right, blocks, number):
-        unit = unit_of(lax.div(number * step, D), blocks)
-        sides = right[:, pl.ds(pl.multiple_of(number * step, step), step)]
+    def product(left, right, blocks, block):
+        unit = unit_of(block, blocks)
+        sides = right[:, pl.ds(pl.multiple_of(block * D + low, 128), width)]
         for across in range(2):
             some = pl.ds(pl.multiple_of((2 * across + core) * quarter, quarter), quarter)
             value = lax.dot_general(
@@ -559,20 +681,18 @@
             )
             put_rows(value, across, rows, put)
 
-    @pl.when(piece < dec_pieces)
+    @pl.when(wave < dec_waves)
     def _():
-        product(dec_left, dec_right, dec_blocks, piece)
-
-    @pl.when(piece >= dec_pieces)
+        product(dec_left, dec_right, dec_blocks, wave)
+
+    @pl.when(wave >= dec_waves)
     def _():
-        product(enc_left, enc_right, enc_blocks, piece - dec_pieces)
-
-
-def layer_column(step, piece):
-    per_block = D // step
-    half = 14 * per_block
-    is_enc = lax.div(piece, half)
-    block = lax.div(piece - is_enc * half, per_block)
+        product(enc_left, enc_right, enc_blocks, wave - dec_waves)
+
+
+def layer_column(wave):
+    is_enc = lax.div(wave, 14)
+    block = wave - is_enc * 14
 
     def past(edge):
         return lax.div(block + 14 - edge, 14)
@@ -580,7 +700,7 @@
     dec_shift = 4 + 2 * past(5) + 8 * past(6)
     enc_shift = 5 * past(4) + past(6)
     shift = dec_shift + is_enc * (enc_shift - dec_shift)
-    return (block + shift) * D + lax.rem(piece, per_block) * step
+    return (block + shift) * D
 
 
 def scatter_layers(dec_pairs, enc_pairs, rows, collective_id):
@@ -599,24 +719,24 @@
         loads.append(((tokens, at), parts))
         counts.append([right_side.shape[1] // D for _, right_side in pairs])
     dec_loads = 2 * len(dec_pairs)
-    dec_waves = loads[1][0][1] // (2 * WAVE_STEP)
     plan = {
-        "waves": dec_waves + loads[3][0][1] // (2 * WAVE_STEP),
-        "slots": 12,
-        "step": WAVE_STEP,
+        "waves": sum(counts[0]) + sum(counts[1]),
+        "slots": 6,
+        "widths": lane_widths(D),
+        "orders": scatter_orders(),
         "rows": rows,
         "wide": (),
         "loads": loads,
-        "waits": ((0, (0, dec_loads)), (dec_waves, (dec_loads, None))),
-        "produce": functools.partial(layer_products, counts[0], counts[1], WAVE_STEP, rows),
-        "column": functools.partial(layer_column, WAVE_STEP),
+        "waits": ((0, (0, dec_loads)), (sum(counts[0]), (dec_loads, None))),
+        "produce": functools.partial(layer_products, counts[0], counts[1], rows),
+        "column": layer_column,
     }
-    return tree_scatter(operands, plan, collective_id, 230)
-
-
-def final_products(step, rows, loaded, piece, core, put):
+    return tree_scatter(operands, plan, collective_id, 210)
+
+
+def final_products(step, rows, loaded, wave, low, width, core, put):
     left, right = loaded
-    sides = right[:, pl.ds(pl.multiple_of(piece * step, step), step)]
+    sides = right[:, pl.ds(pl.multiple_of(wave * step + low, 128), width)]
     for across in range(2):
         value = jnp.dot(left[across, core], sides, preferred_element_type=jnp.float32)
         put_rows(value, across, rows, put)
@@ -624,7 +744,7 @@
 
 def scatter_final(grad_logits, table, collective_id):
     bits = device_bits()
-    n_dev, step, width = (2 ** len(bits), 128, table.shape[1])
+    n_dev, step, width = (2 ** len(bits), 256, table.shape[1])
     rows_all = grad_logits.shape[0] // n_dev
     turns = max(1, n_dev // 32)
     rows = rows_all // turns
@@ -633,15 +753,16 @@
         some = grad_logits.reshape(n_dev, rows_all, -1)[:, turn * rows : (turn + 1) * rows]
         some = some.reshape(2, 2, n_dev // 4 * rows, -1)
         plan = {
-            "waves": width // (2 * step),
+            "waves": width // step,
             "slots": width // step,
-            "step": step,
+            "widths": (step // 2, step // 2),
+            "orders": scatter_orders()[:2],
             "rows": rows,
             "wide": (len(bits) - 2, len(bits) - 1),
             "loads": [(some.shape, [(0, ())]), (table.shape, [(1, ())])],
             "waits": ((0, (0, 2)),),
             "produce": functools.partial(final_products, step, rows),
-            "column": lambda piece: piece * step,
+            "column": lambda wave: wave * step,
         }
         sums.append(tree_scatter([some, table], plan, collective_id + turn, 60))
     return jnp.concatenate(sums, axis=0)
@@ -730,8 +851,8 @@
     return to_low(jnp.einsum("nk,nd->kd", pick, gradient, preferred_element_type=jnp.float32))
 
 
-def return_rows(plan, asked, rounds, first_sums, gradient, rows_here, n_dev):
-    sums = collect(asked, first_sums, rows_here, n_dev)
+def return_rows(plan, asked, rounds, first_sums, gradient, table_grad, n_dev):
+    rows_here = table_grad.shape[0]
 
     def more(state):
         turn, sums = state
@@ -739,7 +860,8 @@
         pick = picking(plan, turn, n_dev)
         return (turn + 1, sums + collect(asked, row_sums(pick, gradient), rows_here, n_dev))
 
-    return lax.while_loop(lambda state: state[0] < rounds, more, (jnp.int32(1), sums))[1]
+    sums = lax.while_loop(lambda state: state[0] < rounds, more, (jnp.int32(1), table_grad))[1]
+    return sums + collect(asked, first_sums, rows_here, n_dev)
 
 
 ENC_BLOCKS = ((0, 3 * D), (3 * D, D), (9 * D, 2 * D), (12 * D, FF), (12 * D + FF, FF))
@@ -759,11 +881,11 @@
 
 
 def split_blocks(part, blocks):
-    gathered, at = ([], 0)
-    for _, width in blocks:
-        gathered.append(part[:, at : at + width])
+    gathered, at = ({}, 0)
+    for low, width in blocks:
+        gathered[low] = (part, at, width)
         at += width
-    return by_column(blocks, gathered)
+    return gathered
 
 
 def after(values, *others):
@@ -771,16 +893,25 @@
 
 
 def columns(layer_full, first_column, column_count):
-    assert layer_full[first_column].shape[1] == column_count
-    return layer_full[first_column]
+    part, start, width = layer_full[first_column]
+    assert width == column_count
+    return part[:, start : start + width]
 
 
 def by_column(blocks, gathered):
-    return {low: value for (low, _), value in zip(blocks, gathered)}
+    return {low: (value, 0, width) for (low, width), value in zip(blocks, gathered)}
+
+
+def feed(residual, gain_row, layer_full, first_column, streamed):
+    if streamed:
+        weights = [layer_full[low][:2] for low in (first_column, first_column + FF)]
+        return feed_streamed(residual, gain_row, *weights)
+    weights = [columns(layer_full, low, FF) for low in (first_column, first_column + FF)]
+    return feed_forward(residual, gain_row, *weights)
 
 
 def shard_stats(final_rows, table_shard, targets, collective_ids):
-    all_rows = gather_whole(final_rows, 128, collective_ids[0], 50, final_rows.shape[0] // 2)
+    all_rows = gather_whole(final_rows, D, collective_ids[0], 45, final_rows.shape[0] // 4)
     all_rows = all_rows.reshape(-1, D)
     logits = jnp.einsum("rd,vd->rv", all_rows, table_shard, preferred_element_type=jnp.float32)
     logits = with_layout_constraint(logits, Layout(major_to_minor=(0, 1)))
@@ -789,15 +920,15 @@
     largest = jnp.max(logits, axis=1)
     total = jnp.sum(jnp.exp(logits - largest[:, None]), axis=1)
     picked = jnp.sum(jnp.where(hot, logits, 0.0), axis=1)
-    stats = jnp.stack([largest, total, picked]).reshape(8, -1)
-    stats = gather_whole(stats, stats.shape[1] // 4, collective_ids[1], 20)
-    stats = stats.reshape(-1, 3, largest.shape[0])
-    peak = jnp.max(stats[:, 0], axis=0)
-    log_own = peak + jnp.log(jnp.sum(stats[:, 1] * jnp.exp(stats[:, 0] - peak), axis=0))
-    return (jnp.sum(stats[:, 2], axis=0) - log_own, log_own, logits, hot, all_rows)
-
-
-def forward(token_rows, enc_full, dec_full_after, gain_rows, batch_data):
+    stats = jnp.concatenate([part.reshape(8, -1) for part in (largest, total, picked)], axis=0)
+    stats = gather_whole(stats, stats.shape[1], collective_ids[1], 20)
+    peak = jnp.max(stats[:, :8], axis=0)
+    log_own = peak + jnp.log(jnp.sum(stats[:, 8:16] * jnp.exp(stats[:, :8] - peak), axis=0))
+    token_logp = (jnp.sum(stats[:, 16:], axis=0) - log_own).reshape(-1)
+    return (token_logp, log_own.reshape(-1), logits, hot, all_rows)
+
+
+def forward(token_rows, enc_full, dec_full_after, gain_rows, batch_data, streamed=False):
     (
         prompt_ids,
         decoder_input,
@@ -819,12 +950,7 @@
         enc_allowed,
         (pairs_here, P_MAX),
     )
-    encoder_two, encoder_ffn = feed_forward(
-        encoder_one,
-        gain_rows[1],
-        columns(enc_full, 12 * D, FF),
-        columns(enc_full, 12 * D + FF, FF),
-    )
+    encoder_two, encoder_ffn = feed(encoder_one, gain_rows[1], enc_full, 12 * D, streamed)
     encoder_final = to_low(rms_norm(encoder_two, gain_rows[2]))
     cross_memory = to_low(matmul(encoder_final, columns(enc_full, 9 * D, 2 * D))).reshape(
         pairs_here, P_MAX, 2 * D
@@ -849,11 +975,8 @@
         cross_allowed,
         (seat_count, R_MAX),
     )
-    decoder_three, decoder_ffn = feed_forward(
-        decoder_two,
-        gain_rows[5],
-        columns(layer_full, 12 * D + 2 * FF, FF),
-        columns(layer_full, 12 * D + 3 * FF, FF),
+    decoder_three, decoder_ffn = feed(
+        decoder_two, gain_rows[5], layer_full, 12 * D + 2 * FF, streamed
     )
     final_rows = to_low(final_norm(decoder_three, gain_rows[6]))
     stored = (
@@ -1019,7 +1142,7 @@
     )
     packed = jnp.pad(packed, (0, -packed.shape[0] % 1024)).reshape(8, -1)
     *policy_enc, notes = tree_gather(
-        to_low(policy_layers), ENC_BLOCKS, WAVE_STEP, 1, 130, extra=packed
+        to_low(policy_layers), ENC_BLOCKS, D, 1, 115, extra=packed
     )
     notes = notes.reshape(n_dev, -1)
     asked = mine_of(notes)
@@ -1082,7 +1205,7 @@
     )
     frozen_inputs = after(frozen_tokens, grad_zero)
     frozen_rows, unused = forward(
-        frozen_inputs, frozen_layer_enc, frozen_after, frozen_gains, batch_data
+        frozen_inputs, frozen_layer_enc, frozen_after, frozen_gains, batch_data, True
     )
     frozen_logp = logp_of(shard_stats(frozen_rows, frozen_embed, targets, (5, 6))[0])
     frozen_mean = lax.dynamic_index_in_dim(
@@ -1102,12 +1225,6 @@
         sign_value * jnp.sum(all_select * pair_slope[:, None, :], axis=2)
         - CHOSEN_WEIGHT * chosen_float / sequence_divisor
     ) / MICRO
-    table_grad = jnp.einsum(
-        "rc,rd->cd",
-        row_slope,
-        to_low(jnp.repeat(sequence_slope.reshape(-1), R_MAX)[:, None] * all_rows),
-        preferred_element_type=jnp.float32,
-    )
     slope_here = lax.dynamic_index_in_dim(sequence_slope, me, 0, keepdims=False)
     slope_rows = jnp.repeat(slope_here, R_MAX)[:, None]
     memory_slope = (select_float * slope_here[:, None])[:, :, None, None, None]
@@ -1135,15 +1252,19 @@
             scaled_pairs.append((left, to_low(slope_rows * right)))
     token_gradient = to_low(token_gradient)
     first_sums = row_sums(picking(plan, 0, n_dev), token_gradient)
+    late_slope = after(sequence_slope, first_sums)
+    table_grad = jnp.einsum(
+        "rc,rd->cd",
+        row_slope,
+        to_low(jnp.repeat(late_slope.reshape(-1), R_MAX)[:, None] * all_rows),
+        preferred_element_type=jnp.float32,
+    )
     table_grad = after(table_grad, first_sums)
     enc_pairs[0] = (after(enc_pairs[0][0], first_sums, table_grad), enc_pairs[0][1])
-    embed_grad = table_grad + return_rows(
-        plan, asked, rounds, first_sums, token_gradient, rows_here, n_dev
-    )
+    embed_grad = return_rows(plan, asked, rounds, first_sums, token_gradient, table_grad, n_dev)
     layer_grad = scatter_layers(scaled_pairs, enc_pairs, policy_layers.shape[0], 8)
     squares_local = jnp.sum(embed_grad * embed_grad) + jnp.sum(layer_grad * layer_grad)
-    shared = jnp.concatenate([gain_grads, jnp.full((1, D), squares_local)], axis=0)
-    shared = jnp.sum(gather_whole(shared, D, 9, 20), axis=0)
+    shared = total_of(jnp.concatenate([gain_grads, jnp.full((1, D), squares_local)], axis=0), 9)
     gain_total, squares_total = (shared[:7], shared[7, 0])
     grad_norm = jnp.sqrt(squares_total + jnp.sum(gain_total * gain_total))
     factor = jnp.minimum(1.0, CLIP_NORM / grad_norm)

time: 1410 us -> 1360 us (0.965)
  matrix products: 261 us -> 227 us
  local copies, waits for them, and re-layouts: 130 us -> 107 us
    pallas_call x0 -> x3, Pallas kernels: none -> 36.1 us  [the longest x2 22.7 us: feed_streamed(): pl.pallas_call(feed_kernel, grid=(FF // FF_STEP,), out_shape=jax.ShapeDty...]
    pallas_call x6 -> x5, Pallas kernels: 337 us -> 307 us  [tree_gather(): pl.pallas_call(functools.partial(gather_kernel, bits, len(operands), wave...]
    dot_general x4 -> x2, matrix products: 35.3 us -> 11 us  [feed_forward(): jnp.einsum('rf,df->rd', active, weight_out, preferred_element_type=jnp.fl...]
  transfers between devices with their start and end apart: 5 -> 5, of which waited for: 2 -> 2; matrix products, arithmetic and copies ran while one was open for 21% -> 18% of each run, Pallas kernels for 34% -> 35%
where the time goes in v3:
time: 1360 us; the launch traced here: 1350 us
  Pallas kernels  698 us (51%)
  matrix products  227 us (17%)
  waiting for transfers between devices  159 us (12%)
  other arithmetic  124 us (9%)
  local copies, waits for them, and re-layouts  107 us (8%)
  between operations  25.6 us (2%)
    pallas_call x2, Pallas kernels, tree_scatter(): pl.pallas_call(functools.partial(scatter_kernel, bits, plan), out_shape=j...  354 us
    pallas_call x5, Pallas kernels, tree_gather(): pl.pallas_call(functools.partial(gather_kernel, bits, len(operands), wave...  307 us
    all_to_all x2, waiting for transfers between devices, swap(): lax.all_to_all(rows.reshape(n_dev, SLOTS, wide), AXES, 0, 0, tiled=True)  124 us
    dot_general x22, matrix products, matmul(): return jnp.dot(left_side, right_side, preferred_element_type=jnp.float32)  81.1 us
    dot_general x9, matrix products, matmul_back(): jnp.einsum('re,de->rd', grad_low, weight, preferred_element_type=jnp.floa...  38.9 us
    all_gather x3, waiting for transfers between devices, gather_offloaded(): return lax.all_gather(part, AXES, axis=0, tiled=True)  35.4 us
    convert_element_type x17, other arithmetic, to_low(): return values.astype(jnp.bfloat16)  30.8 us
    dot_general x2, matrix products, shard_stats(): jnp.einsum('rd,vd->rv', all_rows, table_shard, preferred_element_type=jnp...  30.3 us
  transfers between devices with their start and end apart: 5, of which 2 were waited for; matrix products, arithmetic and copies ran while one was open for 18% of the time, Pallas kernels for 35%

profile of v3, /device:TPU:0, one launch (start us, length us, event | category | flops | bytes accessed | tf_op | source)
XLA Modules:
  0.0 1352.8 jit_solution(17086807005359715264)
XLA Ops:
  18.1 3.4 convert_bitcast_fusion.refs_0_
  21.5 130.0 %shard_map.282 = (bf16[2,2,2,2,2,32,3072]{6,5,4,3,2,1,0:T(8,128)(2,1)}, bf16[2,2,2,2,2,32,1024]{6,5,4,3,2,1,0:T(8,128)(2,1)}, bf16[2,2,2,2,2,32,2048]{6,5,4,3,2,...) custom-call(bf16[1,1,1,1,1,32,28672]{6,5,4,3,2,1,0:T(8,128)(2,1)} %c, ...), custom_call_target="tpu_custom_call" | custom-call | bytes 391000000 | tf_op jit(solution)/shard_map/pallas_call | solution.py:385
  155.1 3.8 convert_element_type.355.refs_1_
  158.9 3.6 fusion.105
  166.3 6.1 all-to-all-start.2
  174.0 123.9 %all-to-all-done.2 = bf16[32,24,2048]{2,1,0:T(8,128)(2,1)S(1)} async-done(((bf16[32,24,2048]{2,1,0:T(8,128)(2,1)}), bf16[32,24,2048]{2,1,0:T(8,128)(2,1)S(1)}, u32[]{:S(2)}, u32[]{:S(2)}) %all-to-all-start.2) | async-done | bytes 3145760 | tf_op jit(solution)/shard_map/all_to_all | solution.py:811
  306.0 5.9 convolution_convert_fusion.1
  326.7 8.1 maximum_convert_fusion.refs_21_
  334.9 3.5 multiply_reduce_fusion.11
  341.7 4.1 convolution_convert_fusion.2
  351.8 35.4 %all-gather.12.cloned.1.call-done = bf16[1024,14336]{1,0:T(8,128)(2,1)} async-done(((bf16[32,14336]{1,0:T(8,128)(2,1)}), bf16[1024,14336]{1,0:T(8,128)(2,1)}) %all-gather.12.cloned.1.call-update) | async-done | bytes 29360144 | tf_op jit(solution)/shard_map/all_gather | solution.py:880
  387.2 3.8 fusion.64
  412.4 4.7 fusion.51.refs_11_
  417.2 7.4 multiply_reduce_fusion.22
  432.9 79.1 %shard_map.283 = bf16[2,2,2,2,2,128,1024]{6,5,4,3,2,1,0:T(8,128)(2,1)} custom-call(bf16[1,1,1,1,1,128,1024]{6,5,4,3,2,1,0:T(8,128)(2,1)} %fusion.352.refs_0_), custom_call_target="tpu_custom_call" | custom-call | bytes 153000000 | tf_op jit(solution)/shard_map/pallas_call | solution.py:385
  512.0 15.4 %fusion.284 = (f32[4096]{0:T(1024)S(1)}, f32[4096,1004]{1,0:T(8,128)}) fusion(bf16[4096,1024]{1,0:T(8,128)(2,1)} %bitcast.242, bf16[1004,1024]{1,0:T(8,128)(2,1)} %convert_element_type.355.refs_1_), kind=kOutput, calls=%fused_computation.475 | convolution fusion | flops 8426270720 | bytes 26910720 | tf_op jit(solution)/shard_map/rd,vd->rv/dot_general | solution.py:916
  527.4 8.3 exponential_reduce_fusion.1
  536.3 31.0 %shard_map.284 = f32[2,2,2,2,2,24,512]{6,5,4,3,2,1,0:T(8,128)} custom-call(f32[1,1,1,1,1,24,512]{6,5,4,3,2,1,0:T(8,128)} %maximum_bitcast_fusion.refs_0_), custom_call_target="tpu_custom_call" | custom-call | bytes 68000000 | tf_op jit(solution)/shard_map/pallas_call | solution.py:385
  570.5 10.8 select_convert_fusion
  581.3 112.1 %shard_map.285 = f32[128,1024]{1,0:T(8,128)} custom-call(bf16[2,2,1024,1004]{3,2,1,0:T(8,128)(2,1)} %bitcast.229, bf16[1004,1024]{1,0:T(8,128)(2,1)} %convert_element_type.355.refs_1_), custom_call_target="tpu_custom_call" | custom-call | bytes 204000000 | tf_op jit(solution)/shard_map/pallas_call | solution.py:633
  695.9 5.0 fusion.56
  701.0 7.1 multiply_reduce_fusion.20
  750.6 5.7 fusion.203
  759.9 4.2 convolution_multiply_fusion
  767.0 5.9 fusion.59
  787.7 12.3 shard_map.286
  800.2 4.0 fusion.79
  809.5 3.8 fusion.67
  831.7 10.4 shard_map.287
  843.0 48.9 %shard_map.288 = bf16[2,2,2,2,2,128,1024]{6,5,4,3,2,1,0:T(8,128)(2,1)} custom-call(bf16[1,1,1,1,1,128,1024]{6,5,4,3,2,1,0:T(8,128)(2,1)} %fusion.226.refs_0_), custom_call_target="tpu_custom_call" | custom-call | bytes 153000000 | tf_op jit(solution)/shard_map/pallas_call | solution.py:385
  892.0 14.9 %fusion.287 = (f32[4096]{0:T(1024)S(1)}, f32[4096,1004]{1,0:T(8,128)}) fusion(bf16[4096,1024]{1,0:T(8,128)(2,1)} %bitcast.244, bf16[1004,1024]{1,0:T(8,128)(2,1)S(1)} %copy-done.163), kind=kOutput, calls=%fused_computation.478 | convolution fusion | flops 8426270720 | bytes 26910720 | tf_op jit(solution)/shard_map/rd,vd->rv/dot_general | solution.py:916
  906.8 8.2 exponential_reduce_fusion
  915.7 18.4 %shard_map.289 = f32[2,2,2,2,2,24,512]{6,5,4,3,2,1,0:T(8,128)} custom-call(f32[1,1,1,1,1,24,512]{6,5,4,3,2,1,0:T(8,128)} %maximum_bitcast_fusion.1.refs_0_), custom_call_target="tpu_custom_call" | custom-call | bytes 68000000 | tf_op jit(solution)/shard_map/pallas_call | solution.py:385
  938.9 5.9 multiply_reduce_fusion
  954.7 4.9 multiply_reduce_fusion.6
  961.8 7.4 select_convert_fusion.1.refs_20_
  969.3 3.7 multiply_reduce_fusion.7
  979.1 5.5 fusion.136
  1004.7 7.8 fusion.117
  1012.8 4.0 multiply_convert_fusion.13
  1020.1 13.1 fusion.30
  1035.9 4.0 all-to-all-start.3
  1046.3 242.1 %shard_map.290 = f32[32,28672]{1,0:T(8,128)} custom-call(bf16[128,1024]{1,0:T(8,128)(2,1)} %copy-done.67, bf16[128,1024]{1,0:T(8,128)(2,1)} %copy-done.65, bf16[128,1024]{1,0:T(8,128)(2,1)} %copy-done.68, bf16[128,1024]{1,0:T(8,128)(2,1)} %copy-done.66, bf16[128,1024]{1,0:T(8,128)(2,1)} %copy-done.69, bf16[128,1024]{1,0:T(8,128)(2,1)} %get-tuple-element.429.refs_5_, ...), custom_call_target="tpu_custom_call" | custom-call | bytes 714000000 | tf_op jit(solution)/shard_map/pallas_call | solution.py:633
  1289.0 3.6 multiply_reduce_fusion.4
  1292.6 7.2 multiply_reduce_fusion.3
  1301.7 13.4 shard_map.291
  1320.5 10.4 add_multiply_fusion.2
  1331.0 12.6 add_multiply_fusion
  (643 shorter events, 232.6 us)
Async XLA Ops:
  7.2 380.1 %all-gather.12.cloned.1.call-start = ((), (), s32[]{:S(2)}) async-start(), calls=%async_computation.4 | async-start | bytes 30277632 | tf_op jit(solution)/shard_map/all_gather | solution.py:880
  12.4 287.5 %copy-start.126 = (s32[512]{0:T(512)}, s32[512]{0:T(512)S(1)}, u32[]{:S(2)}) copy-start(s32[512]{0:T(512)S(1)} %get-tuple-element.421) | copy-start | bytes 6148
  154.9 17.8 %copy-start.73 = (s32[4,8,8,128]{3,1,2,0:T(8,128)}, s32[4,8,8,128]{3,1,2,0:T(8,128)S(1)}, u32[]{:S(2)}) copy-start(s32[4,8,8,128]{3,1,2,0:T(8,128)S(1)} %copy.509) | copy-start | bytes 393220
  166.3 131.6 %all-to-all-start.2 = ((bf16[32,24,2048]{2,1,0:T(8,128)(2,1)}), bf16[32,24,2048]{2,1,0:T(8,128)(2,1)S(1)}, u32[]{:S(2)}, u32[]{:S(2)}) async-start(bf16[32,24,2048]{2,1,0:T(8,128)(2,1)} %bitcast.7), calls=%async_computation.2 | async-start | bytes 6291456 | tf_op jit(solution)/shard_map/all_to_all | solution.py:811
  172.4 594.6 %all-gather.16.cloned.1.call-start = ((), (), s32[]{:S(2)}) async-start(), calls=%async_computation.6 | async-start | bytes 30277632 | tf_op jit(solution)/shard_map/all_gather | solution.py:880
  174.0 130.5 %copy-start.97 = (f32[1,1024]{1,0:T(1,128)}, f32[1,1024]{1,0:T(1,128)S(1)}, u32[]{:S(2)}) copy-start(f32[1,1024]{1,0:T(1,128)S(1)} %get-tuple-element.416) | copy-start | bytes 12292
  174.0 152.5 %copy-start.99 = (f32[1,1024]{1,0:T(1,128)}, f32[1,1024]{1,0:T(1,128)S(1)}, u32[]{:S(2)}) copy-start(f32[1,1024]{1,0:T(1,128)S(1)} %get-tuple-element.415) | copy-start | bytes 12292
  303.1 8.8 copy-start.75
  303.1 8.8 copy-start.79
  303.1 8.8 copy-start.85
  303.1 8.8 copy-start.90
  303.1 8.8 copy-start.92
  323.5 11.4 slice-start.10
  326.5 8.4 copy-start.118
  326.5 8.4 copy-start.8
  326.5 8.4 copy-start.121
  326.7 8.1 copy-start.46
  326.7 8.2 slice-start.11
  341.3 468.1 %all-gather.14.cloned.1.call-start = ((), (), s32[]{:S(2)}) async-start(), calls=%async_computation.5 | async-start | bytes 30277632 | tf_op jit(solution)/shard_map/all_gather | solution.py:880
  341.6 60.4 %copy-start.154 = (pred[4,192]{1,0:T(4,128)(4,1)}, pred[4,192]{1,0:T(4,128)(4,1)S(1)}, u32[]{:S(2)}) copy-start(pred[4,192]{1,0:T(4,128)(4,1)S(1)} %convolution_compare_fusion) | copy-start | bytes 2308
  341.7 51.2 %copy-start.124 = (pred[4,32,32]{1,2,0:T(8,128)(4,1)}, pred[4,32,32]{1,2,0:T(8,128)(4,1)S(1)}, u32[]{:S(2)}) copy-start(pred[4,32,32]{1,2,0:T(8,128)(4,1)S(1)} %broadcast_and_fusion) | copy-start | bytes 12292
  349.0 38.2 %copy-start.67 = (bf16[128,1024]{1,0:T(8,128)(2,1)}, bf16[128,1024]{1,0:T(8,128)(2,1)S(1)}, u32[]{:S(2)}) copy-start(bf16[128,1024]{1,0:T(8,128)(2,1)S(1)} %fusion.193.refs_0_) | copy-start | bytes 786436
  424.7 270.0 %copy-start.139 = (f32[128]{0:T(128)}, f32[128]{0:T(128)S(1)}, u32[]{:S(2)}) copy-start(f32[128]{0:T(128)S(1)} %fusion.260) | copy-start | bytes 1540
  426.9 85.1 %copy-start.81 = (s32[32,4]{1,0:T(8,128)}, s32[32,4]{1,0:T(8,128)S(1)}, u32[]{:S(2)}) copy-start(s32[32,4]{1,0:T(8,128)S(1)} %get-tuple-element.401) | copy-start | bytes 1540
  430.4 140.1 %copy-start.83 = (s32[4096]{0:T(1024)}, s32[4096]{0:T(1024)S(1)}, u32[]{:S(2)}) copy-start(s32[4096]{0:T(1024)S(1)} %fusion.243) | copy-start | bytes 49156
  581.3 112.1 %copy-start.20 = (f32[128,1024]{1,0:T(8,128)S(1)}, f32[128,1024]{1,0:T(8,128)}, u32[]{:S(2)}) copy-start(f32[128,1024]{1,0:T(8,128)} %get-tuple-element.451) | copy-start | bytes 1572868
  695.9 12.2 copy-start.33
  787.7 12.5 copy-start.149
  831.6 10.5 copy-start.123
  843.0 48.9 %copy-start.163 = (bf16[1004,1024]{1,0:T(8,128)(2,1)S(1)}, bf16[1004,1024]{1,0:T(8,128)(2,1)}, u32[]{:S(2)}) copy-start(bf16[1004,1024]{1,0:T(8,128)(2,1)} %get-tuple-element.735) | copy-start | bytes 6168580
  892.0 14.9 %copy-start.84 = (s32[4096]{0:T(1024)S(1)}, s32[4096]{0:T(1024)}, u32[]{:S(2)}) copy-start(s32[4096]{0:T(1024)} %copy-done.83) | copy-start | bytes 49156
  915.0 21.8 %copy-start.82 = (s32[32,4]{1,0:T(8,128)S(1)}, s32[32,4]{1,0:T(8,128)}, u32[]{:S(2)}) copy-start(s32[32,4]{1,0:T(8,128)} %copy-done.81) | copy-start | bytes 1540
  915.7 21.5 %copy-start.120 = (s32[32,4]{0,1:T(4,128)S(1)}, s32[32,4]{0,1:T(4,128)}, u32[]{:S(2)}) copy-start(s32[32,4]{0,1:T(4,128)} %copy.454) | copy-start | bytes 1540
  915.7 21.5 %copy-start.128 = (s32[32,4]{0,1:T(4,128)S(1)}, s32[32,4]{0,1:T(4,128)}, u32[]{:S(2)}) copy-start(s32[32,4]{0,1:T(4,128)} %copy.455) | copy-start | bytes 1540
  915.7 21.5 %copy-start.106 = (f32[32,4,2]{0,1,2:T(4,128)S(1)}, f32[32,4,2]{0,1,2:T(4,128)}, u32[]{:S(2)}) copy-start(f32[32,4,2]{0,1,2:T(4,128)} %multiply_reduce_fusion.26) | copy-start | bytes 3076
  915.7 21.5 %copy-start.110 = (s32[32,4]{0,1:T(4,128)S(1)}, s32[32,4]{0,1:T(4,128)}, u32[]{:S(2)}) copy-start(s32[32,4]{0,1:T(4,128)} %copy-done.109) | copy-start | bytes 1540
  915.7 21.6 %copy-start.153 = (f32[32,2]{0,1:T(2,128)S(1)}, f32[32,2]{0,1:T(2,128)}, u32[]{:S(2)}) copy-start(f32[32,2]{0,1:T(2,128)} %select_reduce_fusion.9) | copy-start | bytes 772
  915.7 23.1 %copy-start.138 = (s32[4]{0:T(128)S(1)}, s32[4]{0:T(128)}, u32[]{:S(2)}) copy-start(s32[4]{0:T(128)} %copy-done.136) | copy-start | bytes 52
  954.7 14.5 %slice-start.8 = ((s8[8388608]{0:T(1024)(128)(4,1)}), s8[4194304]{0:T(1024)(128)(4,1)S(1)}, s32[]{:S(2)}) async-start(s8[8388608]{0:T(1024)(128)(4,1)} %bitcast.310), calls=%async_computation.15 | async-start | bytes 8388608
  975.8 8.8 slice-start
  1004.6 8.1 copy-start.19
  1004.7 8.1 copy-start.21
  1004.7 8.1 copy-start.22
  1035.9 256.6 %all-to-all-start.3 = ((bf16[32,24,1024]{2,1,0:T(8,128)(2,1)}), bf16[32,24,1024]{2,1,0:T(8,128)(2,1)}, u32[]{:S(2)}, u32[]{:S(2)}) async-start(bf16[32,24,1024]{2,1,0:T(8,128)(2,1)} %bitcast.262), calls=%async_computation.3 | async-start | bytes 3145728 | tf_op jit(solution)/shard_map/all_to_all | solution.py:811
  1046.3 242.1 %copy-start.157 = (f32[2]{0:T(128)S(1)}, f32[2]{0:T(128)}, u32[]{:S(2)}) copy-start(f32[2]{0:T(128)} %copy-done.156) | copy-start | bytes 28
  1292.6 26.5 %copy-start.89 = (f32[7,1024]{1,0:T(8,128)S(1)}, f32[7,1024]{1,0:T(8,128)}, u32[]{:S(2)}) copy-start(f32[7,1024]{1,0:T(8,128)} %param.32) | copy-start | bytes 86020
  1292.6 26.5 %copy-start.107 = (f32[7,1024]{1,0:T(8,128)S(1)}, f32[7,1024]{1,0:T(8,128)}, u32[]{:S(2)}) copy-start(f32[7,1024]{1,0:T(8,128)} %param.38) | copy-start | bytes 86020
  1292.6 26.5 %copy-start.108 = (f32[7,1024]{1,0:T(8,128)S(1)}, f32[7,1024]{1,0:T(8,128)}, u32[]{:S(2)}) copy-start(f32[7,1024]{1,0:T(8,128)} %param.35) | copy-start | bytes 86020
  (136 other events, 491.4 us)
Sparse Core Ops, SparseCore 0:
  155.0 232.2 all-gather.11
  390.2 208.2 all-gather.15
  601.4 203.1 all-gather.13

commit v4 on v3

--- a/solution.py
+++ b/solution.py
@@ -293,7 +293,7 @@
 def lane_widths(width):
     if width % D == 0:
         return (3 * width // 8, 3 * width // 8, width // 8, width // 8)
-    return (width // 4,) * 4
+    return (width // 4,) * 4 if width % 512 == 0 else (width,)
 
 
 def bit_of(bit):
@@ -477,8 +477,8 @@
 def scatter_kernel(bits, plan, *refs):
     n_waves, slots, wide, widths = (plan["waves"], plan["slots"], plan["wide"], plan["widths"])
     n_ins, n_loaded = (plan["operands"], len(plan["loads"]))
-    ins, out_ref = (refs[:n_ins], refs[n_ins])
-    loaded, rest_refs = (refs[n_ins + 1 : n_ins + 1 + n_loaded], refs[n_ins + 1 + n_loaded :])
+    ins, out_ref, squares_ref = (refs[:n_ins], refs[n_ins], refs[n_ins + 1])
+    loaded, rest_refs = (refs[n_ins + 2 : n_ins + 2 + n_loaded], refs[n_ins + 2 + n_loaded :])
     buffers = [rest_refs[6 * lane : 6 * lane + 6] for lane in range(len(widths))]
     load_sem, send_sem, recv_sem, free_sem = rest_refs[6 * len(widths) :]
     depth = len(bits)
@@ -563,6 +563,10 @@
                     if step == depth:
                         start = plan["column"](wave) + low
                         out_ref[:, pl.ds(pl.multiple_of(start, 128), width)] = value
+                        squares = value * value
+                        squares_ref[...] += sum(
+                            squares[:, at : at + 128] for at in range(0, width, 128)
+                        )
                     else:
                         keep(here, value, step)
 
@@ -609,6 +613,7 @@
 
         return carry
 
+    squares_ref[...] = jnp.zeros_like(squares_ref)
     greet(bits)
     lax.fori_loop(0, n_waves + depth, turn_of, 0)
     for step in range(depth):
@@ -632,9 +637,12 @@
     marks = (len(widths), slots, len(bits))
     return pl.pallas_call(
         functools.partial(scatter_kernel, bits, plan),
-        out_shape=jax.ShapeDtypeStruct((rows, plan["waves"] * sum(widths)), jnp.float32),
+        out_shape=[
+            jax.ShapeDtypeStruct((rows, plan["waves"] * sum(widths)), jnp.float32),
+            jax.ShapeDtypeStruct((rows, 128), jnp.float32),
+        ],
         in_specs=[pl.BlockSpec(memory_space=pl.ANY)] * len(operands),
-        out_specs=pl.BlockSpec(memory_space=pltpu.VMEM),
+        out_specs=[pl.BlockSpec(memory_space=pltpu.VMEM)] * 2,
         scratch_shapes=scratch
         + [
             pltpu.SemaphoreType.DMA((len(operands),)),
@@ -764,7 +772,7 @@
             "produce": functools.partial(final_products, step, rows),
             "column": lambda wave: wave * step,
         }
-        sums.append(tree_scatter([some, table], plan, collective_id + turn, 60))
+        sums.append(tree_scatter([some, table], plan, collective_id + turn, 60)[0])
     return jnp.concatenate(sums, axis=0)
 
 
@@ -910,22 +918,65 @@
     return feed_forward(residual, gain_row, *weights)
 
 
-def shard_stats(final_rows, table_shard, targets, collective_ids):
-    all_rows = gather_whole(final_rows, D, collective_ids[0], 45, final_rows.shape[0] // 4)
-    all_rows = all_rows.reshape(-1, D)
+STAT_ROWS = 512
+
+
+def stats_kernel(rows_ref, table_ref, targets_ref, stats_ref):
+    logits = lax.dot_general(
+        table_ref[...], rows_ref[...], (((1,), (1,)), ((), ())), preferred_element_type=jnp.float32
+    )
+    largest = jnp.max(logits, axis=0, keepdims=True)
+    total = jnp.sum(jnp.exp(logits - largest), axis=0, keepdims=True)
+    hot = lax.broadcasted_iota(jnp.int32, logits.shape, 0) == targets_ref[...]
+    picked = jnp.sum(jnp.where(hot, logits, 0.0), axis=0, keepdims=True)
+    stats_ref[...] = jnp.concatenate([largest, total, picked], axis=0)
+
+
+def stats_alone(all_rows, table_shard, targets_here):
+    tokens, vocab = (all_rows.shape[0], table_shard.shape[0])
+    return pl.pallas_call(
+        stats_kernel,
+        grid=(tokens // STAT_ROWS,),
+        out_shape=jax.ShapeDtypeStruct((3, tokens), jnp.float32),
+        in_specs=[
+            pl.BlockSpec((STAT_ROWS, D), lambda step: (step, 0)),
+            pl.BlockSpec((vocab, D), lambda step: (0, 0)),
+            pl.BlockSpec((1, STAT_ROWS), lambda step: (0, step)),
+        ],
+        out_specs=pl.BlockSpec((3, STAT_ROWS), lambda step: (0, step)),
+        compiler_params=pltpu.CompilerParams(vmem_limit_bytes=40 * 2**20),
+        cost_estimate=pl.CostEstimate(
+            flops=2 * tokens * vocab * D,
+            bytes_accessed=2 * (tokens + vocab) * D,
+            transcendentals=tokens * vocab,
+        ),
+    )(all_rows, table_shard, targets_here[None])
+
+
+def gather_rows(final_rows, collective_id):
+    rows = gather_whole(final_rows, D, collective_id, 45, final_rows.shape[0] // 4)
+    return rows.reshape(-1, D)
+
+
+def combine_stats(stats, collective_id):
+    tokens = stats.shape[1]
+    stats = stats.reshape(8, -1)
+    stats = gather_whole(stats, stats.shape[1], collective_id, 20).reshape(-1, 3, tokens)
+    peak = jnp.max(stats[:, 0], axis=0)
+    log_own = peak + jnp.log(jnp.sum(stats[:, 1] * jnp.exp(stats[:, 0] - peak), axis=0))
+    return (jnp.sum(stats[:, 2], axis=0) - log_own, log_own)
+
+
+def shard_stats(final_rows, table_shard, targets_here, collective_ids):
+    all_rows = gather_rows(final_rows, collective_ids[0])
     logits = jnp.einsum("rd,vd->rv", all_rows, table_shard, preferred_element_type=jnp.float32)
     logits = with_layout_constraint(logits, Layout(major_to_minor=(0, 1)))
-    low = lax.axis_index(AXES) * table_shard.shape[0]
-    hot = (targets - low)[:, None] == jnp.arange(table_shard.shape[0])[None, :]
+    hot = targets_here[:, None] == jnp.arange(table_shard.shape[0])[None, :]
     largest = jnp.max(logits, axis=1)
     total = jnp.sum(jnp.exp(logits - largest[:, None]), axis=1)
     picked = jnp.sum(jnp.where(hot, logits, 0.0), axis=1)
-    stats = jnp.concatenate([part.reshape(8, -1) for part in (largest, total, picked)], axis=0)
-    stats = gather_whole(stats, stats.shape[1], collective_ids[1], 20)
-    peak = jnp.max(stats[:, :8], axis=0)
-    log_own = peak + jnp.log(jnp.sum(stats[:, 8:16] * jnp.exp(stats[:, :8] - peak), axis=0))
-    token_logp = (jnp.sum(stats[:, 16:], axis=0) - log_own).reshape(-1)
-    return (token_logp, log_own.reshape(-1), logits, hot, all_rows)
+    token_logp, log_own = combine_stats(jnp.stack([largest, total, picked]), collective_ids[1])
+    return (token_logp, log_own, logits, hot, all_rows)
 
 
 def forward(token_rows, enc_full, dec_full_after, gain_rows, batch_data, streamed=False):
@@ -1152,7 +1203,7 @@
         cuts.append(notes[:, at : at + width])
         at += width
     targets, all_lengths, all_pair, all_flag, all_micro, all_rounds = cuts
-    targets = targets.reshape(-1)
+    targets_here = targets.reshape(-1) - me * rows_here
     rounds = jnp.max(all_rounds)
     all_select = (all_pair[:, :, None] == jnp.arange(pairs_here)).astype(jnp.float32)
     pair_micro = (all_micro[:, :, None] == jnp.arange(MICRO)).astype(jnp.float32)
@@ -1192,7 +1243,7 @@
         return split_blocks(after(frozen_dec, memory), DEC_BLOCKS)
 
     token_logp, log_own, logits, hot, all_rows = shard_stats(
-        policy_rows, policy_table, targets, (3, 4)
+        policy_rows, policy_table, targets_here, (3, 4)
     )
     policy_logp = logp_of(token_logp)
     row_slope = jnp.where(
@@ -1207,7 +1258,8 @@
     frozen_rows, unused = forward(
         frozen_inputs, frozen_layer_enc, frozen_after, frozen_gains, batch_data, True
     )
-    frozen_logp = logp_of(shard_stats(frozen_rows, frozen_embed, targets, (5, 6))[0])
+    frozen_stats = stats_alone(gather_rows(frozen_rows, 5), frozen_embed, targets_here)
+    frozen_logp = logp_of(combine_stats(frozen_stats, 6)[0])
     frozen_mean = lax.dynamic_index_in_dim(
         frozen_logp / all_lengths.astype(jnp.float32), me, 0, keepdims=False
     )
@@ -1262,8 +1314,8 @@
     table_grad = after(table_grad, first_sums)
     enc_pairs[0] = (after(enc_pairs[0][0], first_sums, table_grad), enc_pairs[0][1])
     embed_grad = return_rows(plan, asked, rounds, first_sums, token_gradient, table_grad, n_dev)
-    layer_grad = scatter_layers(scaled_pairs, enc_pairs, policy_layers.shape[0], 8)
-    squares_local = jnp.sum(embed_grad * embed_grad) + jnp.sum(layer_grad * layer_grad)
+    layer_grad, layer_squares = scatter_layers(scaled_pairs, enc_pairs, policy_layers.shape[0], 8)
+    squares_local = jnp.sum(embed_grad * embed_grad) + jnp.sum(layer_squares)
     shared = total_of(jnp.concatenate([gain_grads, jnp.full((1, D), squares_local)], axis=0), 9)
     gain_total, squares_total = (shared[:7], shared[7, 0])
     grad_norm = jnp.sqrt(squares_total + jnp.sum(gain_total * gain_total))

time: 1360 us -> 1380 us (1.015)
  local copies, waits for them, and re-layouts: 107 us -> 133 us
  Pallas kernels: 698 us -> 716 us
  matrix products: 227 us -> 212 us
    dot_general x2 -> x1, matrix products: 30.3 us -> 12.7 us  [shard_stats(): jnp.einsum('rd,vd->rv', all_rows, table_shard, preferred_element_type=jnp...]
    pallas_call x2 -> x3, Pallas kernels: 354 us -> 369 us  [the longest x2 354 us: tree_scatter(): pl.pallas_call(functools.partial(scatter_kernel, bits, plan), out_shape=[...]
where the time goes in v4:
time: 1380 us; the launch traced here: 1370 us
  Pallas kernels  716 us (52%)
  matrix products  212 us (15%)
  waiting for transfers between devices  160 us (12%)
  local copies, waits for them, and re-layouts  133 us (10%)
  other arithmetic  111 us (8%)
  between operations  25.5 us (2%)
    pallas_call x2, Pallas kernels, tree_scatter(): pl.pallas_call(functools.partial(scatter_kernel, bits, plan), out_shape=[...  354 us
    pallas_call x5, Pallas kernels, tree_gather(): pl.pallas_call(functools.partial(gather_kernel, bits, len(operands), wave...  310 us
    all_to_all x2, waiting for transfers between devices, swap(): lax.all_to_all(rows.reshape(n_dev, SLOTS, wide), AXES, 0, 0, tiled=True)  124 us
    dot_general x22, matrix products, matmul(): return jnp.dot(left_side, right_side, preferred_element_type=jnp.float32)  82.7 us
    dot_general x9, matrix products, matmul_back(): jnp.einsum('re,de->rd', grad_low, weight, preferred_element_type=jnp.floa...  38.9 us
    all_gather x3, waiting for transfers between devices, gather_offloaded(): return lax.all_gather(part, AXES, axis=0, tiled=True)  35.4 us
    convert_element_type x17, other arithmetic, to_low(): return values.astype(jnp.bfloat16)  31.1 us
  transfers between devices with their start and end apart: 5, of which 2 were waited for; matrix products, arithmetic and copies ran while one was open for 18% of the time, Pallas kernels for 35%

profile of v4, /device:TPU:0, one launch (start us, length us, event | category | flops | bytes accessed | tf_op | source)
XLA Modules:
  0.0 1370.4 jit_solution(17930946152564759534)
XLA Ops:
  21.0 130.0 %shard_map.282 = (bf16[2,2,2,2,2,32,3072]{6,5,4,3,2,1,0:T(8,128)(2,1)}, bf16[2,2,2,2,2,32,1024]{6,5,4,3,2,1,0:T(8,128)(2,1)}, bf16[2,2,2,2,2,32,2048]{6,5,4,3,2,...) custom-call(bf16[1,1,1,1,1,32,28672]{6,5,4,3,2,1,0:T(8,128)(2,1)} %c, ...), custom_call_target="tpu_custom_call" | custom-call | bytes 391000000 | tf_op jit(solution)/shard_map/pallas_call | solution.py:385
  154.6 3.8 convert_element_type.355.refs_1_
  158.4 3.6 fusion.105
  165.8 6.1 all-to-all-start.2
  173.0 124.4 %all-to-all-done.2 = bf16[32,24,2048]{2,1,0:T(8,128)(2,1)S(1)} async-done(((bf16[32,24,2048]{2,1,0:T(8,128)(2,1)}), bf16[32,24,2048]{2,1,0:T(8,128)(2,1)S(1)}, u32[]{:S(2)}, u32[]{:S(2)}) %all-to-all-start.2) | async-done | bytes 3145760 | tf_op jit(solution)/shard_map/all_to_all | solution.py:819
  305.5 6.0 convolution_convert_fusion.1
  326.2 8.1 maximum_convert_fusion.refs_21_
  334.4 3.5 multiply_reduce_fusion.10
  341.3 4.1 convolution_convert_fusion.2
  351.3 35.4 %all-gather.12.cloned.1.call-done = bf16[1024,14336]{1,0:T(8,128)(2,1)} async-done(((bf16[32,14336]{1,0:T(8,128)(2,1)}), bf16[1024,14336]{1,0:T(8,128)(2,1)}) %all-gather.12.cloned.1.call-update) | async-done | bytes 29360144 | tf_op jit(solution)/shard_map/all_gather | solution.py:888
  386.7 3.8 fusion.64
  411.9 4.7 fusion.51.refs_11_
  416.7 7.5 multiply_reduce_fusion.21
  432.4 79.0 %shard_map.283 = bf16[2,2,2,2,2,128,1024]{6,5,4,3,2,1,0:T(8,128)(2,1)} custom-call(bf16[1,1,1,1,1,128,1024]{6,5,4,3,2,1,0:T(8,128)(2,1)} %fusion.356.refs_0_), custom_call_target="tpu_custom_call" | custom-call | bytes 153000000 | tf_op jit(solution)/shard_map/pallas_call | solution.py:385
  511.5 12.7 fusion.290
  524.2 4.7 exponential_reduce_fusion
  530.6 34.9 %shard_map.284 = f32[2,2,2,2,2,8,1536]{6,5,4,3,2,1,0:T(8,128)} custom-call(f32[1,1,1,1,1,8,1536]{6,5,4,3,2,1,0:T(8,128)} %reshape_reshape.35.refs_0_), custom_call_target="tpu_custom_call" | custom-call | bytes 68000000 | tf_op jit(solution)/shard_map/pallas_call | solution.py:385
  565.5 3.8 reshape_reshape_reshape.13
  569.4 4.6 fusion.280
  574.7 11.3 select_convert_fusion
  586.0 110.6 %shard_map.285 = (f32[128,1024]{1,0:T(8,128)}, f32[128,128]{1,0:T(8,128)}) custom-call(bf16[2,2,1024,1004]{3,2,1,0:T(8,128)(2,1)} %bitcast.252, bf16[1004,1024]{1,0:T(8,128)(2,1)} %convert_element_type.355.refs_1_), custom_call_target="tpu_custom_call" | custom-call | bytes 204000000 | tf_op jit(solution)/shard_map/pallas_call | solution.py:638
  699.2 4.9 fusion.56
  704.2 7.1 multiply_reduce_fusion.19
  753.3 5.7 fusion.203
  763.3 4.2 convolution_multiply_fusion
  770.4 6.2 fusion.59
  792.5 12.2 shard_map.286
  805.0 4.5 fusion.79
  814.7 3.9 fusion.67
  844.7 10.4 shard_map.287
  856.1 47.4 %shard_map.288 = bf16[2,2,2,2,2,128,1024]{6,5,4,3,2,1,0:T(8,128)(2,1)} custom-call(bf16[1,1,1,1,1,128,1024]{6,5,4,3,2,1,0:T(8,128)(2,1)} %fusion.232.refs_0_), custom_call_target="tpu_custom_call" | custom-call | bytes 153000000 | tf_op jit(solution)/shard_map/pallas_call | solution.py:385
  906.9 15.1 %shard_map.289 = f32[3,4096]{1,0:T(4,128)S(1)} custom-call(bf16[4096,1024]{1,0:T(8,128)(2,1)S(1)} %bitcast.245, bf16[1004,1024]{1,0:T(8,128)(2,1)} %get-tuple-element.745, s32[1,4096]{1,0:T(1,128)S(1)} %bitcast.246), custom_call_target="tpu_custom_call" | custom-call | flops 8422162432 | bytes 10444800 | tf_op jit(solution)/shard_map/pallas_call | solution.py:937
  922.6 19.0 %shard_map.290 = f32[2,2,2,2,2,8,1536]{6,5,4,3,2,1,0:T(8,128)} custom-call(f32[1,1,1,1,1,8,1536]{6,5,4,3,2,1,0:T(8,128)} %reshape_reshape.39.refs_0_), custom_call_target="tpu_custom_call" | custom-call | bytes 68000000 | tf_op jit(solution)/shard_map/pallas_call | solution.py:385
  948.7 6.2 multiply_reduce_fusion
  963.5 3.6 reshape.1023
  969.2 4.9 multiply_reduce_fusion.5
  976.3 7.8 select_convert_fusion.1.refs_20_
  984.2 3.7 multiply_reduce_fusion.6
  994.9 5.8 fusion.136
  1023.7 7.8 fusion.117
  1031.7 4.0 multiply_convert_fusion.13
  1039.1 13.1 fusion.30
  1054.9 3.8 all-to-all-start.3
  1062.9 243.2 %shard_map.291 = (f32[32,28672]{1,0:T(8,128)}, f32[32,128]{1,0:T(8,128)}) custom-call(bf16[128,1024]{1,0:T(8,128)(2,1)} %copy-done.71, bf16[128,1024]{1,0:T(8,128)(2,1)} %copy-done.69, bf16[128,1024]{1,0:T(8,128)(2,1)} %copy-done.72, bf16[128,1024]{1,0:T(8,128)(2,1)} %copy-done.70, bf16[128,1024]{1,0:T(8,128)(2,1)} %copy-done.73, ...), custom_call_target="tpu_custom_call" | custom-call | bytes 714000000 | tf_op jit(solution)/shard_map/pallas_call | solution.py:638
  1309.3 7.2 multiply_reduce_fusion.3
  1318.5 14.2 %shard_map.292 = f32[8,1024]{1,0:T(8,128)} custom-call(f32[8,1024]{1,0:T(8,128)} %concatenate.131.x_ref), custom_call_target="tpu_custom_call" | custom-call | bytes 40800000 | tf_op jit(solution)/shard_map/pallas_call | solution.py:461
  1338.1 10.4 add_multiply_fusion.2
  1348.5 12.6 add_multiply_fusion
  (615 shorter events, 253.4 us)
Async XLA Ops:
  7.2 379.6 %all-gather.12.cloned.1.call-start = ((), (), s32[]{:S(2)}) async-start(), calls=%async_computation.4 | async-start | bytes 30277632 | tf_op jit(solution)/shard_map/all_gather | solution.py:888
  12.4 287.0 %copy-start.121 = (s32[512]{0:T(512)}, s32[512]{0:T(512)S(1)}, u32[]{:S(2)}) copy-start(s32[512]{0:T(512)S(1)} %get-tuple-element.433) | copy-start | bytes 6148
  16.2 324.8 %copy-start.128 = (s32[4]{0:T(128)}, s32[4]{0:T(128)S(1)}, u32[]{:S(2)}) copy-start(s32[4]{0:T(128)S(1)} %get-tuple-element.379) | copy-start | bytes 52
  16.2 332.4 %copy-start.126 = (pred[4]{0:T(512)(128)(4,1)}, pred[4]{0:T(512)(128)(4,1)S(1)}, u32[]{:S(2)}) copy-start(pred[4]{0:T(512)(128)(4,1)S(1)} %get-tuple-element.378) | copy-start | bytes 16
  154.4 17.8 %copy-start.77 = (s32[4,8,8,128]{3,1,2,0:T(8,128)}, s32[4,8,8,128]{3,1,2,0:T(8,128)S(1)}, u32[]{:S(2)}) copy-start(s32[4,8,8,128]{3,1,2,0:T(8,128)S(1)} %copy.418) | copy-start | bytes 393220
  165.8 131.6 %all-to-all-start.2 = ((bf16[32,24,2048]{2,1,0:T(8,128)(2,1)}), bf16[32,24,2048]{2,1,0:T(8,128)(2,1)S(1)}, u32[]{:S(2)}, u32[]{:S(2)}) async-start(bf16[32,24,2048]{2,1,0:T(8,128)(2,1)} %bitcast.7), calls=%async_computation.2 | async-start | bytes 6291456 | tf_op jit(solution)/shard_map/all_to_all | solution.py:819
  171.9 598.5 %all-gather.16.cloned.1.call-start = ((), (), s32[]{:S(2)}) async-start(), calls=%async_computation.6 | async-start | bytes 30277632 | tf_op jit(solution)/shard_map/all_gather | solution.py:888
  172.9 131.1 %copy-start.100 = (f32[1,1024]{1,0:T(1,128)}, f32[1,1024]{1,0:T(1,128)S(1)}, u32[]{:S(2)}) copy-start(f32[1,1024]{1,0:T(1,128)S(1)} %get-tuple-element.428) | copy-start | bytes 12292
  172.9 153.1 %copy-start.102 = (f32[1,1024]{1,0:T(1,128)}, f32[1,1024]{1,0:T(1,128)S(1)}, u32[]{:S(2)}) copy-start(f32[1,1024]{1,0:T(1,128)S(1)} %get-tuple-element.427) | copy-start | bytes 12292
  172.9 165.1 %copy-start.98 = (f32[1,1024]{1,0:T(1,128)}, f32[1,1024]{1,0:T(1,128)S(1)}, u32[]{:S(2)}) copy-start(f32[1,1024]{1,0:T(1,128)S(1)} %get-tuple-element.426) | copy-start | bytes 12292
  302.6 8.8 copy-start.80
  302.6 8.8 copy-start.84
  302.6 8.8 copy-start.89
  302.6 8.8 copy-start.94
  302.6 8.8 copy-start.96
  323.0 11.4 slice-start.10
  326.0 8.4 copy-start.116
  326.0 8.4 copy-start.9
  326.0 8.4 copy-start.119
  326.2 8.1 copy-start.49
  326.2 8.2 slice-start.11
  340.9 473.8 %all-gather.14.cloned.1.call-start = ((), (), s32[]{:S(2)}) async-start(), calls=%async_computation.5 | async-start | bytes 30277632 | tf_op jit(solution)/shard_map/all_gather | solution.py:888
  341.2 60.4 %copy-start.145 = (pred[4,192]{1,0:T(4,128)(4,1)}, pred[4,192]{1,0:T(4,128)(4,1)S(1)}, u32[]{:S(2)}) copy-start(pred[4,192]{1,0:T(4,128)(4,1)S(1)} %convolution_compare_fusion) | copy-start | bytes 2308
  348.5 38.2 %copy-start.71 = (bf16[128,1024]{1,0:T(8,128)(2,1)}, bf16[128,1024]{1,0:T(8,128)(2,1)S(1)}, u32[]{:S(2)}) copy-start(bf16[128,1024]{1,0:T(8,128)(2,1)S(1)} %fusion.193.refs_0_) | copy-start | bytes 786436
  424.2 273.8 %copy-start.130 = (f32[128]{0:T(128)}, f32[128]{0:T(128)S(1)}, u32[]{:S(2)}) copy-start(f32[128]{0:T(128)S(1)} %fusion.263) | copy-start | bytes 1540
  428.6 82.8 %copy-start.147 = (f32[2]{0:T(128)}, f32[2]{0:T(128)S(1)}, u32[]{:S(2)}) copy-start(f32[2]{0:T(128)S(1)} %fusion.270) | copy-start | bytes 28
  586.0 110.6 %copy-start.21 = (f32[128,1024]{1,0:T(8,128)S(1)}, f32[128,1024]{1,0:T(8,128)}, u32[]{:S(2)}) copy-start(f32[128,1024]{1,0:T(8,128)} %get-tuple-element.463) | copy-start | bytes 1572868
  699.2 12.2 copy-start.34
  792.5 12.4 copy-start.140
  969.2 14.9 %slice-start.8 = ((s8[8388608]{0:T(1024)(128)(4,1)}), s8[4194304]{0:T(1024)(128)(4,1)S(1)}, s32[]{:S(2)}) async-start(s8[8388608]{0:T(1024)(128)(4,1)} %bitcast.331), calls=%async_computation.15 | async-start | bytes 8388608
  976.3 7.9 copy-start.120
  976.3 7.9 slice-start.9
  990.7 9.9 slice-start
  1023.6 7.9 copy-start.40
  1023.6 7.9 copy-start.115
  1023.6 8.1 copy-start.20
  1023.6 8.1 copy-start.22
  1023.6 8.1 copy-start.26
  1023.6 8.0 copy-start.28
  1023.6 8.0 copy-start.131
  1023.6 8.0 copy-start.134
  1023.7 8.0 copy-start.137
  1054.9 254.4 %all-to-all-start.3 = ((bf16[32,24,1024]{2,1,0:T(8,128)(2,1)}), bf16[32,24,1024]{2,1,0:T(8,128)(2,1)}, u32[]{:S(2)}, u32[]{:S(2)}) async-start(bf16[32,24,1024]{2,1,0:T(8,128)(2,1)} %bitcast.280), calls=%async_computation.3 | async-start | bytes 3145728 | tf_op jit(solution)/shard_map/all_to_all | solution.py:819
  1062.9 245.9 %copy-start.148 = (f32[2]{0:T(128)S(1)}, f32[2]{0:T(128)}, u32[]{:S(2)}) copy-start(f32[2]{0:T(128)} %copy-done.147) | copy-start | bytes 28
  1062.9 246.4 %copy-start.143 = (s32[768]{0:T(1024)S(1)}, s32[768]{0:T(1024)}, u32[]{:S(2)}) copy-start(s32[768]{0:T(1024)} %copy-done.142) | copy-start | bytes 9220
  1309.3 27.4 %copy-start.93 = (f32[7,1024]{1,0:T(8,128)S(1)}, f32[7,1024]{1,0:T(8,128)}, u32[]{:S(2)}) copy-start(f32[7,1024]{1,0:T(8,128)} %param.32) | copy-start | bytes 86020
  1309.3 27.4 %copy-start.105 = (f32[7,1024]{1,0:T(8,128)S(1)}, f32[7,1024]{1,0:T(8,128)}, u32[]{:S(2)}) copy-start(f32[7,1024]{1,0:T(8,128)} %param.38) | copy-start | bytes 86020
  1309.3 27.4 %copy-start.106 = (f32[7,1024]{1,0:T(8,128)S(1)}, f32[7,1024]{1,0:T(8,128)}, u32[]{:S(2)}) copy-start(f32[7,1024]{1,0:T(8,128)} %param.35) | copy-start | bytes 86020
  (124 other events, 411.7 us)
Sparse Core Ops, SparseCore 0:
  154.5 232.2 all-gather.11
  389.7 208.5 all-gather.15
  601.2 207.5 all-gather.13

commit v5 on v3

--- a/solution.py
+++ b/solution.py
@@ -758,7 +758,7 @@
             "widths": (step // 2, step // 2),
             "orders": scatter_orders()[:2],
             "rows": rows,
-            "wide": (len(bits) - 2, len(bits) - 1),
+            "wide": (),
             "loads": [(some.shape, [(0, ())]), (table.shape, [(1, ())])],
             "waits": ((0, (0, 2)),),
             "produce": functools.partial(final_products, step, rows),

time: 1360 us -> 1350 us (level)
  Pallas kernels: 698 us -> 665 us
  waiting for transfers between devices: 159 us -> 178 us
    pallas_call x2, Pallas kernels: 354 us -> 321 us  [tree_scatter(): pl.pallas_call(functools.partial(scatter_kernel, bits, plan), out_shape=j...]
    all_gather x3, waiting for transfers between devices: 35.4 us -> 54.5 us  [gather_offloaded(): return lax.all_gather(part, AXES, axis=0, tiled=True)]
  transfers between devices with their start and end apart: 5 -> 5, of which waited for: 2 -> 3; matrix products, arithmetic and copies ran while one was open for 18% -> 19% of each run, Pallas kernels for 35% -> 33%
where the time goes in v5:
time: 1350 us; the launch traced here: 1340 us
  Pallas kernels  665 us (49%)
  matrix products  227 us (17%)
  waiting for transfers between devices  178 us (13%)
  other arithmetic  124 us (9%)
  local copies, waits for them, and re-layouts  107 us (8%)
  between operations  25.6 us (2%)
    pallas_call x2, Pallas kernels, tree_scatter(): pl.pallas_call(functools.partial(scatter_kernel, bits, plan), out_shape=j...  321 us
    pallas_call x5, Pallas kernels, tree_gather(): pl.pallas_call(functools.partial(gather_kernel, bits, len(operands), wave...  309 us
    all_to_all x2, waiting for transfers between devices, swap(): lax.all_to_all(rows.reshape(n_dev, SLOTS, wide), AXES, 0, 0, tiled=True)  124 us
    dot_general x22, matrix products, matmul(): return jnp.dot(left_side, right_side, preferred_element_type=jnp.float32)  81.1 us
    all_gather x3, waiting for transfers between devices, gather_offloaded(): return lax.all_gather(part, AXES, axis=0, tiled=True)  54.5 us
    dot_general x9, matrix products, matmul_back(): jnp.einsum('re,de->rd', grad_low, weight, preferred_element_type=jnp.floa...  38.9 us
    convert_element_type x17, other arithmetic, to_low(): return values.astype(jnp.bfloat16)  30.8 us
    dot_general x2, matrix products, shard_stats(): jnp.einsum('rd,vd->rv', all_rows, table_shard, preferred_element_type=jnp...  30.3 us
  transfers between devices with their start and end apart: 5, of which 3 were waited for; matrix products, arithmetic and copies ran while one was open for 19% of the time, Pallas kernels for 33%

profile of v5, /device:TPU:0, one launch (start us, length us, event | category | flops | bytes accessed | tf_op | source)
XLA Modules:
  0.0 1339.2 jit_solution(11445334104052992502)
XLA Ops:
  21.5 130.0 %shard_map.282 = (bf16[2,2,2,2,2,32,3072]{6,5,4,3,2,1,0:T(8,128)(2,1)}, bf16[2,2,2,2,2,32,1024]{6,5,4,3,2,1,0:T(8,128)(2,1)}, bf16[2,2,2,2,2,32,2048]{6,5,4,3,2,...) custom-call(bf16[1,1,1,1,1,32,28672]{6,5,4,3,2,1,0:T(8,128)(2,1)} %c, ...), custom_call_target="tpu_custom_call" | custom-call | bytes 391000000 | tf_op jit(solution)/shard_map/pallas_call | solution.py:385
  155.1 3.8 convert_element_type.355.refs_1_
  158.9 3.6 fusion.105
  166.3 6.1 all-to-all-start.2
  174.0 123.9 %all-to-all-done.2 = bf16[32,24,2048]{2,1,0:T(8,128)(2,1)S(1)} async-done(((bf16[32,24,2048]{2,1,0:T(8,128)(2,1)}), bf16[32,24,2048]{2,1,0:T(8,128)(2,1)S(1)}, u32[]{:S(2)}, u32[]{:S(2)}) %all-to-all-start.2) | async-done | bytes 3145760 | tf_op jit(solution)/shard_map/all_to_all | solution.py:811
  306.0 5.9 convolution_convert_fusion.1
  326.7 8.1 maximum_convert_fusion.refs_21_
  334.9 3.5 multiply_reduce_fusion.11
  341.7 4.1 convolution_convert_fusion.2
  351.8 35.4 %all-gather.12.cloned.1.call-done = bf16[1024,14336]{1,0:T(8,128)(2,1)} async-done(((bf16[32,14336]{1,0:T(8,128)(2,1)}), bf16[1024,14336]{1,0:T(8,128)(2,1)}) %all-gather.12.cloned.1.call-update) | async-done | bytes 29360144 | tf_op jit(solution)/shard_map/all_gather | solution.py:880
  387.2 3.8 fusion.64
  412.4 4.7 fusion.51.refs_11_
  417.2 7.4 multiply_reduce_fusion.22
  432.9 79.1 %shard_map.283 = bf16[2,2,2,2,2,128,1024]{6,5,4,3,2,1,0:T(8,128)(2,1)} custom-call(bf16[1,1,1,1,1,128,1024]{6,5,4,3,2,1,0:T(8,128)(2,1)} %fusion.352.refs_0_), custom_call_target="tpu_custom_call" | custom-call | bytes 153000000 | tf_op jit(solution)/shard_map/pallas_call | solution.py:385
  512.0 15.4 %fusion.284 = (f32[4096]{0:T(1024)S(1)}, f32[4096,1004]{1,0:T(8,128)}) fusion(bf16[4096,1024]{1,0:T(8,128)(2,1)} %bitcast.242, bf16[1004,1024]{1,0:T(8,128)(2,1)} %convert_element_type.355.refs_1_), kind=kOutput, calls=%fused_computation.475 | convolution fusion | flops 8426270720 | bytes 26910720 | tf_op jit(solution)/shard_map/rd,vd->rv/dot_general | solution.py:916
  527.4 8.3 exponential_reduce_fusion.1
  536.3 31.0 %shard_map.284 = f32[2,2,2,2,2,24,512]{6,5,4,3,2,1,0:T(8,128)} custom-call(f32[1,1,1,1,1,24,512]{6,5,4,3,2,1,0:T(8,128)} %maximum_bitcast_fusion.refs_0_), custom_call_target="tpu_custom_call" | custom-call | bytes 68000000 | tf_op jit(solution)/shard_map/pallas_call | solution.py:385
  570.5 10.8 select_convert_fusion
  581.3 78.3 %shard_map.285 = f32[128,1024]{1,0:T(8,128)} custom-call(bf16[2,2,1024,1004]{3,2,1,0:T(8,128)(2,1)} %bitcast.229, bf16[1004,1024]{1,0:T(8,128)(2,1)} %convert_element_type.355.refs_1_), custom_call_target="tpu_custom_call" | custom-call | bytes 204000000 | tf_op jit(solution)/shard_map/pallas_call | solution.py:633
  662.2 5.0 fusion.56
  667.2 7.1 multiply_reduce_fusion.20
  716.4 5.7 fusion.203
  725.7 4.2 convolution_multiply_fusion
  732.9 5.9 fusion.59
  753.5 12.5 shard_map.286
  766.2 4.0 fusion.79
  775.4 19.1 %all-gather.14.cloned.1.call-done.in_ref.out_ref = bf16[1024,14336]{1,0:T(8,128)(2,1)} async-done(((bf16[32,14336]{1,0:T(8,128)(2,1)}), bf16[1024,14336]{1,0:T(8,128)(2,1)}) %all-gather.14.cloned.1.call-update) | async-done | bytes 29360144 | tf_op jit(solution)/shard_map/all_gather | solution.py:880
  794.5 3.8 fusion.67
  816.8 10.4 shard_map.287
  828.1 49.3 %shard_map.288 = bf16[2,2,2,2,2,128,1024]{6,5,4,3,2,1,0:T(8,128)(2,1)} custom-call(bf16[1,1,1,1,1,128,1024]{6,5,4,3,2,1,0:T(8,128)(2,1)} %fusion.226.refs_0_), custom_call_target="tpu_custom_call" | custom-call | bytes 153000000 | tf_op jit(solution)/shard_map/pallas_call | solution.py:385
  877.4 14.9 %fusion.287 = (f32[4096]{0:T(1024)S(1)}, f32[4096,1004]{1,0:T(8,128)}) fusion(bf16[4096,1024]{1,0:T(8,128)(2,1)} %bitcast.244, bf16[1004,1024]{1,0:T(8,128)(2,1)S(1)} %copy-done.163), kind=kOutput, calls=%fused_computation.478 | convolution fusion | flops 8426270720 | bytes 26910720 | tf_op jit(solution)/shard_map/rd,vd->rv/dot_general | solution.py:916
  892.3 8.2 exponential_reduce_fusion
  901.2 19.4 %shard_map.289 = f32[2,2,2,2,2,24,512]{6,5,4,3,2,1,0:T(8,128)} custom-call(f32[1,1,1,1,1,24,512]{6,5,4,3,2,1,0:T(8,128)} %maximum_bitcast_fusion.1.refs_0_), custom_call_target="tpu_custom_call" | custom-call | bytes 68000000 | tf_op jit(solution)/shard_map/pallas_call | solution.py:385
  925.5 5.9 multiply_reduce_fusion
  941.3 4.9 multiply_reduce_fusion.6
  948.4 7.4 select_convert_fusion.1.refs_20_
  955.8 3.7 multiply_reduce_fusion.7
  965.7 5.5 fusion.136
  991.3 7.8 fusion.117
  999.3 4.0 multiply_convert_fusion.13
  1006.7 13.1 fusion.30
  1022.5 3.8 all-to-all-start.3
  1032.6 242.9 %shard_map.290 = f32[32,28672]{1,0:T(8,128)} custom-call(bf16[128,1024]{1,0:T(8,128)(2,1)} %copy-done.67, bf16[128,1024]{1,0:T(8,128)(2,1)} %copy-done.65, bf16[128,1024]{1,0:T(8,128)(2,1)} %copy-done.68, bf16[128,1024]{1,0:T(8,128)(2,1)} %copy-done.66, bf16[128,1024]{1,0:T(8,128)(2,1)} %copy-done.69, bf16[128,1024]{1,0:T(8,128)(2,1)} %get-tuple-element.429.refs_5_, ...), custom_call_target="tpu_custom_call" | custom-call | bytes 714000000 | tf_op jit(solution)/shard_map/pallas_call | solution.py:633
  1276.1 3.6 multiply_reduce_fusion.4
  1279.7 7.2 multiply_reduce_fusion.3
  1288.9 12.6 shard_map.291
  1306.8 10.4 add_multiply_fusion.2
  1317.3 12.6 add_multiply_fusion
  (643 shorter events, 235.6 us)
Async XLA Ops:
  7.2 380.1 %all-gather.12.cloned.1.call-start = ((), (), s32[]{:S(2)}) async-start(), calls=%async_computation.4 | async-start | bytes 30277632 | tf_op jit(solution)/shard_map/all_gather | solution.py:880
  12.4 287.5 %copy-start.126 = (s32[512]{0:T(512)}, s32[512]{0:T(512)S(1)}, u32[]{:S(2)}) copy-start(s32[512]{0:T(512)S(1)} %get-tuple-element.421) | copy-start | bytes 6148
  154.9 17.8 %copy-start.73 = (s32[4,8,8,128]{3,1,2,0:T(8,128)}, s32[4,8,8,128]{3,1,2,0:T(8,128)S(1)}, u32[]{:S(2)}) copy-start(s32[4,8,8,128]{3,1,2,0:T(8,128)S(1)} %copy.509) | copy-start | bytes 393220
  166.3 131.6 %all-to-all-start.2 = ((bf16[32,24,2048]{2,1,0:T(8,128)(2,1)}), bf16[32,24,2048]{2,1,0:T(8,128)(2,1)S(1)}, u32[]{:S(2)}, u32[]{:S(2)}) async-start(bf16[32,24,2048]{2,1,0:T(8,128)(2,1)} %bitcast.7), calls=%async_computation.2 | async-start | bytes 6291456 | tf_op jit(solution)/shard_map/all_to_all | solution.py:811
  172.4 560.4 %all-gather.16.cloned.1.call-start = ((), (), s32[]{:S(2)}) async-start(), calls=%async_computation.6 | async-start | bytes 30277632 | tf_op jit(solution)/shard_map/all_gather | solution.py:880
  174.0 130.5 %copy-start.97 = (f32[1,1024]{1,0:T(1,128)}, f32[1,1024]{1,0:T(1,128)S(1)}, u32[]{:S(2)}) copy-start(f32[1,1024]{1,0:T(1,128)S(1)} %get-tuple-element.416) | copy-start | bytes 12292
  174.0 152.5 %copy-start.99 = (f32[1,1024]{1,0:T(1,128)}, f32[1,1024]{1,0:T(1,128)S(1)}, u32[]{:S(2)}) copy-start(f32[1,1024]{1,0:T(1,128)S(1)} %get-tuple-element.415) | copy-start | bytes 12292
  303.1 8.8 copy-start.75
  303.1 8.8 copy-start.79
  303.1 8.8 copy-start.85
  303.1 8.8 copy-start.90
  303.1 8.8 copy-start.92
  323.5 11.4 slice-start.10
  326.5 8.4 copy-start.118
  326.5 8.4 copy-start.8
  326.5 8.4 copy-start.121
  326.7 8.1 copy-start.46
  326.7 8.2 slice-start.11
  341.3 453.2 %all-gather.14.cloned.1.call-start = ((), (), s32[]{:S(2)}) async-start(), calls=%async_computation.5 | async-start | bytes 30277632 | tf_op jit(solution)/shard_map/all_gather | solution.py:880
  341.6 60.4 %copy-start.154 = (pred[4,192]{1,0:T(4,128)(4,1)}, pred[4,192]{1,0:T(4,128)(4,1)S(1)}, u32[]{:S(2)}) copy-start(pred[4,192]{1,0:T(4,128)(4,1)S(1)} %convolution_compare_fusion) | copy-start | bytes 2308
  341.7 51.2 %copy-start.124 = (pred[4,32,32]{1,2,0:T(8,128)(4,1)}, pred[4,32,32]{1,2,0:T(8,128)(4,1)S(1)}, u32[]{:S(2)}) copy-start(pred[4,32,32]{1,2,0:T(8,128)(4,1)S(1)} %broadcast_and_fusion) | copy-start | bytes 12292
  349.0 38.2 %copy-start.67 = (bf16[128,1024]{1,0:T(8,128)(2,1)}, bf16[128,1024]{1,0:T(8,128)(2,1)S(1)}, u32[]{:S(2)}) copy-start(bf16[128,1024]{1,0:T(8,128)(2,1)S(1)} %fusion.193.refs_0_) | copy-start | bytes 786436
  424.7 236.3 %copy-start.139 = (f32[128]{0:T(128)}, f32[128]{0:T(128)S(1)}, u32[]{:S(2)}) copy-start(f32[128]{0:T(128)S(1)} %fusion.260) | copy-start | bytes 1540
  426.9 85.1 %copy-start.81 = (s32[32,4]{1,0:T(8,128)}, s32[32,4]{1,0:T(8,128)S(1)}, u32[]{:S(2)}) copy-start(s32[32,4]{1,0:T(8,128)S(1)} %get-tuple-element.401) | copy-start | bytes 1540
  430.4 140.1 %copy-start.83 = (s32[4096]{0:T(1024)}, s32[4096]{0:T(1024)S(1)}, u32[]{:S(2)}) copy-start(s32[4096]{0:T(1024)S(1)} %fusion.243) | copy-start | bytes 49156
  581.3 78.3 %copy-start.20 = (f32[128,1024]{1,0:T(8,128)S(1)}, f32[128,1024]{1,0:T(8,128)}, u32[]{:S(2)}) copy-start(f32[128,1024]{1,0:T(8,128)} %get-tuple-element.451) | copy-start | bytes 1572868
  662.1 12.2 copy-start.33
  753.5 12.7 copy-start.149
  773.8 20.7 %copy-start.148 = (f32[1,1024]{1,0:T(1,128)S(1)}, f32[1,1024]{1,0:T(1,128)}, u32[]{:S(2)}) copy-start(f32[1,1024]{1,0:T(1,128)} %get-tuple-element.409) | copy-start | bytes 12292
  816.7 10.5 copy-start.123
  828.1 49.3 %copy-start.163 = (bf16[1004,1024]{1,0:T(8,128)(2,1)S(1)}, bf16[1004,1024]{1,0:T(8,128)(2,1)}, u32[]{:S(2)}) copy-start(bf16[1004,1024]{1,0:T(8,128)(2,1)} %get-tuple-element.735) | copy-start | bytes 6168580
  877.4 14.9 %copy-start.84 = (s32[4096]{0:T(1024)S(1)}, s32[4096]{0:T(1024)}, u32[]{:S(2)}) copy-start(s32[4096]{0:T(1024)} %copy-done.83) | copy-start | bytes 49156
  900.5 22.8 %copy-start.82 = (s32[32,4]{1,0:T(8,128)S(1)}, s32[32,4]{1,0:T(8,128)}, u32[]{:S(2)}) copy-start(s32[32,4]{1,0:T(8,128)} %copy-done.81) | copy-start | bytes 1540
  901.2 22.6 %copy-start.120 = (s32[32,4]{0,1:T(4,128)S(1)}, s32[32,4]{0,1:T(4,128)}, u32[]{:S(2)}) copy-start(s32[32,4]{0,1:T(4,128)} %copy.454) | copy-start | bytes 1540
  901.2 22.6 %copy-start.128 = (s32[32,4]{0,1:T(4,128)S(1)}, s32[32,4]{0,1:T(4,128)}, u32[]{:S(2)}) copy-start(s32[32,4]{0,1:T(4,128)} %copy.455) | copy-start | bytes 1540
  901.2 22.6 %copy-start.106 = (f32[32,4,2]{0,1,2:T(4,128)S(1)}, f32[32,4,2]{0,1,2:T(4,128)}, u32[]{:S(2)}) copy-start(f32[32,4,2]{0,1,2:T(4,128)} %multiply_reduce_fusion.26) | copy-start | bytes 3076
  901.2 22.6 %copy-start.110 = (s32[32,4]{0,1:T(4,128)S(1)}, s32[32,4]{0,1:T(4,128)}, u32[]{:S(2)}) copy-start(s32[32,4]{0,1:T(4,128)} %copy-done.109) | copy-start | bytes 1540
  901.2 22.7 %copy-start.153 = (f32[32,2]{0,1:T(2,128)S(1)}, f32[32,2]{0,1:T(2,128)}, u32[]{:S(2)}) copy-start(f32[32,2]{0,1:T(2,128)} %select_reduce_fusion.9) | copy-start | bytes 772
  901.2 24.2 %copy-start.138 = (s32[4]{0:T(128)S(1)}, s32[4]{0:T(128)}, u32[]{:S(2)}) copy-start(s32[4]{0:T(128)} %copy-done.136) | copy-start | bytes 52
  941.3 14.5 %slice-start.8 = ((s8[8388608]{0:T(1024)(128)(4,1)}), s8[4194304]{0:T(1024)(128)(4,1)S(1)}, s32[]{:S(2)}) async-start(s8[8388608]{0:T(1024)(128)(4,1)} %bitcast.310), calls=%async_computation.15 | async-start | bytes 8388608
  962.3 8.8 slice-start
  991.2 8.1 copy-start.19
  991.2 8.1 copy-start.21
  1022.5 257.2 %all-to-all-start.3 = ((bf16[32,24,1024]{2,1,0:T(8,128)(2,1)}), bf16[32,24,1024]{2,1,0:T(8,128)(2,1)}, u32[]{:S(2)}, u32[]{:S(2)}) async-start(bf16[32,24,1024]{2,1,0:T(8,128)(2,1)} %bitcast.262), calls=%async_computation.3 | async-start | bytes 3145728 | tf_op jit(solution)/shard_map/all_to_all | solution.py:811
  1032.6 242.9 %copy-start.157 = (f32[2]{0:T(128)S(1)}, f32[2]{0:T(128)}, u32[]{:S(2)}) copy-start(f32[2]{0:T(128)} %copy-done.156) | copy-start | bytes 28
  1279.7 25.7 %copy-start.89 = (f32[7,1024]{1,0:T(8,128)S(1)}, f32[7,1024]{1,0:T(8,128)}, u32[]{:S(2)}) copy-start(f32[7,1024]{1,0:T(8,128)} %param.32) | copy-start | bytes 86020
  1279.7 25.7 %copy-start.107 = (f32[7,1024]{1,0:T(8,128)S(1)}, f32[7,1024]{1,0:T(8,128)}, u32[]{:S(2)}) copy-start(f32[7,1024]{1,0:T(8,128)} %param.38) | copy-start | bytes 86020
  1279.7 25.7 %copy-start.108 = (f32[7,1024]{1,0:T(8,128)S(1)}, f32[7,1024]{1,0:T(8,128)}, u32[]{:S(2)}) copy-start(f32[7,1024]{1,0:T(8,128)} %param.35) | copy-start | bytes 86020
  (136 other events, 497.2 us)
Sparse Core Ops, SparseCore 0:
  155.0 232.2 all-gather.11
  390.2 208.2 all-gather.15
  601.4 193.1 all-gather.13
